TPU v7x, 128 devices: a whole 4x4x4 slice. The times are simulated.
128 devices in a mesh: stream: 8 (over z, core), radial: 4 (over x), azim: 4 (over y).
Axes of the slice: x: 4, y: 4, z: 4, core: 2. Of those that a mesh axis runs over, the one named last changes fastest.
Arguments:
- component_fractions: float32 [53, 64, 32, 512], P(None, 'stream', 'radial', 'azim'), may hold values from 0 to 1
- kilokelvin_field: float32 [64, 32, 512], P('stream', 'radial', 'azim'), may hold values from 1 to 2.5
- axial_courant_number: float32 [64, 32, 512], P('stream', 'radial', 'azim'), may hold values from 0.1 to 0.4
- spreading_number: float32 [54], replicated, may hold values from 0.01 to 0.08
- arrhenius_multiplier_exponent: float32 [325], replicated, may hold values from -1 to 1
- thermal_exponents: float32 [325], replicated, may hold values from -1 to 1
- arrhenius_barrier: float32 [325], replicated, may hold values from 0 to 2
- balance_constant_exponents: float32 [325], replicated, may hold values from -2 to 2
- enthalpy_formation: float32 [53], replicated, may hold values from -0.3 to 0.3
- consumed_stoich_matrix: float32 [53, 325], replicated
- yield_stoich_matrix: float32 [53, 325], replicated
- processor_tiles_burning: int32 [128, 64], P(('stream', 'radial', 'azim')), may hold values from 0 to 63, as said below
- tile_transfer_tally: int32 [128, 128], P(('stream', 'radial', 'azim')), may hold values from 0 to 1, as said below
Outputs:
- species_out: float32 [53, 64, 32, 512], P(None, 'stream', 'radial', 'azim')
- temperature_out: float32 [64, 32, 512], P('stream', 'radial', 'azim')
Inputs may be any that keep to these rules, and one draw needn't show every extreme that they name: `processor_tiles_burning`: each row is a permutation of 0 to 63; the first c entries of row d are device d's flame blocks, c the sum of row d of tile_transfer_tally. Row sums lie in 0 to 64, one row sums to exactly 64; an entry is at most 1, reached in every draw; every column sums to exactly 24. Device d's flame blocks go to devices in increasing order: the first tile_transfer_tally[d, 0] of them to device 0, the next tile_transfer_tally[d, 1] to device 1, and so on.
All inputs are finite; a program needn't handle non-finite values.
Results may differ from a plain program's by a relative error of at most 0.0001.
Values sent between devices are 32-bit elements; how exact they have to be, the bound alone decides.
A program may use at most 128 MiB of HBM per device.

v0:
```python
import jax
import jax.numpy as jnp
from jax import lax
from jax.sharding import PartitionSpec as P

NCYC = 4
SUBSTEPS = 2
FLAME_DEV = 24


chem_step = 0.02
mass_offset = 0.05


def extended(value, sides, width, wrap):
    for axis, dim in sides:
        devices, length = (lax.axis_size(axis), value.shape[dim])
        up = [(i, (i + 1) % devices) for i in range(devices if wrap else devices - 1)]
        down = [(j, i) for i, j in up]
        last = lax.slice_in_dim(value, length - width, length, axis=dim)
        leading = lax.slice_in_dim(value, 0, width, axis=dim)
        before = lax.ppermute(last, axis, up)
        after = lax.ppermute(leading, axis, down)
        value = jnp.concatenate([before, value, after], axis=dim)
    return value


def chemistry(rows, kinetic_settings):
    (
        consumed_stoich_matrix,
        yield_stoich_matrix,
        arrhenius_multiplier_exponent,
        thermal_exponents,
        arrhenius_barrier,
        balance_constant_exponents,
        enthalpy_formation,
    ) = kinetic_settings
    fine = lax.Precision.HIGHEST
    nspec = consumed_stoich_matrix.shape[0]
    mass = rows[:, :nspec]
    thermal_scratch = rows[:, nspec]
    for cycle in range(NCYC):
        logc = jnp.log(mass + mass_offset)
        natural_log_kilokelvin = jnp.log(thermal_scratch)
        starting_point = (
            arrhenius_multiplier_exponent[None, :, None]
            + thermal_exponents[None, :, None] * natural_log_kilokelvin[:, None, :]
            - arrhenius_barrier[None, :, None] / thermal_scratch[:, None, :]
        )
        forward = jnp.exp(
            starting_point + jnp.einsum("sr,ksw->krw", consumed_stoich_matrix, logc, precision=fine)
        )
        backward = jnp.exp(
            starting_point
            - balance_constant_exponents[None, :, None]
            + jnp.einsum("sr,ksw->krw", yield_stoich_matrix, logc, precision=fine)
        )
        made = jnp.einsum("sr,krw->ksw", yield_stoich_matrix, forward, precision=fine) + jnp.einsum(
            "sr,krw->ksw", consumed_stoich_matrix, backward, precision=fine
        )
        lost = jnp.einsum(
            "sr,krw->ksw", consumed_stoich_matrix, forward, precision=fine
        ) + jnp.einsum("sr,krw->ksw", yield_stoich_matrix, backward, precision=fine)
        mass = (mass + chem_step * made) / (1.0 + chem_step * lost / (mass + mass_offset))
        thermal_scratch = thermal_scratch * jnp.exp(
            chem_step * jnp.einsum("s,ksw->kw", enthalpy_formation, made - lost, precision=fine)
        )
    return jnp.concatenate([mass, thermal_scratch[:, None, :]], 1)


def transport(fluid_fields, axial_courant_number, spreading_number):
    padded = extended(fluid_fields, (("stream", 1), ("radial", 2)), 1, False)
    padded = extended(padded, (("azim", 3),), 1, True)
    centre = padded[:, 1:-1, 1:-1, 1:-1]
    beside_all = padded[:, 2:, 1:-1, 1:-1] + padded[:, :-2, 1:-1, 1:-1]
    beside_all = beside_all + padded[:, 1:-1, 2:, 1:-1] + padded[:, 1:-1, :-2, 1:-1]
    beside_all = beside_all + padded[:, 1:-1, 1:-1, 2:] + padded[:, 1:-1, 1:-1, :-2]
    rate = spreading_number[:, None, None, None]
    return (
        (1.0 - 6.0 * rate - axial_courant_number) * centre
        + rate * beside_all
        + axial_courant_number * padded[:, :-2, 1:-1, 1:-1]
    )


def migrate(rows, targets, sent, live, kinetic_settings):
    devices = lax.axis_size(("stream", "radial", "azim"))
    nblock, nvar, width = rows.shape
    cap = -(-nblock // devices)
    picks = (
        (targets[:, None] == jnp.arange(devices, dtype=jnp.int32)[None, :]) & live[:, None]
    ).astype(jnp.int32)
    earlier = jnp.cumsum(picks, 0) - picks
    slot = jnp.sum(earlier * picks, 1)
    place = jnp.where(live, targets * cap + slot, devices * cap)
    outgoing = jnp.zeros((devices * cap, nvar, width), jnp.float32).at[place].set(rows, mode="drop")
    tally = sent.astype(jnp.float32)
    arrived, counted = (
        lax.all_to_all(
            outgoing.reshape(devices, cap, nvar, width),
            ("stream", "radial", "azim"),
            split_axis=0,
            concat_axis=0,
            tiled=True,
        ),
        lax.all_to_all(
            tally, ("stream", "radial", "azim"), split_axis=0, concat_axis=0, tiled=True
        ),
    )
    arrived = arrived.reshape(devices * cap, nvar, width)
    counted = counted.astype(jnp.int32)
    filled = (jnp.arange(cap, dtype=jnp.int32)[None, :] < counted[:, None]).reshape(devices * cap)
    marks = filled.astype(jnp.int32)
    ordinal = jnp.cumsum(marks) - marks
    packed = (
        jnp.zeros((FLAME_DEV, nvar, width), jnp.float32)
        .at[jnp.where(filled, ordinal, FLAME_DEV)]
        .set(arrived, mode="drop")
    )
    reacted = chemistry(packed, kinetic_settings)
    answer = jnp.where(filled[:, None, None], reacted[jnp.minimum(ordinal, FLAME_DEV - 1)], 0.0)
    returned = lax.all_to_all(
        answer.reshape(devices, cap, nvar, width),
        ("stream", "radial", "azim"),
        split_axis=0,
        concat_axis=0,
        tiled=True,
    )
    returned = returned.reshape(devices * cap, nvar, width)
    return returned[jnp.minimum(place, devices * cap - 1)]


def react(fluid_fields, blocks, targets, sent, live, kinetic_settings):
    nvar, xcells, ycells, width = fluid_fields.shape
    flat = fluid_fields.reshape(nvar, xcells * ycells, width)
    rows = jnp.moveaxis(jnp.take(flat, blocks, axis=1), 1, 0)
    reacted = migrate(rows, targets, sent, live, kinetic_settings)
    updated = jnp.where(live[:, None, None], reacted, rows)
    flat = flat.at[:, blocks].set(jnp.moveaxis(updated, 0, 1))
    return flat.reshape(fluid_fields.shape)


def shards(
    component_fractions,
    kilokelvin_field,
    axial_courant_number,
    spreading_number,
    arrhenius_multiplier_exponent,
    thermal_exponents,
    arrhenius_barrier,
    balance_constant_exponents,
    enthalpy_formation,
    consumed_stoich_matrix,
    yield_stoich_matrix,
    processor_tiles_burning,
    tile_transfer_tally,
):
    nspec = component_fractions.shape[0]
    kinetic_settings = (
        consumed_stoich_matrix,
        yield_stoich_matrix,
        arrhenius_multiplier_exponent,
        thermal_exponents,
        arrhenius_barrier,
        balance_constant_exponents,
        enthalpy_formation,
    )
    fluid_fields = jnp.concatenate([component_fractions, kilokelvin_field[None]], 0)
    blocks = processor_tiles_burning[0]
    sent = tile_transfer_tally[0]
    running = jnp.cumsum(sent)
    positions = jnp.arange(blocks.shape[0], dtype=jnp.int32)
    targets = jnp.sum((running[None, :] <= positions[:, None]).astype(jnp.int32), 1)
    live = positions < jnp.sum(sent)
    for substep in range(SUBSTEPS):
        fluid_fields = transport(fluid_fields, axial_courant_number, spreading_number)
        fluid_fields = react(fluid_fields, blocks, targets, sent, live, kinetic_settings)
    return (fluid_fields[:nspec], fluid_fields[nspec])


def solution(mesh):
    in_specs = (
        P(None, "stream", "radial", "azim"),
        P("stream", "radial", "azim"),
        P("stream", "radial", "azim"),
        P(),
        P(),
        P(),
        P(),
        P(),
        P(),
        P(),
        P(),
        P(("stream", "radial", "azim"), None),
        P(("stream", "radial", "azim"), None),
    )
    out_specs = (P(None, "stream", "radial", "azim"), P("stream", "radial", "azim"))
    return jax.shard_map(shards, mesh=mesh, in_specs=in_specs, out_specs=out_specs, check_vma=False)
```

profile of v0, /device:TPU:0, one launch (start us, length us, event | category | flops | bytes accessed | tf_op | source)
XLA Modules:
  0.0 629.2 jit_solution(17964541329284462721)
XLA Ops:
  9.8 11.8 %all-to-all-start = ((f32[128,1,1]{2,1,0:T(1,128)}), f32[128,1,1]{2,1,0:T(1,128)S(1)}, u32[]{:S(2)}, u32[]{:S(2)}) async-start(f32[128,1,1]{2,1,0:T(1,128)} %copy.186), calls=%async_computation | async-start | bytes 131072 | tf_op jit(solution)/shard_map/all_to_all | solution.py:106
  26.3 4.6 collective-permute-start.3
  37.0 3.4 fusion.223
  40.4 4.1 copy.182
  50.9 3.5 copy.183
  58.7 8.5 %fusion.17 = f32[54,8,8,128]{3,0,2,1:T(8,128)S(1)} fusion(f32[1,8,8,128]{3,0,2,1:T(1,128)S(1)} %bitcast.460, f32[54,10,10,1]{3,0,2,1:T(8,128)} %copy.185, f32[54,10,1,128]{3,0,2,1:T(8,128)S(1)} %copy-done.7, f32[54,10,1,128]{3,0,2,1:T(8,128)S(1)} %copy-done.9, f32[54,1,8,128]{3,0,2,1:T(8,128)S(1)} %collective-permute-done, ...), kind=kLoop, calls=%fused_computation.66 | loop fusion | flops 15925248 | bytes 4610672 | tf_op jit(solution)/shard_map/add | solution.py:80
  74.1 9.7 %scatter_fusion = f32[128,54,128]{2,1,0:T(8,128)} fusion(f32[128,54,128]{2,1,0:T(8,128)} %broadcast.269.clone, s32[64]{0:T(128)S(1)} %copy-done.18, f32[64,54,128]{2,1,0:T(8,128)} %broadcast_select_fusion.1), kind=kCustom, calls=%fused_computation.6 | custom fusion | bytes 5308672 | tf_op jit(solution)/shard_map/scatter | solution.py:96
  83.9 7.5 %copy.190 = f32[128,1,54,128]{3,1,2,0:T(1,128)} copy(f32[128,1,54,128]{3,2,0,1:T(8,128)} %bitcast.452) | data formatting | bytes 7077888 | tf_op jit(solution)/shard_map/reshape | solution.py:100
  91.4 10.4 %all-to-all-start.1 = ((f32[128,1,54,128]{3,1,2,0:T(1,128)}), f32[128,1,54,128]{3,1,2,0:T(1,128)}, u32[]{:S(2)}, u32[]{:S(2)}) async-start(f32[128,1,54,128]{3,1,2,0:T(1,128)} %copy.190), calls=%async_computation.1 | async-start | bytes 7077888 | tf_op jit(solution)/shard_map/all_to_all | solution.py:99
  104.5 41.5 %all-to-all-done.1 = f32[128,1,54,128]{3,1,2,0:T(1,128)} async-done(((f32[128,1,54,128]{3,1,2,0:T(1,128)}), f32[128,1,54,128]{3,1,2,0:T(1,128)}, u32[]{:S(2)}, u32[]{:S(2)}) %all-to-all-start.1) | async-done | bytes 3538976 | tf_op jit(solution)/shard_map/all_to_all | solution.py:99
  146.0 4.1 copy.233
  150.2 12.8 %scatter_fusion.1 = f32[24,54,128]{2,1,0:T(8,128)S(1)} fusion(f32[24,54,128]{2,1,0:T(8,128)S(1)} %broadcast.267.clone, s32[128]{0:T(128)S(1)} %get-tuple-element.16, f32[128,54,128]{2,1,0:T(8,128)} %bitcast.454), kind=kCustom, calls=%fused_computation.7 | custom fusion | bytes 10617344 | tf_op jit(solution)/shard_map/scatter | solution.py:118
  163.1 4.2 fusion.15
  173.4 4.6 fusion.14
  181.1 3.2 fusion.65
  184.9 4.4 fusion.12
  189.3 4.6 fusion.13
  200.1 3.2 convolution_add_fusion.13
  203.3 3.2 fusion.61
  207.2 4.4 fusion.10
  211.6 4.3 fusion.11
  215.8 3.3 fusion.142
  225.3 3.2 fusion.57
  229.1 4.8 fusion.8
  233.9 4.3 fusion.9
  241.2 3.2 fusion.168
  247.6 3.2 fusion.53
  256.5 5.4 copy.194
  261.9 6.3 all-to-all-start.2
  268.3 44.2 %all-to-all-done.2 = f32[128,1,54,128]{3,1,2,0:T(1,128)} async-done(((f32[128,1,54,128]{3,1,2,0:T(1,128)}), f32[128,1,54,128]{3,1,2,0:T(1,128)}, u32[]{:S(2)}, u32[]{:S(2)}) %all-to-all-start.2) | async-done | bytes 3538976 | tf_op jit(solution)/shard_map/all_to_all | solution.py:122
  312.4 4.1 copy.232
  316.5 3.9 gather_fusion.1
  320.5 3.5 fusion.33
  324.0 6.6 %scatter_fusion.2 = f32[54,64,128]{2,0,1:T(8,128)S(1)} fusion(f32[54,64,128]{2,0,1:T(8,128)S(1)} %bitcast.443, s32[64]{0:T(128)S(1)} %fusion.188, f32[64,54,128]{2,1,0:T(8,128)} %fusion.33), kind=kCustom, calls=%fused_computation.8 | custom fusion | bytes 5308672 | tf_op jit(solution)/shard_map/scatter | solution.py:139
  337.4 4.6 collective-permute-start.9
  346.9 3.3 fusion.222
  350.3 3.3 copy.197
  355.3 3.4 copy.199
  367.0 5.9 fusion.19
  378.8 10.3 %scatter_fusion.3 = f32[128,54,128]{2,1,0:T(8,128)} fusion(f32[128,54,128]{2,1,0:T(8,128)} %broadcast.269, s32[64]{0:T(128)S(1)} %copy-done.19, f32[64,54,128]{2,1,0:T(8,128)} %broadcast_select_fusion), kind=kCustom, calls=%fused_computation.9 | custom fusion | bytes 5308672 | tf_op jit(solution)/shard_map/scatter | solution.py:96
  389.2 5.7 copy.201
  394.9 54.0 %all_to_all.27 = f32[128,1,54,128]{3,1,2,0:T(1,128)S(1)} all-to-all(f32[128,1,54,128]{3,1,2,0:T(1,128)S(1)} %copy.201), channel_id=1, replica_groups=mesh['stream'=8,'radial'=4,'azim'=4] {'stream','radial','azim'}, dimensions={0} | all-to-all | bytes 7077888 | tf_op jit(solution)/shard_map/all_to_all | solution.py:99
  450.9 12.8 %scatter_fusion.4 = f32[24,54,128]{2,1,0:T(8,128)S(1)} fusion(f32[24,54,128]{2,1,0:T(8,128)S(1)} %broadcast.267, s32[128]{0:T(128)S(1)} %get-tuple-element.16, f32[128,54,128]{2,1,0:T(8,128)} %bitcast.453), kind=kCustom, calls=%fused_computation.10 | custom fusion | bytes 10617344 | tf_op jit(solution)/shard_map/scatter | solution.py:118
  463.8 4.4 fusion.6
  468.2 4.2 fusion.7
  475.5 3.3 fusion.164
  481.9 3.3 fusion.49
  485.7 4.4 fusion.4
  490.1 4.6 fusion.5
  500.9 3.2 convolution_add_fusion.5
  504.1 3.2 fusion.45
  507.9 4.4 fusion.2
  512.3 4.3 fusion.3
  516.6 3.3 fusion.126
  526.0 3.2 fusion.41
  529.8 4.9 fusion
  534.7 4.2 fusion.1
  542.0 3.2 fusion.152
  548.3 3.2 fusion.37
  557.2 3.6 copy.206
  560.8 49.7 %all_to_all.28 = f32[128,1,54,128]{3,1,2,0:T(1,128)S(1)} all-to-all(f32[128,1,54,128]{3,1,2,0:T(1,128)S(1)} %copy.206), channel_id=1, replica_groups=mesh['stream'=8,'radial'=4,'azim'=4] {'stream','radial','azim'}, dimensions={0} | all-to-all | bytes 7077888 | tf_op jit(solution)/shard_map/all_to_all | solution.py:122
  612.6 4.1 gather_fusion.3
  616.7 3.6 fusion.32
  620.3 6.6 %scatter_fusion.5 = f32[54,64,128]{2,0,1:T(8,128)S(1)} fusion(f32[54,64,128]{2,0,1:T(8,128)S(1)} %bitcast.449, s32[64]{0:T(128)S(1)} %fusion.188, f32[64,54,128]{2,1,0:T(8,128)} %fusion.32), kind=kCustom, calls=%fused_computation.11 | custom fusion | bytes 5308672 | tf_op jit(solution)/shard_map/scatter | solution.py:139
  (172 shorter events, 140.7 us)
Async XLA Ops:
  0.6 169.8 %copy-start = (f32[53,325]{1,0:T(8,128)S(1)}, f32[53,325]{1,0:T(8,128)}, u32[]{:S(2)}) copy-start(f32[53,325]{1,0:T(8,128)} %param.25) | copy-start | bytes 206704
  0.6 24.3 %copy-start.10 = (f32[8,8,128]{2,1,0:T(8,128)S(1)}, f32[8,8,128]{2,1,0:T(8,128)}, u32[]{:S(2)}) copy-start(f32[8,8,128]{2,1,0:T(8,128)} %param.16) | copy-start | bytes 98308
  0.7 7.7 %copy-start.23 = (s32[1,128]{1,0:T(1,128)S(1)}, s32[1,128]{1,0:T(1,128)}, u32[]{:S(2)}) copy-start(s32[1,128]{1,0:T(1,128)} %param.27) | copy-start | bytes 1540
  0.7 20.9 %copy-start.28 = (s32[1,64]{1,0:T(1,128)S(1)}, s32[1,64]{1,0:T(1,128)}, u32[]{:S(2)}) copy-start(s32[1,64]{1,0:T(1,128)} %param.26) | copy-start | bytes 772
  0.7 30.2 %copy-start.15 = (f32[54]{0:T(128)S(1)}, f32[54]{0:T(128)}, u32[]{:S(2)}) copy-start(f32[54]{0:T(128)} %param.18) | copy-start | bytes 652
  3.2 33.2 %copy-start.1 = (f32[53,8,8,128]{3,0,2,1:T(8,128)}, f32[53,8,8,128]{3,0,2,1:T(8,128)S(1)}, u32[]{:S(2)}) copy-start(f32[53,8,8,128]{3,0,2,1:T(8,128)S(1)} %copy.181) | copy-start | bytes 5210116
  4.1 20.9 %collective-permute-start = (f32[54,1,8,128]{3,0,2,1:T(8,128)S(1)}, f32[54,1,8,128]{3,0,2,1:T(8,128)S(1)}, u32[]{:S(2)}, u32[]{:S(2)}) collective-permute-start(f32[54,1,8,128]{3,0,2,1:T(8,128)S(1)} %get-tuple-element.42), channel_id=1, source_target_pairs={{16,0},{32,16},{48,32},{64,48},{80,64},{96,80},{112,96},{17,1},{33... | collective-permute-start | bytes 663560 | tf_op jit(solution)/shard_map/ppermute | solution.py:23
  5.4 19.6 %collective-permute-start.1 = (f32[54,1,8,128]{3,0,2,1:T(8,128)S(1)}, f32[54,1,8,128]{3,0,2,1:T(8,128)S(1)}, u32[]{:S(2)}, u32[]{:S(2)}) collective-permute-start(f32[54,1,8,128]{3,0,2,1:T(8,128)S(1)} %get-tuple-element.41), channel_id=1, source_target_pairs={{0,16},{16,32},{32,48},{48,64},{64,80},{80,96},{96,112},{1,17},{17... | collective-permute-start | bytes 663560 | tf_op jit(solution)/shard_map/ppermute | solution.py:22
  9.8 81.6 %all-to-all-start = ((f32[128,1,1]{2,1,0:T(1,128)}), f32[128,1,1]{2,1,0:T(1,128)S(1)}, u32[]{:S(2)}, u32[]{:S(2)}) async-start(f32[128,1,1]{2,1,0:T(1,128)} %copy.186), calls=%async_computation | async-start | bytes 131072 | tf_op jit(solution)/shard_map/all_to_all | solution.py:106
  25.0 10.1 %collective-permute-start.2 = (f32[54,10,1,128]{3,0,2,1:T(8,128)S(1)}, f32[54,10,1,128]{3,0,2,1:T(8,128)S(1)}, u32[]{:S(2)}, u32[]{:S(2)}) collective-permute-start(f32[54,10,1,128]{3,0,2,1:T(8,128)S(1)} %get-tuple-element.38), channel_id=1, source_target_pairs={{4,0},{8,4},{12,8},{5,1},{9,5},{13,9},{6,2},{10,6},{14,10},{7,3},{... | collective-permute-start | bytes 829448 | tf_op jit(solution)/shard_map/ppermute | solution.py:23
  26.3 10.0 %collective-permute-start.3 = (f32[54,10,1,128]{3,0,2,1:T(8,128)S(1)}, f32[54,10,1,128]{3,0,2,1:T(8,128)S(1)}, u32[]{:S(2)}, u32[]{:S(2)}) collective-permute-start(f32[54,10,1,128]{3,0,2,1:T(8,128)S(1)} %get-tuple-element.37), channel_id=1, source_target_pairs={{0,4},{4,8},{8,12},{1,5},{5,9},{9,13},{2,6},{6,10},{10,14},{3,7},{... | collective-permute-start | bytes 829448 | tf_op jit(solution)/shard_map/ppermute | solution.py:22
  35.1 1.4 copy-start.6
  36.2 0.7 copy-start.8
  40.4 7.1 %copy-start.5 = (f32[54,10,10,1]{3,0,2,1:T(8,128)S(1)}, f32[54,10,10,1]{3,0,2,1:T(8,128)}, u32[]{:S(2)}) copy-start(f32[54,10,10,1]{3,0,2,1:T(8,128)} %get-tuple-element.36) | copy-start | bytes 64804
  44.5 6.3 %collective-permute-start.4 = (f32[54,10,10,1]{0,2,3,1:T(8,128)}, f32[54,10,10,1]{0,2,3,1:T(8,128)}, u32[]{:S(2)}, u32[]{:S(2)}) collective-permute-start(f32[54,10,10,1]{0,2,3,1:T(8,128)} %copy.182), channel_id=1, source_target_pairs={{1,0},{2,1},{3,2},{0,3},{5,4},{6,5},{7,6},{4,7},{9,8},{10,9},{11,1... | collective-permute-start | bytes 64808 | tf_op jit(solution)/shard_map/ppermute | solution.py:23
  47.5 11.2 %copy-start.11 = (f32[8,8,128]{2,1,0:T(8,128)S(1)}, f32[8,8,128]{2,1,0:T(8,128)}, u32[]{:S(2)}) copy-start(f32[8,8,128]{2,1,0:T(8,128)} %param.17) | copy-start | bytes 98308
  49.6 9.0 %copy-start.7 = (f32[54,10,1,128]{3,0,2,1:T(8,128)S(1)}, f32[54,10,1,128]{3,0,2,1:T(8,128)}, u32[]{:S(2)}) copy-start(f32[54,10,1,128]{3,0,2,1:T(8,128)} %copy-done.6) | copy-start | bytes 829444
  49.6 9.0 %copy-start.9 = (f32[54,10,1,128]{3,0,2,1:T(8,128)S(1)}, f32[54,10,1,128]{3,0,2,1:T(8,128)}, u32[]{:S(2)}) copy-start(f32[54,10,1,128]{3,0,2,1:T(8,128)} %copy-done.8) | copy-start | bytes 829444
  49.6 9.0 %copy-start.16 = (f32[54]{0:T(128)S(1)}, f32[54]{0:T(128)}, u32[]{:S(2)}) copy-start(f32[54]{0:T(128)} %param.18) | copy-start | bytes 652
  49.6 9.0 %copy-start.20 = (f32[54]{0:T(128)S(1)}, f32[54]{0:T(128)}, u32[]{:S(2)}) copy-start(f32[54]{0:T(128)} %multiply_subtract_fusion) | copy-start | bytes 652
  49.6 6.4 %collective-permute-start.5 = (f32[54,10,10,1]{0,2,3,1:T(8,128)}, f32[54,10,10,1]{0,2,3,1:T(8,128)S(1)}, u32[]{:S(2)}, u32[]{:S(2)}) collective-permute-start(f32[54,10,10,1]{0,2,3,1:T(8,128)} %copy.184), channel_id=1, source_target_pairs={{0,1},{1,2},{2,3},{3,0},{4,5},{5,6},{6,7},{7,4},{8,9},{9,10},{10,1... | collective-permute-start | bytes 64808 | tf_op jit(solution)/shard_map/ppermute | solution.py:22
  69.1 5.0 copy-start.18
  91.4 54.6 %all-to-all-start.1 = ((f32[128,1,54,128]{3,1,2,0:T(1,128)}), f32[128,1,54,128]{3,1,2,0:T(1,128)}, u32[]{:S(2)}, u32[]{:S(2)}) async-start(f32[128,1,54,128]{3,1,2,0:T(1,128)} %copy.190), calls=%async_computation.1 | async-start | bytes 7077888 | tf_op jit(solution)/shard_map/all_to_all | solution.py:99
  104.2 149.9 %copy-start.13 = (pred[128]{0:T(512)(128)(4,1)}, pred[128]{0:T(512)(128)(4,1)S(1)}, u32[]{:S(2)}) copy-start(pred[128]{0:T(512)(128)(4,1)S(1)} %get-tuple-element.45) | copy-start | bytes 388
  150.2 12.9 %copy-start.3 = (f32[53,325]{1,0:T(8,128)S(1)}, f32[53,325]{1,0:T(8,128)}, u32[]{:S(2)}) copy-start(f32[53,325]{1,0:T(8,128)} %param.24) | copy-start | bytes 206704
  150.2 12.9 %copy-start.25 = (f32[325]{0:T(512)S(1)}, f32[325]{0:T(512)}, u32[]{:S(2)}) copy-start(f32[325]{0:T(512)} %param.21) | copy-start | bytes 3904
  150.2 12.9 %copy-start.26 = (f32[325]{0:T(512)S(1)}, f32[325]{0:T(512)}, u32[]{:S(2)}) copy-start(f32[325]{0:T(512)} %param.20) | copy-start | bytes 3904
  150.2 12.9 %copy-start.27 = (f32[325]{0:T(512)S(1)}, f32[325]{0:T(512)}, u32[]{:S(2)}) copy-start(f32[325]{0:T(512)} %param.19) | copy-start | bytes 3904
  167.3 6.1 copy-start.24
  181.1 3.3 copy-start.12
  261.9 6.3 %copy-start.22 = (s32[64]{0:T(128)S(1)}, s32[64]{0:T(128)}, u32[]{:S(2)}) copy-start(s32[64]{0:T(128)} %get-tuple-element.23) | copy-start | bytes 772
  261.9 6.3 %copy-start.29 = (s32[1,64]{1,0:T(1,128)S(1)}, s32[1,64]{1,0:T(1,128)}, u32[]{:S(2)}) copy-start(s32[1,64]{1,0:T(1,128)} %param.26) | copy-start | bytes 772
  261.9 50.5 %all-to-all-start.2 = ((f32[128,1,54,128]{3,1,2,0:T(1,128)}), f32[128,1,54,128]{3,1,2,0:T(1,128)}, u32[]{:S(2)}, u32[]{:S(2)}) async-start(f32[128,1,54,128]{3,1,2,0:T(1,128)} %copy.194), calls=%async_computation.2 | async-start | bytes 7077888 | tf_op jit(solution)/shard_map/all_to_all | solution.py:122
  330.6 4.4 collective-permute-start.6
  331.9 4.1 collective-permute-start.7
  336.1 8.9 %collective-permute-start.8 = (f32[54,10,1,128]{3,0,2,1:T(8,128)S(1)}, f32[54,10,1,128]{3,0,2,1:T(8,128)S(1)}, u32[]{:S(2)}, u32[]{:S(2)}) collective-permute-start(f32[54,10,1,128]{3,0,2,1:T(8,128)S(1)} %get-tuple-element.40), channel_id=1, source_target_pairs={{4,0},{8,4},{12,8},{5,1},{9,5},{13,9},{6,2},{10,6},{14,10},{7,3},{... | collective-permute-start | bytes 829448 | tf_op jit(solution)/shard_map/ppermute | solution.py:23
  337.4 9.4 %collective-permute-start.9 = (f32[54,10,1,128]{3,0,2,1:T(8,128)S(1)}, f32[54,10,1,128]{3,0,2,1:T(8,128)S(1)}, u32[]{:S(2)}, u32[]{:S(2)}) collective-permute-start(f32[54,10,1,128]{3,0,2,1:T(8,128)S(1)} %get-tuple-element.39), channel_id=1, source_target_pairs={{0,4},{4,8},{8,12},{1,5},{5,9},{9,13},{2,6},{6,10},{10,14},{3,7},{... | collective-permute-start | bytes 829448 | tf_op jit(solution)/shard_map/ppermute | solution.py:22
  353.6 5.8 collective-permute-start.10
  355.3 11.7 %copy-start.17 = (f32[54]{0:T(128)S(1)}, f32[54]{0:T(128)}, u32[]{:S(2)}) copy-start(f32[54]{0:T(128)} %param.18) | copy-start | bytes 652
  355.3 11.7 %copy-start.21 = (f32[54]{0:T(128)S(1)}, f32[54]{0:T(128)}, u32[]{:S(2)}) copy-start(f32[54]{0:T(128)} %multiply_subtract_fusion) | copy-start | bytes 652
  358.7 5.7 collective-permute-start.11
  375.1 14.1 %copy-start.4 = (f32[64,54,128]{2,1,0:T(8,128)}, f32[64,54,128]{2,1,0:T(8,128)S(1)}, u32[]{:S(2)}) copy-start(f32[64,54,128]{2,1,0:T(8,128)S(1)} %gather_fusion.5) | copy-start | bytes 5308420
  375.1 3.7 copy-start.19
  552.1 2.7 copy-start.14
  612.6 7.7 %copy-start.2 = (f32[54,8,8,128]{3,0,2,1:T(8,128)S(1)}, f32[54,8,8,128]{3,0,2,1:T(8,128)}, u32[]{:S(2)}) copy-start(f32[54,8,8,128]{3,0,2,1:T(8,128)} %fusion.19) | copy-start | bytes 5308420
where the time goes:
time: 638 us; the launch traced here: 629 us
  matrix products  176 us (28%)
  local copies, waits for them, and re-layouts  153 us (24%)
  blocking collectives  104 us (16%)
  waiting for transfers between devices  99.9 us (16%)
  starting transfers between devices  54.7 us (9%)
  other arithmetic  40.6 us (6%)
    all_to_all x1, blocking collectives, migrate(): lax.all_to_all(outgoing.reshape(devices, cap, nvar, width), ('stream', 'r...  54 us
    all_to_all x1, blocking collectives, migrate(): lax.all_to_all(answer.reshape(devices, cap, nvar, width), ('stream', 'rad...  49.7 us
    all_to_all x1, waiting for transfers between devices, migrate(): lax.all_to_all(answer.reshape(devices, cap, nvar, width), ('stream', 'rad...  44.2 us
    all_to_all x1, waiting for transfers between devices, migrate(): lax.all_to_all(outgoing.reshape(devices, cap, nvar, width), ('stream', 'r...  41.5 us
    dot_general x8, matrix products, chemistry(): jnp.einsum('sr,ksw->krw', yield_stoich_matrix, logc, precision=fine)  36.2 us
    dot_general x8, matrix products, chemistry(): jnp.einsum('sr,ksw->krw', consumed_stoich_matrix, logc, precision=fine)  34.8 us
    dot_general x8, matrix products, chemistry(): jnp.einsum('sr,krw->ksw', yield_stoich_matrix, backward, precision=fine)  25.9 us
    scatter x2, local copies, waits for them, and re-layouts, migrate(): packed = jnp.zeros((FLAME_DEV, nvar, width), jnp.float32).at[jnp.where(fi...  25.7 us
  transfers between devices with their start and end apart: 15, of which 9 were waited for; matrix products, arithmetic and copies ran while one was open for 10% of the time, Pallas kernels for 0%

commit v1 on v0

v1 whole, which is shorter than its diff:
```python
import functools

import jax
import jax.numpy as jnp
from jax import lax
from jax.experimental import pallas as pl
from jax.experimental.pallas import tpu as pltpu
from jax.sharding import PartitionSpec as P

NCYC = 4
ROWS = 56
GROUP = 8
chem_step = 0.02
mass_offset = 0.05
LOG2E = 1.4426950408889634
F32 = jnp.float32
BF16 = jnp.bfloat16
MESH = pl.DeviceIdType.MESH
AXES = ("stream", "radial", "azim")
LIMIT = 50 * 2**20


def halves(value):
    high = lax.reduce_precision(value, 8, 7)
    low = lax.reduce_precision(value - high, 8, 7)
    return high.astype(BF16), low.astype(BF16)


def weights(consumed, made, exponent, thermal, barrier, balance, enthalpy):
    nspec, nrxn = consumed.shape
    padded = -(-nrxn // 8) * 8

    def columns(table, constant):
        rows = [table, thermal[None], -LOG2E * barrier[None], LOG2E * constant[None]]
        return jnp.pad(jnp.concatenate(rows, 0), ((0, 0), (0, padded - nrxn)))

    ahead = columns(consumed, exponent)
    back = columns(made, exponent - balance)
    high, low = halves(jnp.concatenate([ahead, back], 1).T)
    rates = jnp.concatenate([high, high, low, high], 1)
    heat = LOG2E * jnp.sum(enthalpy[:, None] * (made - consumed), 0, keepdims=True)

    def stack(gain, loss, warm):
        rows = [gain, warm, jnp.zeros((2, nrxn), F32), loss, jnp.zeros((3, nrxn), F32)]
        return jnp.pad(jnp.concatenate(rows, 0), ((0, 0), (0, padded - nrxn)))

    both = jnp.concatenate([stack(made, consumed, heat), stack(consumed, made, -heat)], 1)
    high, low = halves(chem_step * both)
    return rates, jnp.concatenate([high, low], 0)


def parted(value):
    high = value.astype(BF16)
    return high, value - high.astype(F32)


def product(a, b):
    return lax.dot_general(a, b, (((1,), (0,)), ((), ())), preferred_element_type=F32)


def cycle(state, rates, sums):
    row = lax.broadcasted_iota(jnp.int32, state.shape, 0)
    moved = state + jnp.where(row < 53, mass_offset, jnp.where(row == 53, 0.0, 1.0))
    heat = state[53:54]
    logs = jnp.log2(moved)
    logs = jnp.where(row == 54, 1.0 / heat, jnp.where(row == 55, 1.0, logs))
    first, rest = parted(logs)
    second, third = parted(rest)
    first, second = first.astype(F32), second.astype(F32)
    stacked = jnp.concatenate([first, second, first, third], 0).astype(BF16)
    flux = jnp.exp2(product(rates, stacked))
    high, low = parted(flux)
    half = sums.shape[0] // 2
    both = product(sums, high)
    total = both[:half] + both[half:] + product(sums[:half], low.astype(BF16))
    gain, loss = total[:ROWS], total[ROWS:]
    species = (state + gain) * moved / (moved + loss)
    return jnp.where(row == 53, heat * jnp.exp2(gain[53:54]), species)


def chem_kernel(last, blocks_ref, tally_ref, state_ref, rates_ref, sums_ref, *outs):
    count = jnp.sum(tally_ref[...])
    work = outs[-1]
    work[...] = state_ref[...]

    def group(g, carry):
        at = [blocks_ref[0, g * GROUP + k] for k in range(GROUP)]
        state = jnp.concatenate([work[at[k]] for k in range(GROUP)], 1)
        state = lax.fori_loop(
            0, NCYC, lambda c, s: cycle(s, rates_ref[...], sums_ref[...]), state
        )
        for k in range(GROUP):

            @pl.when(g * GROUP + k < count)
            def _():
                work[at[k]] = state[:, k * 128 : (k + 1) * 128]

        return carry

    lax.fori_loop(0, (count + GROUP - 1) // GROUP, group, 0)
    if last:
        species_ref, heat_ref = outs[:2]

        def put(b, carry):
            species_ref[pl.ds(b, 53, stride=64), :] = work[b, pl.ds(0, 53), :]
            heat_ref[pl.ds(b, 1), :] = work[b, pl.ds(53, 1), :]
            return carry

        lax.fori_loop(0, 64, put, 0)


def react(last, blocks, tally, state, rates, sums):
    vmem = pl.BlockSpec(memory_space=pltpu.VMEM)
    if last:
        shape = [jax.ShapeDtypeStruct((53 * 64, 128), F32), jax.ShapeDtypeStruct((64, 128), F32)]
        scratch = [pltpu.VMEM(state.shape, F32)]
    else:
        shape = [jax.ShapeDtypeStruct(state.shape, F32)]
        scratch = []
    return pl.pallas_call(
        functools.partial(chem_kernel, last),
        out_shape=shape,
        in_specs=[pl.BlockSpec(memory_space=pltpu.SMEM)] + [vmem] * 4,
        out_specs=[vmem] * len(shape),
        scratch_shapes=scratch,
        compiler_params=pltpu.CompilerParams(vmem_limit_bytes=LIMIT),
    )(blocks, tally, state, rates, sums)


def neighbours():
    found = []
    for axis in AXES:
        n, me = lax.axis_size(axis), lax.axis_index(axis)
        found += [{axis: lax.rem(me + n - 1, n)}, {axis: lax.rem(me + 1, n)}]
    return found


def move_kernel(first, *refs):
    if first:
        species_ref, heat_ref, courant_ref, spread_ref, out_ref = refs[:5]
    else:
        state_ref, courant_ref, spread_ref, out_ref = refs[:4]
    grid, edge, halo, send_sem, recv_sem = refs[-5:]
    peers = neighbours()
    barrier = pltpu.get_barrier_semaphore()
    for peer in peers:
        pl.semaphore_signal(barrier, inc=1, device_id=peer, device_id_type=MESH)
    edge[...] = jnp.zeros_like(edge)
    lane = lax.broadcasted_iota(jnp.int32, (ROWS, 128), 1)

    def load(b, carry):
        i, j = b // 8 + 1, b % 8 + 1
        if first:
            grid[i, j, pl.ds(0, 53), :] = species_ref[pl.ds(b, 53, stride=64), :]
            grid[i, j, pl.ds(53, 1), :] = heat_ref[pl.ds(b, 1), :]
            grid[i, j, pl.ds(54, 2), :] = jnp.zeros((2, 128), F32)
            here = grid[i, j]
        else:
            here = state_ref[b]
            grid[i, j] = here
        low, high = carry
        low = jnp.where(lane == b, pltpu.roll(here, b, 1), low)
        high = jnp.where(lane == b, pltpu.roll(here, b + 1, 1), high)
        return low, high

    low, high = lax.fori_loop(0, 64, load, (jnp.zeros((ROWS, 128), F32),) * 2)
    edge[0] = low
    edge[1] = high
    pl.semaphore_wait(barrier, 6)
    inner = pl.ds(1, 8)
    plans = [
        (grid.at[1, inner], grid.at[9, inner]),
        (grid.at[8, inner], grid.at[0, inner]),
        (grid.at[inner, 1], grid.at[inner, 9]),
        (grid.at[inner, 8], grid.at[inner, 0]),
        (edge.at[0], halo.at[1]),
        (edge.at[1], halo.at[0]),
    ]
    copies = [
        pltpu.make_async_remote_copy(
            src_ref=src,
            dst_ref=dst,
            send_sem=send_sem.at[k],
            recv_sem=recv_sem.at[k],
            device_id=peers[k],
            device_id_type=MESH,
        )
        for k, (src, dst) in enumerate(plans)
    ]
    for copy in copies:
        copy.start()
    for copy in copies:
        copy.wait()
    blank = jnp.zeros((8, ROWS, 128), F32)
    stream, radial = lax.axis_index("stream"), lax.axis_index("radial")

    @pl.when(stream == 0)
    def _():
        grid[0, inner] = blank

    @pl.when(stream == lax.axis_size("stream") - 1)
    def _():
        grid[9, inner] = blank

    @pl.when(radial == 0)
    def _():
        grid[inner, 0] = blank

    @pl.when(radial == lax.axis_size("radial") - 1)
    def _():
        grid[inner, 9] = blank

    rate = spread_ref[...]
    keep = 1.0 - 6.0 * rate

    def step(b, carry):
        i, j = b // 8 + 1, b % 8 + 1
        here = grid[i, j]
        behind = grid[i - 1, j]
        left = jnp.where(lane == 0, pltpu.roll(halo[0], lax.rem(128 - b, 128), 1), pltpu.roll(here, 1, 1))
        right = jnp.where(lane == 127, pltpu.roll(halo[1], 127 - b, 1), pltpu.roll(here, 127, 1))
        beside = (behind + grid[i + 1, j]) + (grid[i, j - 1] + grid[i, j + 1]) + (left + right)
        speed = courant_ref[pl.ds(b, 1), :]
        out_ref[b] = (keep - speed) * here + rate * beside + speed * behind
        return carry

    lax.fori_loop(0, 64, step, 0)


def move(first, args):
    vmem = pl.BlockSpec(memory_space=pltpu.VMEM)
    return pl.pallas_call(
        functools.partial(move_kernel, first),
        out_shape=jax.ShapeDtypeStruct((64, ROWS, 128), F32),
        in_specs=[vmem] * len(args),
        out_specs=vmem,
        scratch_shapes=[
            pltpu.VMEM((10, 10, ROWS, 128), F32),
            pltpu.VMEM((2, ROWS, 128), F32),
            pltpu.VMEM((2, ROWS, 128), F32),
            pltpu.SemaphoreType.DMA((6,)),
            pltpu.SemaphoreType.DMA((6,)),
        ],
        compiler_params=pltpu.CompilerParams(
            collective_id=0 if first else 1, has_side_effects=True, vmem_limit_bytes=LIMIT
        ),
    )(*args)


def shards(
    component_fractions,
    kilokelvin_field,
    axial_courant_number,
    spreading_number,
    arrhenius_multiplier_exponent,
    thermal_exponents,
    arrhenius_barrier,
    balance_constant_exponents,
    enthalpy_formation,
    consumed_stoich_matrix,
    yield_stoich_matrix,
    processor_tiles_burning,
    tile_transfer_tally,
):
    shape = component_fractions.shape
    rates, sums = weights(
        consumed_stoich_matrix,
        yield_stoich_matrix,
        arrhenius_multiplier_exponent,
        thermal_exponents,
        arrhenius_barrier,
        balance_constant_exponents,
        enthalpy_formation,
    )
    species = component_fractions.reshape(53 * 64, 128)
    heat = kilokelvin_field.reshape(64, 128)
    courant = axial_courant_number.reshape(64, 128)
    spread = jnp.broadcast_to(jnp.pad(spreading_number, (0, 2))[:, None], (ROWS, 128))
    blocks, tally = processor_tiles_burning, tile_transfer_tally
    state = move(True, (species, heat, courant, spread))
    (state,) = react(False, blocks, tally, state, rates, sums)
    state = move(False, (state, courant, spread))
    species, heat = react(True, blocks, tally, state, rates, sums)
    return species.reshape(shape), heat.reshape(shape[1:])


def solution(mesh):
    in_specs = (
        P(None, "stream", "radial", "azim"),
        P("stream", "radial", "azim"),
        P("stream", "radial", "azim"),
        P(),
        P(),
        P(),
        P(),
        P(),
        P(),
        P(),
        P(),
        P(AXES, None),
        P(AXES, None),
    )
    out_specs = (P(None, "stream", "radial", "azim"), P("stream", "radial", "azim"))
    return jax.shard_map(shards, mesh=mesh, in_specs=in_specs, out_specs=out_specs, check_vma=False)
```

time: 638 us -> 125 us (0.20)
  the two profiles are of different devices: /device:TPU:0 before, /device:TPU:78 now
where the time goes in v1:
time: 125 us; the launch traced here: 124 us
  Pallas kernels  114 us (91%)
  local copies, waits for them, and re-layouts  5.93 us (5%)
  other arithmetic  3.24 us (3%)
    pallas_call x2, Pallas kernels, react(): pl.pallas_call(functools.partial(chem_kernel, last), out_shape=shape, in_...  77.8 us
    pallas_call x2, Pallas kernels, move(): pl.pallas_call(functools.partial(move_kernel, first), out_shape=jax.Shape...  36.5 us
    unnamed x18, local copies, waits for them, and re-layouts  4 us

profile of v1, /device:TPU:78, one launch (start us, length us, event | category | flops | bytes accessed | tf_op | source)
XLA Modules:
  0.0 124.3 jit_solution(13131652090414378926)
XLA Ops:
  0.6 0.7 pad.18
  1.3 0.7 broadcast_multiply_fusion.2
  2.0 1.0 multiply_reduce_fusion
  3.0 0.7 broadcast_multiply_fusion.1
  3.7 0.1 broadcast_in_dim.4.refs_3_.refs_2_
  3.8 0.1 mul.64
  3.9 0.0 copy-start.6
  3.9 0.0 copy-start.7
  3.9 0.1 mul.63
  4.0 0.1 mul.65
  4.2 0.8 broadcast_in_dim.6
  5.0 1.0 copy.17
  6.0 1.0 copy.21
  7.0 0.2 pad_maximum_fusion.2
  7.2 0.0 copy-start.1
  7.2 0.0 copy-start.2
  7.3 0.0 copy-start.3
  7.3 0.1 fusion.4
  7.3 0.3 pad_maximum_fusion.1.rates_ref
  7.7 0.0 copy-done.6
  7.7 0.0 copy-done.7
  7.7 0.1 concatenate.29
  7.8 0.1 reduce-precision_convert_fusion
  8.0 0.7 copy-done.1
  8.7 0.0 copy-done.2
  8.7 0.0 copy-done.3
  8.7 0.0 copy-start.4
  8.7 0.0 copy-start.5
  8.7 20.6 %shard_map.140.state_ref = f32[64,56,128]{2,1,0:T(8,128)S(1)} custom-call(f32[3392,128]{1,0:T(8,128)S(1)} %bitcast.11, f32[64,128]{1,0:T(8,128)S(1)} %bitcast.14, f32[64,128]{1,0:T(8,128)S(1)} %bitcast.12, f32[56,128]{1,0:T(8,128)S(1)} %broadcast_in_dim.4.refs_3_.refs_2_), custom_call_target="tpu_custom_call" | custom-call | tf_op jit(solution)/shard_map/pallas_call | solution.py:232
  29.3 0.0 copy-start
  29.3 1.3 %copy-done = f32[64,56,128]{2,1,0:T(8,128)} copy-done((f32[64,56,128]{2,1,0:T(8,128)}, f32[64,56,128]{2,1,0:T(8,128)S(1)}, u32[]{:S(2)}) %copy-start) | copy-done | bytes 1835032
  30.5 0.0 copy-done.4
  30.5 0.0 copy-done.5
  30.5 37.9 %shard_map.141.refs_0_ = f32[64,56,128]{2,1,0:T(8,128)S(1)} custom-call(s32[1,64]{1,0:T(1,128)S(1)} %copy-done.4, s32[1,128]{1,0:T(1,128)S(1)} %copy-done.5, f32[64,56,128]{2,1,0:T(8,128)} %copy-done, bf16[656,224]{1,0:T(8,128)(2,1)S(1)} %pad_maximum_fusion.1.rates_ref, bf16[224,656]{1,0:T(8,128)(2,1)S(1)} %pad_maximum_fusion.sums_ref), custom_call_target="tpu_custom_call" | custom-call | tf_op jit(solution)/shard_map/pallas_call | solution.py:120
  68.5 15.9 %shard_map.142.state_ref = f32[64,56,128]{2,1,0:T(8,128)S(1)} custom-call(f32[64,56,128]{2,1,0:T(8,128)S(1)} %shard_map.141.refs_0_, f32[64,128]{1,0:T(8,128)S(1)} %bitcast.13, f32[56,128]{1,0:T(8,128)S(1)} %broadcast_in_dim.4.refs_3_.refs_2_), custom_call_target="tpu_custom_call" | custom-call | tf_op jit(solution)/shard_map/pallas_call | solution.py:232
  84.4 39.9 %shard_map.143 = (f32[3392,128]{1,0:T(8,128)}, f32[64,128]{1,0:T(8,128)}) custom-call(s32[1,64]{1,0:T(1,128)S(1)} %copy-done.4, s32[1,128]{1,0:T(1,128)S(1)} %copy-done.5, f32[64,56,128]{2,1,0:T(8,128)S(1)} %shard_map.142.state_ref, bf16[656,224]{1,0:T(8,128)(2,1)S(1)} %pad_maximum_fusion.1.rates_ref, bf16[224,656]{1,0:T(8,128)(2,1)S(1)} %pad_maximum_fusion.sums_ref), custom_call_target="tpu_custom_call" | custom-call | tf_op jit(solution)/shard_map/pallas_call | solution.py:120
  (7 shorter events, 0.1 us)
Async XLA Ops:
  3.9 3.8 %copy-start.6 = (f32[53,325]{1,0:T(8,128)S(1)}, f32[53,325]{1,0:T(8,128)}, u32[]{:S(2)}) copy-start(f32[53,325]{1,0:T(8,128)} %param.22) | copy-start | bytes 206704
  3.9 3.8 %copy-start.7 = (f32[53,325]{1,0:T(8,128)S(1)}, f32[53,325]{1,0:T(8,128)}, u32[]{:S(2)}) copy-start(f32[53,325]{1,0:T(8,128)} %param.23) | copy-start | bytes 206704
  7.2 1.5 %copy-start.1 = (f32[53,8,8,128]{3,2,1,0:T(8,128)S(1)}, f32[53,8,8,128]{3,2,1,0:T(8,128)}, u32[]{:S(2)}) copy-start(f32[53,8,8,128]{3,2,1,0:T(8,128)} %param.13) | copy-start | bytes 5210116
  7.2 1.5 %copy-start.2 = (f32[8,8,128]{2,1,0:T(8,128)S(1)}, f32[8,8,128]{2,1,0:T(8,128)}, u32[]{:S(2)}) copy-start(f32[8,8,128]{2,1,0:T(8,128)} %param.15) | copy-start | bytes 98308
  7.3 1.4 %copy-start.3 = (f32[8,8,128]{2,1,0:T(8,128)S(1)}, f32[8,8,128]{2,1,0:T(8,128)}, u32[]{:S(2)}) copy-start(f32[8,8,128]{2,1,0:T(8,128)} %param.14) | copy-start | bytes 98308
  8.7 21.8 %copy-start.4 = (s32[1,64]{1,0:T(1,128)S(1)}, s32[1,64]{1,0:T(1,128)}, u32[]{:S(2)}) copy-start(s32[1,64]{1,0:T(1,128)} %blocks_ref.3) | copy-start | bytes 772
  8.7 21.8 %copy-start.5 = (s32[1,128]{1,0:T(1,128)S(1)}, s32[1,128]{1,0:T(1,128)}, u32[]{:S(2)}) copy-start(s32[1,128]{1,0:T(1,128)} %tally_ref.3) | copy-start | bytes 1540
  29.3 1.3 %copy-start = (f32[64,56,128]{2,1,0:T(8,128)}, f32[64,56,128]{2,1,0:T(8,128)S(1)}, u32[]{:S(2)}) copy-start(f32[64,56,128]{2,1,0:T(8,128)S(1)} %shard_map.140.state_ref) | copy-start | bytes 5505028

commit v2 on v1

v2 whole, which is shorter than its diff:
```python
import functools

import jax
import jax.numpy as jnp
from jax import lax
from jax.experimental import pallas as pl
from jax.experimental.pallas import tpu as pltpu
from jax.sharding import PartitionSpec as P

NCYC = 4
ROWS = 56
GROUP = 8
chem_step = 0.02
mass_offset = 0.05
LOG2E = 1.4426950408889634
F32 = jnp.float32
BF16 = jnp.bfloat16
MESH = pl.DeviceIdType.MESH
AXES = ("stream", "radial", "azim")
LIMIT = 50 * 2**20
WORK = 32
EARLY = 8
LATE = 8
SPAN = WORK - EARLY - LATE
FLOOR = 24
SWEEPS = 3
PAIR = 16
SIDE = 6
SIZES = (PAIR,) + (SIDE,) * 6
BASES = tuple(sum(SIZES[:k]) for k in range(7))
SLOTS = sum(SIZES)
OPPOSITE = (0, 2, 1, 4, 3, 6, 5)
SEND_AT, WORK_AT, REPLY_AT, FINAL_AT, REST_AT = 0, 64, 96, 160, 224


def halves(value):
    high = lax.reduce_precision(value, 8, 7)
    low = lax.reduce_precision(value - high, 8, 7)
    return high.astype(BF16), low.astype(BF16)


def weights(consumed, made, exponent, thermal, barrier, balance, enthalpy):
    nspec, nrxn = consumed.shape
    padded = -(-nrxn // 8) * 8

    def columns(table, constant):
        rows = [table, thermal[None], -LOG2E * barrier[None], LOG2E * constant[None]]
        return jnp.pad(jnp.concatenate(rows, 0), ((0, 0), (0, padded - nrxn)))

    ahead = columns(consumed, exponent)
    back = columns(made, exponent - balance)
    high, low = halves(jnp.concatenate([ahead, back], 1).T)
    rates = jnp.concatenate([high, high, low, high], 1)
    heat = LOG2E * jnp.sum(enthalpy[:, None] * (made - consumed), 0, keepdims=True)

    def stack(gain, loss, warm):
        rows = [gain, warm, jnp.zeros((2, nrxn), F32), loss, jnp.zeros((3, nrxn), F32)]
        return jnp.pad(jnp.concatenate(rows, 0), ((0, 0), (0, padded - nrxn)))

    both = jnp.concatenate([stack(made, consumed, heat), stack(consumed, made, -heat)], 1)
    high, low = halves(chem_step * both)
    return rates, jnp.concatenate([high, low], 0)


def parted(value):
    high = value.astype(BF16)
    return high, value - high.astype(F32)


def product(a, b):
    return lax.dot_general(a, b, (((1,), (0,)), ((), ())), preferred_element_type=F32)


def cycle(state, rates, sums):
    row = lax.broadcasted_iota(jnp.int32, state.shape, 0)
    moved = state + jnp.where(row < 53, mass_offset, jnp.where(row == 53, 0.0, 1.0))
    heat = state[53:54]
    logs = jnp.log2(moved)
    logs = jnp.where(row == 54, 1.0 / heat, jnp.where(row == 55, 1.0, logs))
    first, rest = parted(logs)
    second, third = parted(rest)
    first, second = first.astype(F32), second.astype(F32)
    stacked = jnp.concatenate([first, second, first, third], 0).astype(BF16)
    flux = jnp.exp2(product(rates, stacked))
    high, low = parted(flux)
    half = sums.shape[0] // 2
    both = product(sums, high)
    total = both[:half] + both[half:] + product(sums[:half], low.astype(BF16))
    gain, loss = total[:ROWS], total[ROWS:]
    species = (state + gain) * moved / (moved + loss)
    return jnp.where(row == 53, heat * jnp.exp2(gain[53:54]), species)


def toward(value, k):
    lane = lax.broadcasted_iota(jnp.int32, value.shape, 1)
    azim, radial, core = lane & 3, (lane >> 2) & 3, (lane >> 4) & 1

    def ahead(step):
        return pltpu.roll(value, (128 - step) % 128, 1)

    return (
        lambda: jnp.where(core == 0, ahead(16), ahead(-16)),
        lambda: ahead(32),
        lambda: ahead(-32),
        lambda: jnp.where(radial < 3, ahead(4), ahead(-12)),
        lambda: jnp.where(radial > 0, ahead(-4), ahead(12)),
        lambda: jnp.where(azim < 3, ahead(1), ahead(-3)),
        lambda: jnp.where(azim > 0, ahead(-1), ahead(3)),
    )[k]()


def flows(counts):
    load, own = jnp.maximum(counts, EARLY + LATE), counts
    given = [jnp.zeros_like(counts) for _ in SIZES]
    taken = [jnp.zeros_like(counts) for _ in SIZES]
    for sweep in range(SWEEPS):
        for k, size in enumerate(SIZES):
            other = toward(load, k)
            gap = load - other + (1 if sweep == SWEEPS - 1 else 0)
            spare = jnp.maximum(own - (EARLY + LATE), 0)
            give = jnp.minimum(jnp.minimum(size - given[k], spare), jnp.maximum(gap, 0) >> 1)
            give = jnp.minimum(give, jnp.maximum(load - FLOOR, 0))
            give = jnp.minimum(give, jnp.maximum(WORK - other, 0))
            take = toward(give, OPPOSITE[k])
            given[k], taken[k] = given[k] + give, taken[k] + take
            own, load = own - give, load - give + take
    return own, given, taken


def plan_kernel(me_ref, blocks_ref, counts_ref, out_ref):
    counts = jnp.broadcast_to(counts_ref[...], (8, 128))
    own, given, taken = flows(counts)
    place = lax.broadcasted_iota(jnp.int32, (8, 128), 0) * 128
    place = place + lax.broadcasted_iota(jnp.int32, (8, 128), 1)
    mine = place == me_ref[0]

    def pick(value):
        return jnp.sum(jnp.where(mine, value, 0))

    own, total = pick(own), pick(counts)
    given, taken = [pick(v) for v in given], [pick(v) for v in taken]
    received = sum(taken)
    kept = jnp.minimum(own, WORK - received)

    def clear(k, carry):
        out_ref[k] = 0
        return carry

    def clear_final(k, carry):
        out_ref[FINAL_AT + k] = k
        return carry

    lax.fori_loop(0, FINAL_AT, clear, 0)
    lax.fori_loop(0, 64, clear_final, 0)

    def keep(o, carry):
        block = blocks_ref[0, o]
        late = WORK - LATE + o - EARLY
        middle = EARLY + received + o - EARLY - LATE
        slot = jnp.where(o < EARLY, o, jnp.where(o < EARLY + LATE, late, middle))
        out_ref[WORK_AT + slot] = block
        out_ref[FINAL_AT + block] = 128 + slot
        return carry

    lax.fori_loop(0, kept, keep, 0)
    start, reached = kept, jnp.int32(EARLY)
    for p, base in enumerate(BASES):

        def give(k, carry):
            block = blocks_ref[0, start + k]
            out_ref[SEND_AT + base + k] = block
            out_ref[FINAL_AT + block] = 64 + base + k
            return carry

        def take(k, carry):
            out_ref[WORK_AT + reached + k] = 64 + base + k
            out_ref[REPLY_AT + base + k] = reached + k
            return carry

        lax.fori_loop(0, given[p], give, 0)
        lax.fori_loop(0, taken[p], take, 0)
        start, reached = start + given[p], reached + taken[p]
    out_ref[REST_AT] = start
    out_ref[REST_AT + 1] = total


def plan(me, blocks, counts):
    smem = pl.BlockSpec(memory_space=pltpu.SMEM)
    return pl.pallas_call(
        plan_kernel,
        out_shape=jax.ShapeDtypeStruct((256,), jnp.int32),
        in_specs=[smem, smem, pl.BlockSpec(memory_space=pltpu.VMEM)],
        out_specs=smem,
    )(me, blocks, counts)


def subcycles(state, rates_ref, sums_ref):
    return lax.fori_loop(0, NCYC, lambda c, s: cycle(s, rates_ref[...], sums_ref[...]), state)


def rest_kernel(lists_ref, blocks_ref, state_ref, rates_any, sums_any, out_ref, rates, sums, held, sem):
    start, count = lists_ref[REST_AT], lists_ref[REST_AT + 1]

    def bring(source, target):
        copy = pltpu.make_async_copy(source, target, sem)
        copy.start()
        copy.wait()

    @pl.when(start < count)
    def _():
        bring(rates_any, rates)
        bring(sums_any, sums)

        def group(g, carry):
            first = start + g * GROUP
            for k in range(GROUP):
                bring(out_ref.at[blocks_ref[0, jnp.minimum(first + k, 63)]], held.at[k])
            state = jnp.concatenate([held[k] for k in range(GROUP)], 1)
            state = subcycles(state, rates, sums)
            for k in range(GROUP):
                held[k] = state[:, k * 128 : (k + 1) * 128]

                @pl.when(first + k < count)
                def _():
                    bring(held.at[k], out_ref.at[blocks_ref[0, jnp.minimum(first + k, 63)]])

            return carry

        lax.fori_loop(0, (count - start + GROUP - 1) // GROUP, group, 0)


def react_rest(lists, blocks, state, rates, sums):
    smem, anywhere = pl.BlockSpec(memory_space=pltpu.SMEM), pl.BlockSpec(memory_space=pl.ANY)
    return pl.pallas_call(
        rest_kernel,
        out_shape=jax.ShapeDtypeStruct(state.shape, F32),
        in_specs=[smem, smem] + [anywhere] * 3,
        out_specs=anywhere,
        scratch_shapes=[
            pltpu.VMEM(rates.shape, BF16),
            pltpu.VMEM(sums.shape, BF16),
            pltpu.VMEM((GROUP, ROWS, 128), F32),
            pltpu.SemaphoreType.DMA(()),
        ],
        input_output_aliases={2: 0},
        compiler_params=pltpu.CompilerParams(vmem_limit_bytes=LIMIT),
    )(lists, blocks, state, rates, sums)


def last_kernel(lists_ref, blocks_ref, state_ref, rates_ref, sums_ref, species_ref, heat_ref, work):
    start, count = lists_ref[REST_AT], lists_ref[REST_AT + 1]

    def put(source, b):
        species_ref[pl.ds(b, 53, stride=64), :] = source[b, pl.ds(0, 53), :]
        heat_ref[pl.ds(b, 1), :] = source[b, pl.ds(53, 1), :]

    def put_row(i, carry):
        for j in range(8):
            put(state_ref, i * 8 + j)
        return carry

    lax.fori_loop(0, 8, put_row, 0)

    def group(g, carry):
        first = start + g * GROUP
        at = [blocks_ref[0, jnp.minimum(first + k, 63)] for k in range(GROUP)]
        state = jnp.concatenate([state_ref[at[k]] for k in range(GROUP)], 1)
        state = subcycles(state, rates_ref, sums_ref)
        for k in range(GROUP):

            @pl.when(first + k < count)
            def _():
                work[at[k]] = state[:, k * 128 : (k + 1) * 128]
                put(work, at[k])

        return carry

    lax.fori_loop(0, (count - start + GROUP - 1) // GROUP, group, 0)


def finish(lists, blocks, state, rates, sums):
    smem, vmem = pl.BlockSpec(memory_space=pltpu.SMEM), pl.BlockSpec(memory_space=pltpu.VMEM)
    return pl.pallas_call(
        last_kernel,
        out_shape=[jax.ShapeDtypeStruct((53 * 64, 128), F32), jax.ShapeDtypeStruct((64, 128), F32)],
        in_specs=[smem, smem] + [vmem] * 3,
        out_specs=[vmem] * 2,
        scratch_shapes=[pltpu.VMEM(state.shape, F32)],
        compiler_params=pltpu.CompilerParams(vmem_limit_bytes=LIMIT),
    )(lists, blocks, state, rates, sums)


def shifted(axis, step):
    n, me = lax.axis_size(axis), lax.axis_index(axis)
    return {axis: lax.rem(me + (n + step), n)}


def faces():
    return [shifted(axis, step) for axis in AXES for step in (-1, 1)]


def partners():
    me = lax.axis_index("stream")
    sides = [("stream", 2), ("stream", -2), ("radial", 1), ("radial", -1), ("azim", 1), ("azim", -1)]
    return [{"stream": me + 1 - 2 * lax.rem(me, 2)}] + [shifted(*side) for side in sides]


def greet(peers):
    barrier = pltpu.get_barrier_semaphore()
    for peer in peers:
        pl.semaphore_signal(barrier, inc=1, device_id=peer, device_id_type=MESH)
    return lambda: pl.semaphore_wait(barrier, len(peers))


def remote(source, target, sems, k, peer):
    return pltpu.make_async_remote_copy(
        src_ref=source,
        dst_ref=target,
        send_sem=sems[0].at[k],
        recv_sem=sems[1].at[k],
        device_id=peer,
        device_id_type=MESH,
    )


def transport(fill, met, courant_ref, spread_ref, out, grid, edge, halo, sems):
    lane = lax.broadcasted_iota(jnp.int32, (ROWS, 128), 1)

    def load(i, carry):
        low, high = carry
        for j in range(8):
            b = i * 8 + j
            fill(b, grid.at[i + 1, j + 1])
            here = grid[i + 1, j + 1]
            low = jnp.where(lane == b, pltpu.roll(here, b, 1), low)
            high = jnp.where(lane == b, pltpu.roll(here, b + 1, 1), high)
        return low, high

    low, high = lax.fori_loop(0, 8, load, (jnp.zeros((ROWS, 128), F32),) * 2)
    edge[0] = low
    edge[1] = high
    met()
    peers = faces()
    inner = pl.ds(1, 8)
    plans = [
        (grid.at[1, inner], grid.at[9, inner]),
        (grid.at[8, inner], grid.at[0, inner]),
        (grid.at[inner, 1], grid.at[inner, 9]),
        (grid.at[inner, 8], grid.at[inner, 0]),
        (edge.at[0], halo.at[1]),
        (edge.at[1], halo.at[0]),
    ]
    copies = [remote(*plans[k], sems, k, peers[k]) for k in range(6)]
    for copy in copies:
        copy.start()
    for copy in copies:
        copy.wait()
    blank = jnp.zeros((8, ROWS, 128), F32)
    stream, radial = lax.axis_index("stream"), lax.axis_index("radial")

    @pl.when(stream == 0)
    def _():
        grid[0, inner] = blank

    @pl.when(stream == lax.axis_size("stream") - 1)
    def _():
        grid[9, inner] = blank

    @pl.when(radial == 0)
    def _():
        grid[inner, 0] = blank

    @pl.when(radial == lax.axis_size("radial") - 1)
    def _():
        grid[inner, 9] = blank

    rate = spread_ref[...]
    keep = 1.0 - 6.0 * rate

    def step(i, carry):
        for j in range(8):
            b = i * 8 + j
            here = grid[i + 1, j + 1]
            behind = grid[i, j + 1]
            low = pltpu.roll(halo[0], lax.rem(128 - b, 128), 1)
            high = pltpu.roll(halo[1], 127 - b, 1)
            left = jnp.where(lane == 0, low, pltpu.roll(here, 1, 1))
            right = jnp.where(lane == 127, high, pltpu.roll(here, 127, 1))
            beside = (behind + grid[i + 2, j + 1]) + (grid[i + 1, j] + grid[i + 1, j + 2])
            beside = beside + (left + right)
            speed = courant_ref[pl.ds(b, 1), :]
            out[b] = (keep - speed) * here + rate * beside + speed * behind
        return carry

    lax.fori_loop(0, 8, step, 0)


def chemistry(lists_ref, state, rates_ref, sums_ref, out, send, recv, reply, back, result, sems, met):
    def pack(s, carry):
        send[s] = state[lists_ref[SEND_AT + s]]
        return carry

    lax.fori_loop(0, SLOTS, pack, 0)
    met()
    peers = partners()

    def exchange(source, target, first, turned):
        found = []
        for k, (base, size) in enumerate(zip(BASES, SIZES)):
            area = pl.ds(base, size)
            peer = peers[OPPOSITE[k] if turned else k]
            found.append(remote(source.at[area], target.at[area], sems, first + k, peer))
            found[-1].start()
        return found

    def run(first, items):
        whole = subcycles(jnp.concatenate(items, 1), rates_ref, sums_ref)
        for k in range(len(items)):
            result[first + k] = whole[:, k * 128 : (k + 1) * 128]

    def own(first):
        run(first, [state[lists_ref[WORK_AT + first + k]] for k in range(GROUP)])

    def any_item(slot):
        code = lists_ref[WORK_AT + slot]
        there = recv[jnp.maximum(code - 64, 0)]
        return jnp.where(code < 64, state[jnp.minimum(code, 63)], there)

    def middle(g, carry):
        first = EARLY + g * GROUP
        run(first, [any_item(first + k) for k in range(GROUP)])
        return carry

    copies = exchange(send, recv, 0, False)
    own(0)
    for copy in copies:
        copy.wait()
    lax.fori_loop(0, SPAN // GROUP, middle, 0)

    def answer(s, carry):
        reply[s] = result[lists_ref[REPLY_AT + s]]
        return carry

    lax.fori_loop(0, SLOTS, answer, 0)
    copies = exchange(reply, back, 7, True)
    own(WORK - LATE)
    for copy in copies:
        copy.wait()

    def settle(b, carry):
        code = lists_ref[FINAL_AT + b]
        here = state[jnp.minimum(code, 63)]
        there = back[jnp.clip(code - 64, 0, SLOTS - 1)]
        done = result[jnp.clip(code - 128, 0, WORK - 1)]
        out[b] = jnp.where(code < 64, here, jnp.where(code < 128, there, done))
        return carry

    lax.fori_loop(0, 64, settle, 0)


STATE = (64, ROWS, 128)
MOVE_SCRATCH = [
    pltpu.VMEM((10, 10, ROWS, 128), F32),
    pltpu.VMEM((2, ROWS, 128), F32),
    pltpu.VMEM((2, ROWS, 128), F32),
    pltpu.SemaphoreType.DMA((6,)),
    pltpu.SemaphoreType.DMA((6,)),
]
CHEM_SCRATCH = [pltpu.VMEM((SLOTS, ROWS, 128), F32)] * 4 + [
    pltpu.VMEM((WORK, ROWS, 128), F32),
    pltpu.SemaphoreType.DMA((14,)),
    pltpu.SemaphoreType.DMA((14,)),
]


def communicating(kernel, name, smem, args, scratch):
    vmem = pl.BlockSpec(memory_space=pltpu.VMEM)
    specs = [pl.BlockSpec(memory_space=pltpu.SMEM)] * smem + [vmem] * (len(args) - smem)
    return pl.pallas_call(
        kernel,
        out_shape=jax.ShapeDtypeStruct(STATE, F32),
        in_specs=specs,
        out_specs=vmem,
        scratch_shapes=scratch,
        compiler_params=pltpu.CompilerParams(
            collective_id=name, has_side_effects=True, vmem_limit_bytes=LIMIT
        ),
    )(*args)


def first_move(species, heat, courant, spread):
    def kernel(species_ref, heat_ref, courant_ref, spread_ref, out, grid, edge, halo, *sems):
        def fill(b, cell):
            cell[pl.ds(0, 53), :] = species_ref[pl.ds(b, 53, stride=64), :]
            cell[pl.ds(53, 1), :] = heat_ref[pl.ds(b, 1), :]
            cell[pl.ds(54, 2), :] = jnp.zeros((2, 128), F32)

        met = greet(faces())
        transport(fill, met, courant_ref, spread_ref, out, grid, edge, halo, sems)

    return communicating(kernel, 0, 0, (species, heat, courant, spread), MOVE_SCRATCH)


def first_chem(lists, state, rates, sums):
    def kernel(lists_ref, state_ref, rates_ref, sums_ref, out, *scratch):
        met = greet(partners())
        chemistry(lists_ref, state_ref, rates_ref, sums_ref, out, *scratch[:5], scratch[5:], met)

    return communicating(kernel, 1, 1, (lists, state, rates, sums), CHEM_SCRATCH)


def second_step(lists, state, courant, spread, rates, sums):
    def kernel(lists_ref, state_ref, courant_ref, spread_ref, rates_ref, sums_ref, out, *scratch):
        grid, edge, halo, *sems = scratch[: len(MOVE_SCRATCH)]
        moved, *others = scratch[len(MOVE_SCRATCH) :]

        def fill(b, cell):
            cell[...] = state_ref[b]

        met = greet(faces() + [shifted("stream", 2), shifted("stream", -2)])
        transport(fill, met, courant_ref, spread_ref, moved, grid, edge, halo, sems)
        chemistry(
            lists_ref, moved, rates_ref, sums_ref, out, *others[:5], others[5:], lambda: None
        )

    scratch = MOVE_SCRATCH + [pltpu.VMEM(STATE, F32)] + CHEM_SCRATCH
    return communicating(kernel, 2, 1, (lists, state, courant, spread, rates, sums), scratch)


def shards(
    component_fractions,
    kilokelvin_field,
    axial_courant_number,
    spreading_number,
    arrhenius_multiplier_exponent,
    thermal_exponents,
    arrhenius_barrier,
    balance_constant_exponents,
    enthalpy_formation,
    consumed_stoich_matrix,
    yield_stoich_matrix,
    processor_tiles_burning,
    tile_transfer_tally,
):
    shape = component_fractions.shape
    rates, sums = weights(
        consumed_stoich_matrix,
        yield_stoich_matrix,
        arrhenius_multiplier_exponent,
        thermal_exponents,
        arrhenius_barrier,
        balance_constant_exponents,
        enthalpy_formation,
    )
    species = component_fractions.reshape(53 * 64, 128)
    heat = kilokelvin_field.reshape(64, 128)
    courant = axial_courant_number.reshape(64, 128)
    spread = jnp.broadcast_to(jnp.pad(spreading_number, (0, 2))[:, None], (ROWS, 128))
    blocks, tally = processor_tiles_burning, tile_transfer_tally
    count = jnp.sum(tally, 1)
    counts = lax.all_gather(count, AXES, tiled=True)[None]
    me = jnp.int32(0)
    for axis in AXES:
        me = me * lax.axis_size(axis) + lax.axis_index(axis)
    lists = plan(me[None], blocks, counts)
    state = first_move(species, heat, courant, spread)
    state = first_chem(lists, state, rates, sums)
    state = react_rest(lists, blocks, state, rates, sums)
    state = second_step(lists, state, courant, spread, rates, sums)
    species, heat = finish(lists, blocks, state, rates, sums)
    return species.reshape(shape), heat.reshape(shape[1:])


def solution(mesh):
    in_specs = (
        P(None, "stream", "radial", "azim"),
        P("stream", "radial", "azim"),
        P("stream", "radial", "azim"),
        P(),
        P(),
        P(),
        P(),
        P(),
        P(),
        P(),
        P(),
        P(AXES, None),
        P(AXES, None),
    )
    out_specs = (P(None, "stream", "radial", "azim"), P("stream", "radial", "azim"))
    return jax.shard_map(shards, mesh=mesh, in_specs=in_specs, out_specs=out_specs, check_vma=False)
```

time: 125 us -> 164 us (1.31)
  the two profiles are of different devices: /device:TPU:78 before, /device:TPU:0 now
where the time goes in v2:
time: 164 us
  Pallas kernels  82.4 us (50%)
  blocking collectives  68.1 us (42%)
  local copies, waits for them, and re-layouts  7.91 us (5%)
  other arithmetic  4.54 us (3%)
    pallas_call x3, Pallas kernels, communicating(): pl.pallas_call(kernel, out_shape=jax.ShapeDtypeStruct(STATE, F32), in_spe...  72 us
    unnamed x1, blocking collectives  68.1 us
    pallas_call x1, Pallas kernels, plan(): pl.pallas_call(plan_kernel, out_shape=jax.ShapeDtypeStruct((256,), jnp.in...  6.3 us
    unnamed x22, local copies, waits for them, and re-layouts  5.99 us
    pallas_call x1, Pallas kernels, finish(): pl.pallas_call(last_kernel, out_shape=[jax.ShapeDtypeStruct((53 * 64, 128...  3.53 us

profile of v2, /device:TPU:0, one launch (start us, length us, event | category | flops | bytes accessed | tf_op | source)
XLA Modules:
  0.0 163.9 jit_solution(10171136059436250770)
XLA Ops:
  0.6 1.3 reduce_sum.20
  1.9 0.7 pad.18
  2.6 0.8 dynamic-update-slice
  3.4 68.1 %all-reduce.5 = s32[128]{0:T(128)} all-reduce(s32[128]{0:T(128)S(1)} %dynamic-update-slice), channel_id=1, replica_groups=mesh['stream'=8,'radial'=4,'azim'=4] {'stream','radial','azim'}, use_global_device_ids=true, to_apply=%add.5 | all-reduce | flops 128 | bytes 1024
  71.5 6.3 %shard_map.140.lists_ref = s32[256]{0:T(256)} custom-call(s32[1]{0:T(128)} %bitcast.me_ref, s32[1,64]{1,0:T(1,128)} %blocks_ref.5, s32[1,128]{1,0:T(1,128)} %bitcast.18), custom_call_target="tpu_custom_call" | custom-call | tf_op jit(solution)/shard_map/pallas_call | solution.py:189
  77.8 0.7 broadcast_multiply_fusion.2
  78.5 1.0 multiply_reduce_fusion
  79.5 0.7 broadcast_multiply_fusion.1
  80.2 0.1 broadcast_in_dim.10.spread_ref
  80.3 0.1 mul.72
  80.4 0.0 copy-start.7
  80.4 0.0 copy-start.8
  80.4 0.1 mul.71
  80.5 0.1 mul.73
  80.6 0.8 broadcast_in_dim.12
  81.4 1.0 copy.18
  82.5 1.0 copy.22
  83.5 0.2 pad_maximum_fusion.2
  83.7 0.0 copy-start.2
  83.7 0.0 copy-start.3
  83.7 0.0 copy-start.4
  83.8 0.1 fusion.4
  83.8 0.3 pad_maximum_fusion.1.rates_ref.rates_any
  84.2 0.0 copy-done.7
  84.2 0.0 copy-done.8
  84.2 0.1 concatenate.29
  84.3 0.1 reduce-precision_convert_fusion
  84.5 0.7 copy-done.2
  85.2 0.0 copy-done.3
  85.2 0.0 copy-done.4
  85.2 0.0 copy-start.5
  85.2 11.0 %shard_map.141.state_ref = f32[64,56,128]{2,1,0:T(8,128)S(1)} custom-call(f32[3392,128]{1,0:T(8,128)S(1)} %bitcast.14, f32[64,128]{1,0:T(8,128)S(1)} %bitcast.17, f32[64,128]{1,0:T(8,128)S(1)} %bitcast.15, f32[56,128]{1,0:T(8,128)S(1)} %broadcast_in_dim.10.spread_ref), custom_call_target="tpu_custom_call" | custom-call | tf_op jit(solution)/shard_map/pallas_call | solution.py:479
  96.2 0.0 copy-start.1
  96.2 1.2 copy-done.1
  97.4 0.0 copy-done.5
  97.4 0.0 copy-start.6
  97.4 25.3 %shard_map.142.state_ref = f32[64,56,128]{2,1,0:T(8,128)S(1)} custom-call(s32[256]{0:T(256)S(1)} %copy-done.5, f32[64,56,128]{2,1,0:T(8,128)} %copy-done.1, bf16[656,224]{1,0:T(8,128)(2,1)S(1)} %pad_maximum_fusion.1.rates_ref.rates_any, bf16[224,656]{1,0:T(8,128)(2,1)S(1)} %pad_maximum_fusion.sums_ref.sums_any), custom_call_target="tpu_custom_call" | custom-call | tf_op jit(solution)/shard_map/pallas_call | solution.py:479
  122.7 0.0 copy-done.6
  122.7 0.6 shard_map.143.state_ref
  123.3 0.0 copy-start
  123.3 1.2 copy-done
  124.6 35.8 %shard_map.144.state_ref = f32[64,56,128]{2,1,0:T(8,128)S(1)} custom-call(s32[256]{0:T(256)S(1)} %copy-done.5, f32[64,56,128]{2,1,0:T(8,128)} %copy-done, f32[64,128]{1,0:T(8,128)S(1)} %bitcast.16, f32[56,128]{1,0:T(8,128)S(1)} %broadcast_in_dim.10.spread_ref, bf16[656,224]{1,0:T(8,128)(2,1)S(1)} %pad_maximum_fusion.1.rates_ref.rates_any, ...), custom_call_target="tpu_custom_call" | custom-call | tf_op jit(solution)/shard_map/pallas_call | solution.py:479
  160.3 3.5 %shard_map.145 = (f32[3392,128]{1,0:T(8,128)}, f32[64,128]{1,0:T(8,128)}) custom-call(s32[256]{0:T(256)S(1)} %copy-done.5, s32[1,64]{1,0:T(1,128)S(1)} %copy-done.6, f32[64,56,128]{2,1,0:T(8,128)S(1)} %shard_map.144.state_ref, bf16[656,224]{1,0:T(8,128)(2,1)S(1)} %pad_maximum_fusion.1.rates_ref.rates_any, bf16[224,656]{1,0:T(8,128)(2,1)S(1)} %pad_maximum_fusion.sums_ref.sums_any), custom_call_target="tpu_custom_call" | custom-call | tf_op jit(solution)/shard_map/pallas_call | solution.py:283
  (8 shorter events, 0.1 us)
Async XLA Ops:
  80.4 3.8 %copy-start.7 = (f32[53,325]{1,0:T(8,128)S(1)}, f32[53,325]{1,0:T(8,128)}, u32[]{:S(2)}) copy-start(f32[53,325]{1,0:T(8,128)} %param.22) | copy-start | bytes 206704
  80.4 3.8 %copy-start.8 = (f32[53,325]{1,0:T(8,128)S(1)}, f32[53,325]{1,0:T(8,128)}, u32[]{:S(2)}) copy-start(f32[53,325]{1,0:T(8,128)} %param.23) | copy-start | bytes 206704
  83.7 1.5 copy-start.2
  83.7 1.5 copy-start.3
  83.7 1.4 copy-start.4
  85.2 12.2 %copy-start.5 = (s32[256]{0:T(256)S(1)}, s32[256]{0:T(256)}, u32[]{:S(2)}) copy-start(s32[256]{0:T(256)} %shard_map.140.lists_ref) | copy-start | bytes 3076
  96.2 1.2 copy-start.1
  97.4 25.3 %copy-start.6 = (s32[1,64]{1,0:T(1,128)S(1)}, s32[1,64]{1,0:T(1,128)}, u32[]{:S(2)}) copy-start(s32[1,64]{1,0:T(1,128)} %blocks_ref.5) | copy-start | bytes 772
  123.3 1.2 copy-start

commit v3 on v2

--- a/solution.py
+++ b/solution.py
@@ -33,33 +33,40 @@
 SEND_AT, WORK_AT, REPLY_AT, FINAL_AT, REST_AT = 0, 64, 96, 160, 224
 
 
-def halves(value):
-    high = lax.reduce_precision(value, 8, 7)
-    low = lax.reduce_precision(value - high, 8, 7)
-    return high.astype(BF16), low.astype(BF16)
-
-
-def weights(consumed, made, exponent, thermal, barrier, balance, enthalpy):
-    nspec, nrxn = consumed.shape
-    padded = -(-nrxn // 8) * 8
-
-    def columns(table, constant):
-        rows = [table, thermal[None], -LOG2E * barrier[None], LOG2E * constant[None]]
-        return jnp.pad(jnp.concatenate(rows, 0), ((0, 0), (0, padded - nrxn)))
-
-    ahead = columns(consumed, exponent)
-    back = columns(made, exponent - balance)
-    high, low = halves(jnp.concatenate([ahead, back], 1).T)
-    rates = jnp.concatenate([high, high, low, high], 1)
-    heat = LOG2E * jnp.sum(enthalpy[:, None] * (made - consumed), 0, keepdims=True)
-
-    def stack(gain, loss, warm):
-        rows = [gain, warm, jnp.zeros((2, nrxn), F32), loss, jnp.zeros((3, nrxn), F32)]
-        return jnp.pad(jnp.concatenate(rows, 0), ((0, 0), (0, padded - nrxn)))
-
-    both = jnp.concatenate([stack(made, consumed, heat), stack(consumed, made, -heat)], 1)
-    high, low = halves(chem_step * both)
-    return rates, jnp.concatenate([high, low], 0)
+def prepare(consumed, made, exponent, thermal, barrier, balance, enthalpy, rates, sums, table):
+    half = rates.shape[0] // 2
+
+    def put(side, row, value):
+        rows, lanes = value.shape
+        table[pl.ds(row, rows), pl.ds(side * half, lanes)] = value
+
+    def halves(value):
+        high = value.astype(BF16).astype(F32)
+        return high, value - high
+
+    table[...] = jnp.zeros_like(table)
+    for side, change in enumerate((0.0, balance[...])):
+        put(side, 0, (consumed, made)[side][...])
+        put(side, 53, thermal[...])
+        put(side, 54, -LOG2E * barrier[...])
+        put(side, 55, LOG2E * (exponent[...] - change))
+    high, low = halves(table[:ROWS])
+    stacked = jnp.concatenate([high, high, low, high], 0).T
+    rates[...] = stacked[: 2 * half].astype(BF16)
+    heat = LOG2E * lax.dot_general(
+        enthalpy[...],
+        made[...] - consumed[...],
+        (((1,), (0,)), ((), ())),
+        preferred_element_type=F32,
+        precision=lax.Precision.HIGHEST,
+    )
+    table[...] = jnp.zeros_like(table)
+    for side, (gain, loss, warm) in enumerate(((made, consumed, heat), (consumed, made, -heat))):
+        put(side, 0, gain[...])
+        put(side, 53, warm)
+        put(side, ROWS, loss[...])
+    high, low = halves(chem_step * table[...])
+    sums[...] = jnp.concatenate([high, low], 0)[:, : 2 * half].astype(BF16)
 
 
 def parted(value):
@@ -127,12 +134,11 @@
     return own, given, taken
 
 
-def plan_kernel(me_ref, blocks_ref, counts_ref, out_ref):
-    counts = jnp.broadcast_to(counts_ref[...], (8, 128))
+def plan(me, counts, blocks_ref, lists, codes, codes_smem, sem):
     own, given, taken = flows(counts)
     place = lax.broadcasted_iota(jnp.int32, (8, 128), 0) * 128
-    place = place + lax.broadcasted_iota(jnp.int32, (8, 128), 1)
-    mine = place == me_ref[0]
+    lane = lax.broadcasted_iota(jnp.int32, (8, 128), 1)
+    mine = place + lane == me
 
     def pick(value):
         return jnp.sum(jnp.where(mine, value, 0))
@@ -141,57 +147,61 @@
     given, taken = [pick(v) for v in given], [pick(v) for v in taken]
     received = sum(taken)
     kept = jnp.minimum(own, WORK - received)
-
-    def clear(k, carry):
-        out_ref[k] = 0
-        return carry
-
-    def clear_final(k, carry):
-        out_ref[FINAL_AT + k] = k
-        return carry
-
-    lax.fori_loop(0, FINAL_AT, clear, 0)
-    lax.fori_loop(0, 64, clear_final, 0)
-
-    def keep(o, carry):
-        block = blocks_ref[0, o]
-        late = WORK - LATE + o - EARLY
-        middle = EARLY + received + o - EARLY - LATE
-        slot = jnp.where(o < EARLY, o, jnp.where(o < EARLY + LATE, late, middle))
-        out_ref[WORK_AT + slot] = block
-        out_ref[FINAL_AT + block] = 128 + slot
-        return carry
-
-    lax.fori_loop(0, kept, keep, 0)
-    start, reached = kept, jnp.int32(EARLY)
+    sent_before, taken_before = [kept], [jnp.int32(0)]
+    for p in range(len(SIZES)):
+        sent_before.append(sent_before[p] + given[p])
+        taken_before.append(taken_before[p] + taken[p])
+
+    position = jnp.zeros((8, 128), jnp.int32)
+    for n in range(64):
+        position = jnp.where(lane == blocks_ref[0, n], n, position)
+    late = WORK - LATE - EARLY + position
+    middle = received + position - LATE
+    slot = jnp.where(position < EARLY, position, jnp.where(position < EARLY + LATE, late, middle))
+    code = jnp.where(position < kept, 128 + slot, lane)
     for p, base in enumerate(BASES):
-
-        def give(k, carry):
-            block = blocks_ref[0, start + k]
-            out_ref[SEND_AT + base + k] = block
-            out_ref[FINAL_AT + block] = 64 + base + k
+        inside = (position >= sent_before[p]) & (position < sent_before[p + 1])
+        code = jnp.where(inside, 64 + base + position - sent_before[p], code)
+    codes[...] = code
+    copy = pltpu.make_async_copy(codes, codes_smem, sem)
+    copy.start()
+
+    for p, (base, size) in enumerate(zip(BASES, SIZES)):
+
+        def per_slot(k, carry):
+            at = jnp.clip(sent_before[p] + k, 0, 63)
+            lists[SEND_AT + base + k] = blocks_ref[0, at]
+            lists[REPLY_AT + base + k] = jnp.clip(EARLY + taken_before[p] + k, 0, WORK - 1)
             return carry
 
-        def take(k, carry):
-            out_ref[WORK_AT + reached + k] = 64 + base + k
-            out_ref[REPLY_AT + base + k] = reached + k
-            return carry
-
-        lax.fori_loop(0, given[p], give, 0)
-        lax.fori_loop(0, taken[p], take, 0)
-        start, reached = start + given[p], reached + taken[p]
-    out_ref[REST_AT] = start
-    out_ref[REST_AT + 1] = total
-
-
-def plan(me, blocks, counts):
-    smem = pl.BlockSpec(memory_space=pltpu.SMEM)
-    return pl.pallas_call(
-        plan_kernel,
-        out_shape=jax.ShapeDtypeStruct((256,), jnp.int32),
-        in_specs=[smem, smem, pl.BlockSpec(memory_space=pltpu.VMEM)],
-        out_specs=smem,
-    )(me, blocks, counts)
+        lax.fori_loop(0, size, per_slot, 0)
+
+    def per_early(w, carry):
+        lists[WORK_AT + w] = blocks_ref[0, w]
+        lists[WORK_AT + WORK - LATE + w] = blocks_ref[0, EARLY + w]
+        return carry
+
+    lax.fori_loop(0, EARLY, per_early, 0)
+
+    def per_middle(j, carry):
+        at = jnp.clip(EARLY + LATE + j - received, 0, 63)
+        value = blocks_ref[0, at]
+        for p, base in enumerate(BASES):
+            inside = (j >= taken_before[p]) & (j < taken_before[p + 1])
+            value = jnp.where(inside, 64 + base + j - taken_before[p], value)
+        lists[WORK_AT + EARLY + j] = value
+        return carry
+
+    lax.fori_loop(0, SPAN, per_middle, 0)
+    lists[REST_AT] = sent_before[-1]
+    lists[REST_AT + 1] = total
+    copy.wait()
+
+    def per_block(b, carry):
+        lists[FINAL_AT + b] = codes_smem[0, b]
+        return carry
+
+    lax.fori_loop(0, 64, per_block, 0)
 
 
 def subcycles(state, rates_ref, sums_ref):
@@ -323,7 +333,7 @@
     )
 
 
-def transport(fill, met, courant_ref, spread_ref, out, grid, edge, halo, sems):
+def transport(fill, met, beside, courant_ref, spread_ref, out, grid, edge, halo, sems):
     lane = lax.broadcasted_iota(jnp.int32, (ROWS, 128), 1)
 
     def load(i, carry):
@@ -353,6 +363,7 @@
     copies = [remote(*plans[k], sems, k, peers[k]) for k in range(6)]
     for copy in copies:
         copy.start()
+    beside()
     for copy in copies:
         copy.wait()
     blank = jnp.zeros((8, ROWS, 128), F32)
@@ -386,10 +397,10 @@
             high = pltpu.roll(halo[1], 127 - b, 1)
             left = jnp.where(lane == 0, low, pltpu.roll(here, 1, 1))
             right = jnp.where(lane == 127, high, pltpu.roll(here, 127, 1))
-            beside = (behind + grid[i + 2, j + 1]) + (grid[i + 1, j] + grid[i + 1, j + 2])
-            beside = beside + (left + right)
+            around = (behind + grid[i + 2, j + 1]) + (grid[i + 1, j] + grid[i + 1, j + 2])
+            around = around + (left + right)
             speed = courant_ref[pl.ds(b, 1), :]
-            out[b] = (keep - speed) * here + rate * beside + speed * behind
+            out[b] = (keep - speed) * here + rate * around + speed * behind
         return carry
 
     lax.fori_loop(0, 8, step, 0)
@@ -473,14 +484,71 @@
 ]
 
 
-def communicating(kernel, name, smem, args, scratch):
-    vmem = pl.BlockSpec(memory_space=pltpu.VMEM)
-    specs = [pl.BlockSpec(memory_space=pltpu.SMEM)] * smem + [vmem] * (len(args) - smem)
+COUNT_SCRATCH = [
+    pltpu.VMEM((8, 8, 128), jnp.int32),
+    pltpu.VMEM((4, 8, 128), jnp.int32),
+    pltpu.VMEM((4, 4, 8, 128), jnp.int32),
+    pltpu.SemaphoreType.DMA((13,)),
+    pltpu.SemaphoreType.DMA((13,)),
+    pltpu.VMEM((8, 128), jnp.int32),
+    pltpu.SMEM((8, 128), jnp.int32),
+    pltpu.SemaphoreType.DMA(()),
+    pltpu.VMEM((2 * ROWS, 768), F32),
+]
+
+
+def others(axis):
+    return [shifted(axis, step) for step in range(1, lax.axis_size(axis))]
+
+
+def spread_counts(first, second, third, sems):
+    stream, radial, azim = (lax.axis_index(axis) for axis in AXES)
+
+    def stage(source, target, axis, start):
+        copies = [remote(source, target, sems, start + k, p) for k, p in enumerate(others(axis))]
+        for copy in copies:
+            copy.start()
+
+        def wait():
+            for copy in copies:
+                copy.wait()
+
+        return wait
+
+    def along_stream():
+        return stage(first.at[stream], first.at[stream], "stream", 0)
+
+    def along_radial():
+        row = lax.broadcasted_iota(jnp.int32, (8, 128), 0)
+        joined = first[0]
+        for s in range(1, 8):
+            joined = jnp.where(row == s, first[s], joined)
+        second[radial] = joined
+        return stage(second.at[radial], second.at[radial], "radial", 7)
+
+    def along_azim():
+        third[azim] = second[...]
+        return stage(third.at[azim], third.at[azim], "azim", 10)
+
+    def whole():
+        row = lax.broadcasted_iota(jnp.int32, (8, 128), 0)
+        lane = lax.broadcasted_iota(jnp.int32, (8, 128), 1)
+        total = jnp.zeros((8, 128), jnp.int32)
+        for a in range(4):
+            for r in range(4):
+                here = (lane & 15 == r * 4 + a) & (lane >> 4 == row)
+                total = jnp.where(here, third[a, r], total)
+        return jnp.broadcast_to(jnp.sum(total, 0, keepdims=True), (8, 128))
+
+    return along_stream, along_radial, along_azim, whole
+
+
+def communicating(kernel, name, out_shape, out_specs, specs, args, scratch):
     return pl.pallas_call(
         kernel,
-        out_shape=jax.ShapeDtypeStruct(STATE, F32),
+        out_shape=out_shape,
         in_specs=specs,
-        out_specs=vmem,
+        out_specs=out_specs,
         scratch_shapes=scratch,
         compiler_params=pltpu.CompilerParams(
             collective_id=name, has_side_effects=True, vmem_limit_bytes=LIMIT
@@ -488,43 +556,89 @@
     )(*args)
 
 
-def first_move(species, heat, courant, spread):
-    def kernel(species_ref, heat_ref, courant_ref, spread_ref, out, grid, edge, halo, *sems):
+def first_step(blocks, tally, species, heat, courant, spread, settings):
+    nrxn = settings[0].shape[1]
+    padded = -(-nrxn // 8) * 8
+
+    def kernel(blocks_ref, tally_ref, species_ref, heat_ref, courant_ref, spread_ref, *refs):
+        settings_refs, refs = refs[: len(settings)], refs[len(settings) :]
+        out, lists, rates, sums = refs[:4]
+        scratch = refs[4:]
+        grid, edge, halo, *sems = scratch[: len(MOVE_SCRATCH)]
+        scratch = scratch[len(MOVE_SCRATCH) :]
+        first, second, third, *count_sems = scratch[:5]
+        codes, codes_smem, code_sem, table = scratch[5:9]
+        moved, *chem = scratch[9:]
+
         def fill(b, cell):
             cell[pl.ds(0, 53), :] = species_ref[pl.ds(b, 53, stride=64), :]
             cell[pl.ds(53, 1), :] = heat_ref[pl.ds(b, 1), :]
             cell[pl.ds(54, 2), :] = jnp.zeros((2, 128), F32)
 
-        met = greet(faces())
-        transport(fill, met, courant_ref, spread_ref, out, grid, edge, halo, sems)
-
-    return communicating(kernel, 0, 0, (species, heat, courant, spread), MOVE_SCRATCH)
-
-
-def first_chem(lists, state, rates, sums):
-    def kernel(lists_ref, state_ref, rates_ref, sums_ref, out, *scratch):
-        met = greet(partners())
-        chemistry(lists_ref, state_ref, rates_ref, sums_ref, out, *scratch[:5], scratch[5:], met)
-
-    return communicating(kernel, 1, 1, (lists, state, rates, sums), CHEM_SCRATCH)
+        met = greet(others("stream") + others("radial") + others("azim"))
+        stream, radial, azim = (lax.axis_index(axis) for axis in AXES)
+        me = (stream * 4 + radial) * 4 + azim
+        own = jnp.sum(tally_ref[...], 1, keepdims=True)
+        first[stream] = jnp.broadcast_to(own, (8, 128))
+        stages = spread_counts(first, second, third, count_sems)
+        waiting = []
+
+        def ready():
+            met()
+            waiting.append(stages[0]())
+
+        def beside():
+            waiting[0]()
+            wait = stages[1]()
+            prepare(*settings_refs, rates, sums, table)
+            wait()
+            stages[2]()()
+            plan(me, stages[3](), blocks_ref, lists, codes, codes_smem, code_sem)
+
+        transport(fill, ready, beside, courant_ref, spread_ref, moved, grid, edge, halo, sems)
+        chemistry(lists, moved, rates, sums, out, *chem[:5], chem[5:], lambda: None)
+
+    smem, vmem = pl.BlockSpec(memory_space=pltpu.SMEM), pl.BlockSpec(memory_space=pltpu.VMEM)
+    args = (blocks, tally, species, heat, courant, spread, *settings)
+    return communicating(
+        kernel,
+        0,
+        [
+            jax.ShapeDtypeStruct(STATE, F32),
+            jax.ShapeDtypeStruct((256,), jnp.int32),
+            jax.ShapeDtypeStruct((2 * padded, 4 * ROWS), BF16),
+            jax.ShapeDtypeStruct((4 * ROWS, 2 * padded), BF16),
+        ],
+        [vmem, smem, vmem, vmem],
+        [smem] + [vmem] * (len(args) - 1),
+        args,
+        MOVE_SCRATCH + COUNT_SCRATCH + [pltpu.VMEM(STATE, F32)] + CHEM_SCRATCH,
+    )
 
 
 def second_step(lists, state, courant, spread, rates, sums):
     def kernel(lists_ref, state_ref, courant_ref, spread_ref, rates_ref, sums_ref, out, *scratch):
         grid, edge, halo, *sems = scratch[: len(MOVE_SCRATCH)]
-        moved, *others = scratch[len(MOVE_SCRATCH) :]
+        moved, *chem = scratch[len(MOVE_SCRATCH) :]
 
         def fill(b, cell):
             cell[...] = state_ref[b]
 
         met = greet(faces() + [shifted("stream", 2), shifted("stream", -2)])
-        transport(fill, met, courant_ref, spread_ref, moved, grid, edge, halo, sems)
-        chemistry(
-            lists_ref, moved, rates_ref, sums_ref, out, *others[:5], others[5:], lambda: None
-        )
-
-    scratch = MOVE_SCRATCH + [pltpu.VMEM(STATE, F32)] + CHEM_SCRATCH
-    return communicating(kernel, 2, 1, (lists, state, courant, spread, rates, sums), scratch)
+        nothing = lambda: None
+        transport(fill, met, nothing, courant_ref, spread_ref, moved, grid, edge, halo, sems)
+        chemistry(lists_ref, moved, rates_ref, sums_ref, out, *chem[:5], chem[5:], nothing)
+
+    smem, vmem = pl.BlockSpec(memory_space=pltpu.SMEM), pl.BlockSpec(memory_space=pltpu.VMEM)
+    return communicating(
+        kernel,
+        1,
+        jax.ShapeDtypeStruct(STATE, F32),
+        vmem,
+        [smem] + [vmem] * 5,
+        (lists, state, courant, spread, rates, sums),
+        MOVE_SCRATCH + [pltpu.VMEM(STATE, F32)] + CHEM_SCRATCH,
+    )
 
 
 def shards(
@@ -543,28 +657,21 @@
     tile_transfer_tally,
 ):
     shape = component_fractions.shape
-    rates, sums = weights(
+    settings = (
         consumed_stoich_matrix,
         yield_stoich_matrix,
-        arrhenius_multiplier_exponent,
-        thermal_exponents,
-        arrhenius_barrier,
-        balance_constant_exponents,
-        enthalpy_formation,
+        arrhenius_multiplier_exponent[None],
+        thermal_exponents[None],
+        arrhenius_barrier[None],
+        balance_constant_exponents[None],
+        enthalpy_formation[None],
     )
     species = component_fractions.reshape(53 * 64, 128)
     heat = kilokelvin_field.reshape(64, 128)
     courant = axial_courant_number.reshape(64, 128)
     spread = jnp.broadcast_to(jnp.pad(spreading_number, (0, 2))[:, None], (ROWS, 128))
     blocks, tally = processor_tiles_burning, tile_transfer_tally
-    count = jnp.sum(tally, 1)
-    counts = lax.all_gather(count, AXES, tiled=True)[None]
-    me = jnp.int32(0)
-    for axis in AXES:
-        me = me * lax.axis_size(axis) + lax.axis_index(axis)
-    lists = plan(me[None], blocks, counts)
-    state = first_move(species, heat, courant, spread)
-    state = first_chem(lists, state, rates, sums)
+    state, lists, rates, sums = first_step(blocks, tally, species, heat, courant, spread, settings)
     state = react_rest(lists, blocks, state, rates, sums)
     state = second_step(lists, state, courant, spread, rates, sums)
     species, heat = finish(lists, blocks, state, rates, sums)

time: 164 us -> 102 us (0.62)
  blocking collectives: 68.1 us -> 0 us
  Pallas kernels: 82.4 us -> 88.2 us
  local copies, waits for them, and re-layouts: 7.91 us -> 12.9 us
  other arithmetic: 4.54 us -> 0 us
    unnamed x1 -> x0, blocking collectives: 68.1 us -> none
    pallas_call x4 -> x2, Pallas kernels: 78.3 us -> 84.1 us  [communicating(): pl.pallas_call(kernel, out_shape=out_shape, in_specs=specs, out_specs=out...]
    unnamed x22, local copies, waits for them, and re-layouts: 5.99 us -> 9.46 us
    reduce_sum x2 -> x0, other arithmetic: 2.32 us -> none  [the longest x1 1.29 us: shards(): count = jnp.sum(tally, 1)]
    broadcast_in_dim x1 -> x4, local copies, waits for them, and re-layouts: 0.79 us -> 2.73 us  [the longest x1 0.68 us: shards(): arrhenius_multiplier_exponent[None]]
where the time goes in v3:
time: 102 us
  Pallas kernels  88.2 us (86%)
  local copies, waits for them, and re-layouts  12.9 us (13%)
    pallas_call x2, Pallas kernels, communicating(): pl.pallas_call(kernel, out_shape=out_shape, in_specs=specs, out_specs=out...  84.1 us
    unnamed x22, local copies, waits for them, and re-layouts  9.46 us
    pallas_call x1, Pallas kernels, finish(): pl.pallas_call(last_kernel, out_shape=[jax.ShapeDtypeStruct((53 * 64, 128...  3.53 us

profile of v3, /device:TPU:0, one launch (start us, length us, event | category | flops | bytes accessed | tf_op | source)
XLA Modules:
  0.0 101.9 jit_solution(2737580214601117561)
XLA Ops:
  0.6 0.7 pad.4
  1.3 0.7 broadcast_in_dim.22.refs_2_
  2.0 0.7 broadcast_in_dim.23.refs_3_
  2.7 0.7 broadcast_in_dim.24.refs_4_
  3.3 0.7 broadcast_in_dim.25.refs_5_
  4.0 0.1 broadcast_in_dim.21.spread_ref
  4.1 0.0 copy-start.2
  4.1 1.5 %copy-done.2 = f32[53,8,8,128]{3,2,1,0:T(8,128)S(1)} copy-done((f32[53,8,8,128]{3,2,1,0:T(8,128)S(1)}, f32[53,8,8,128]{3,2,1,0:T(8,128)}, u32[]{:S(2)}) %copy-start.2) | copy-done | bytes 1736728
  5.6 0.0 copy-start.3
  5.6 0.8 copy-done.3
  6.3 0.0 copy-start.5
  6.3 0.9 copy-done.5
  7.2 0.0 copy-start.6
  7.2 0.9 copy-done.6
  8.1 0.0 copy-start.7
  8.1 0.8 copy-done.7
  8.9 0.0 copy-start.8
  8.9 0.7 copy-done.8
  9.5 0.0 copy-start.9
  9.5 0.7 copy-done.9
  10.2 0.0 copy-start.10
  10.2 0.7 copy-done.10
  10.8 48.9 %shard_map.140 = (f32[64,56,128]{2,1,0:T(8,128)}, s32[256]{0:T(256)S(1)}, bf16[656,224]{1,0:T(8,128)(2,1)S(1)}, bf16[224,656]{1,0:T(8,128)(2,1)S(1)}) custom-call(s32[1,64]{1,0:T(1,128)S(1)} %copy-done.8, s32[1,128]{1,0:T(1,128)S(1)} %copy-done.9, f32[3392,128]{1,0:T(8,128)S(1)} %bitcast.6, f32[64,128]{1,0:T(8,128)S(1)} %bitcast.9, f32[64,128]{1,0:T(8,128)S(1)} %bitcast.7, ...), custom_call_target="tpu_custom_call" | custom-call | tf_op jit(solution)/shard_map/pallas_call | solution.py:547
  59.7 0.0 copy-start
  59.7 1.5 %copy-done = f32[64,56,128]{2,1,0:T(8,128)S(1)} copy-done((f32[64,56,128]{2,1,0:T(8,128)S(1)}, f32[64,56,128]{2,1,0:T(8,128)}, u32[]{:S(2)}) %copy-start) | copy-done | bytes 1835032
  61.2 0.0 copy-start.4
  61.2 0.6 shard_map.141.state_ref
  61.8 0.0 copy-start.1
  61.8 1.2 %copy-done.1 = f32[64,56,128]{2,1,0:T(8,128)} copy-done((f32[64,56,128]{2,1,0:T(8,128)}, f32[64,56,128]{2,1,0:T(8,128)S(1)}, u32[]{:S(2)}) %copy-start.1) | copy-done | bytes 1835032
  63.0 0.0 copy-done.4
  63.0 35.3 %shard_map.142.state_ref = f32[64,56,128]{2,1,0:T(8,128)S(1)} custom-call(s32[256]{0:T(256)S(1)} %get-tuple-element.8.lists_ref, f32[64,56,128]{2,1,0:T(8,128)} %copy-done.1, f32[64,128]{1,0:T(8,128)S(1)} %bitcast.8, f32[56,128]{1,0:T(8,128)S(1)} %broadcast_in_dim.21.spread_ref, bf16[656,224]{1,0:T(8,128)(2,1)S(1)} %get-tuple-element.10.rates_any.rates_ref, ...), custom_call_target="tpu_custom_call" | custom-call | tf_op jit(solution)/shard_map/pallas_call | solution.py:547
  98.3 3.5 %shard_map.143 = (f32[3392,128]{1,0:T(8,128)}, f32[64,128]{1,0:T(8,128)}) custom-call(s32[256]{0:T(256)S(1)} %get-tuple-element.8.lists_ref, s32[1,64]{1,0:T(1,128)S(1)} %copy-done.8, f32[64,56,128]{2,1,0:T(8,128)S(1)} %shard_map.142.state_ref, bf16[656,224]{1,0:T(8,128)(2,1)S(1)} %get-tuple-element.10.rates_any.rates_ref, ...), custom_call_target="tpu_custom_call" | custom-call | tf_op jit(solution)/shard_map/pallas_call | solution.py:293
Async XLA Ops:
  4.1 1.5 %copy-start.2 = (f32[53,8,8,128]{3,2,1,0:T(8,128)S(1)}, f32[53,8,8,128]{3,2,1,0:T(8,128)}, u32[]{:S(2)}) copy-start(f32[53,8,8,128]{3,2,1,0:T(8,128)} %param.13) | copy-start | bytes 5210116
  5.6 0.8 copy-start.3
  6.3 0.9 copy-start.5
  7.2 0.9 copy-start.6
  8.1 0.8 copy-start.7
  8.9 0.7 copy-start.8
  9.5 0.7 copy-start.9
  10.2 0.7 copy-start.10
  59.7 1.5 %copy-start = (f32[64,56,128]{2,1,0:T(8,128)S(1)}, f32[64,56,128]{2,1,0:T(8,128)}, u32[]{:S(2)}) copy-start(f32[64,56,128]{2,1,0:T(8,128)} %get-tuple-element.9.state_ref) | copy-start | bytes 5505028
  61.2 1.8 %copy-start.4 = (f32[8,8,128]{2,1,0:T(8,128)S(1)}, f32[8,8,128]{2,1,0:T(8,128)}, u32[]{:S(2)}) copy-start(f32[8,8,128]{2,1,0:T(8,128)} %param.15) | copy-start | bytes 98308
  61.8 1.3 %copy-start.1 = (f32[64,56,128]{2,1,0:T(8,128)}, f32[64,56,128]{2,1,0:T(8,128)S(1)}, u32[]{:S(2)}) copy-start(f32[64,56,128]{2,1,0:T(8,128)S(1)} %shard_map.141.state_ref) | copy-start | bytes 5505028

commit v4 on v3

--- a/solution.py
+++ b/solution.py
@@ -17,7 +17,7 @@
 BF16 = jnp.bfloat16
 MESH = pl.DeviceIdType.MESH
 AXES = ("stream", "radial", "azim")
-LIMIT = 50 * 2**20
+LIMIT = 63 * 2**20
 WORK = 32
 EARLY = 8
 LATE = 8
@@ -35,6 +35,9 @@
 
 def prepare(consumed, made, exponent, thermal, barrier, balance, enthalpy, rates, sums, table):
     half = rates.shape[0] // 2
+    exponent, thermal, barrier, balance, enthalpy = (
+        vector[...].reshape(1, -1) for vector in (exponent, thermal, barrier, balance, enthalpy)
+    )
 
     def put(side, row, value):
         rows, lanes = value.shape
@@ -45,16 +48,16 @@
         return high, value - high
 
     table[...] = jnp.zeros_like(table)
-    for side, change in enumerate((0.0, balance[...])):
+    for side, change in enumerate((0.0, balance)):
         put(side, 0, (consumed, made)[side][...])
-        put(side, 53, thermal[...])
-        put(side, 54, -LOG2E * barrier[...])
-        put(side, 55, LOG2E * (exponent[...] - change))
+        put(side, 53, thermal)
+        put(side, 54, -LOG2E * barrier)
+        put(side, 55, LOG2E * (exponent - change))
     high, low = halves(table[:ROWS])
     stacked = jnp.concatenate([high, high, low, high], 0).T
     rates[...] = stacked[: 2 * half].astype(BF16)
     heat = LOG2E * lax.dot_general(
-        enthalpy[...],
+        enthalpy,
         made[...] - consumed[...],
         (((1,), (0,)), ((), ())),
         preferred_element_type=F32,
@@ -204,6 +207,13 @@
     lax.fori_loop(0, 64, per_block, 0)
 
 
+def fetch(pairs, sem):
+    copies = [pltpu.make_async_copy(*pair, sem.at[k]) for k, pair in enumerate(pairs)]
+    for copy in copies:
+        copy.start()
+    return [copy.wait for copy in copies]
+
+
 def subcycles(state, rates_ref, sums_ref):
     return lax.fori_loop(0, NCYC, lambda c, s: cycle(s, rates_ref[...], sums_ref[...]), state)
 
@@ -257,45 +267,78 @@
     )(lists, blocks, state, rates, sums)
 
 
-def last_kernel(lists_ref, blocks_ref, state_ref, rates_ref, sums_ref, species_ref, heat_ref, work):
+def last_kernel(
+    lists_ref, blocks_ref, state_any, rates_any, sums_any, species_any, heat_any, *scratch
+):
+    state, work, species, heat, rates, sums, in_sem, out_sem, sem = scratch
     start, count = lists_ref[REST_AT], lists_ref[REST_AT + 1]
+    rows = [pl.ds(8 * i, 8) for i in range(8)]
+    waits = fetch([(state_any.at[row], state.at[row]) for row in rows], in_sem)
 
     def put(source, b):
-        species_ref[pl.ds(b, 53, stride=64), :] = source[b, pl.ds(0, 53), :]
-        heat_ref[pl.ds(b, 1), :] = source[b, pl.ds(53, 1), :]
-
-    def put_row(i, carry):
+        species[pl.ds(b, 53, stride=64), :] = source[b, pl.ds(0, 53), :]
+        heat[pl.ds(b, 1), :] = source[b, pl.ds(53, 1), :]
+
+    copies = []
+    for i, row in enumerate(rows):
+        waits[i]()
         for j in range(8):
-            put(state_ref, i * 8 + j)
-        return carry
-
-    lax.fori_loop(0, 8, put_row, 0)
-
-    def group(g, carry):
-        first = start + g * GROUP
-        at = [blocks_ref[0, jnp.minimum(first + k, 63)] for k in range(GROUP)]
-        state = jnp.concatenate([state_ref[at[k]] for k in range(GROUP)], 1)
-        state = subcycles(state, rates_ref, sums_ref)
-        for k in range(GROUP):
-
-            @pl.when(first + k < count)
-            def _():
-                work[at[k]] = state[:, k * 128 : (k + 1) * 128]
-                put(work, at[k])
-
-        return carry
-
-    lax.fori_loop(0, (count - start + GROUP - 1) // GROUP, group, 0)
+            put(state, 8 * i + j)
+        view = species.reshape(53, 64, 128).at[:, row]
+        copies.append(pltpu.make_async_copy(view, species_any.at[:, row], out_sem.at[i]))
+        copies[-1].start()
+    copies.append(pltpu.make_async_copy(heat, heat_any, out_sem.at[8]))
+    copies[-1].start()
+    for copy in copies:
+        copy.wait()
+
+    def bring(source, target):
+        copy = pltpu.make_async_copy(source, target, sem)
+        copy.start()
+        copy.wait()
+
+    @pl.when(start < count)
+    def _():
+        bring(rates_any, rates)
+        bring(sums_any, sums)
+
+        def group(g, carry):
+            first = start + g * GROUP
+            at = [blocks_ref[0, jnp.minimum(first + k, 63)] for k in range(GROUP)]
+            value = jnp.concatenate([state[at[k]] for k in range(GROUP)], 1)
+            value = subcycles(value, rates, sums)
+            for k in range(GROUP):
+
+                @pl.when(first + k < count)
+                def _():
+                    work[at[k]] = value[:, k * 128 : (k + 1) * 128]
+                    put(work, at[k])
+
+            return carry
+
+        lax.fori_loop(0, (count - start + GROUP - 1) // GROUP, group, 0)
+        bring(species.reshape(53, 64, 128), species_any)
+        bring(heat, heat_any)
 
 
 def finish(lists, blocks, state, rates, sums):
-    smem, vmem = pl.BlockSpec(memory_space=pltpu.SMEM), pl.BlockSpec(memory_space=pltpu.VMEM)
+    smem, anywhere = pl.BlockSpec(memory_space=pltpu.SMEM), pl.BlockSpec(memory_space=pl.ANY)
     return pl.pallas_call(
         last_kernel,
-        out_shape=[jax.ShapeDtypeStruct((53 * 64, 128), F32), jax.ShapeDtypeStruct((64, 128), F32)],
-        in_specs=[smem, smem] + [vmem] * 3,
-        out_specs=[vmem] * 2,
-        scratch_shapes=[pltpu.VMEM(state.shape, F32)],
+        out_shape=[jax.ShapeDtypeStruct((53, 64, 128), F32), jax.ShapeDtypeStruct((64, 128), F32)],
+        in_specs=[smem, smem] + [anywhere] * 3,
+        out_specs=[anywhere] * 2,
+        scratch_shapes=[
+            pltpu.VMEM(state.shape, F32),
+            pltpu.VMEM(state.shape, F32),
+            pltpu.VMEM((53 * 64, 128), F32),
+            pltpu.VMEM((64, 128), F32),
+            pltpu.VMEM(rates.shape, BF16),
+            pltpu.VMEM(sums.shape, BF16),
+            pltpu.SemaphoreType.DMA((8,)),
+            pltpu.SemaphoreType.DMA((9,)),
+            pltpu.SemaphoreType.DMA(()),
+        ],
         compiler_params=pltpu.CompilerParams(vmem_limit_bytes=LIMIT),
     )(lists, blocks, state, rates, sums)
 
@@ -333,23 +376,8 @@
     )
 
 
-def transport(fill, met, beside, courant_ref, spread_ref, out, grid, edge, halo, sems):
+def transport(met, courant_ref, spread_ref, out, grid, edge, halo, sems, hooks):
     lane = lax.broadcasted_iota(jnp.int32, (ROWS, 128), 1)
-
-    def load(i, carry):
-        low, high = carry
-        for j in range(8):
-            b = i * 8 + j
-            fill(b, grid.at[i + 1, j + 1])
-            here = grid[i + 1, j + 1]
-            low = jnp.where(lane == b, pltpu.roll(here, b, 1), low)
-            high = jnp.where(lane == b, pltpu.roll(here, b + 1, 1), high)
-        return low, high
-
-    low, high = lax.fori_loop(0, 8, load, (jnp.zeros((ROWS, 128), F32),) * 2)
-    edge[0] = low
-    edge[1] = high
-    met()
     peers = faces()
     inner = pl.ds(1, 8)
     plans = [
@@ -361,35 +389,32 @@
         (edge.at[1], halo.at[0]),
     ]
     copies = [remote(*plans[k], sems, k, peers[k]) for k in range(6)]
-    for copy in copies:
-        copy.start()
-    beside()
-    for copy in copies:
-        copy.wait()
-    blank = jnp.zeros((8, ROWS, 128), F32)
-    stream, radial = lax.axis_index("stream"), lax.axis_index("radial")
-
-    @pl.when(stream == 0)
-    def _():
-        grid[0, inner] = blank
-
-    @pl.when(stream == lax.axis_size("stream") - 1)
-    def _():
-        grid[9, inner] = blank
-
-    @pl.when(radial == 0)
-    def _():
-        grid[inner, 0] = blank
-
-    @pl.when(radial == lax.axis_size("radial") - 1)
-    def _():
-        grid[inner, 9] = blank
-
+    met()
+    for k in (2, 3, 0, 1):
+        copies[k].start()
+
+    def ends(i, carry):
+        low, high = carry
+        for j in range(8):
+            b = i * 8 + j
+            here = grid[i + 1, j + 1]
+            low = jnp.where(lane == b, pltpu.roll(here, b, 1), low)
+            high = jnp.where(lane == b, pltpu.roll(here, b + 1, 1), high)
+        return low, high
+
+    low, high = lax.fori_loop(0, 8, ends, (jnp.zeros((ROWS, 128), F32),) * 2)
+    edge[0] = low
+    edge[1] = high
+    copies[4].start()
+    copies[5].start()
+    hooks[0]()
+    copies[4].wait()
+    copies[5].wait()
     rate = spread_ref[...]
     keep = 1.0 - 6.0 * rate
 
-    def step(i, carry):
-        for j in range(8):
+    def cells(i, columns):
+        for j in columns:
             b = i * 8 + j
             here = grid[i + 1, j + 1]
             behind = grid[i, j + 1]
@@ -401,9 +426,45 @@
             around = around + (left + right)
             speed = courant_ref[pl.ds(b, 1), :]
             out[b] = (keep - speed) * here + rate * around + speed * behind
-        return carry
-
-    lax.fori_loop(0, 8, step, 0)
+
+    def middle(i, carry):
+        cells(i, range(1, 7))
+        return carry
+
+    lax.fori_loop(1, 7, middle, 0)
+    hooks[1]()
+    for k in range(4):
+        copies[k].wait()
+    blank = jnp.zeros((8, ROWS, 128), F32)
+    stream, radial = lax.axis_index("stream"), lax.axis_index("radial")
+
+    @pl.when(stream == 0)
+    def _():
+        grid[0, inner] = blank
+
+    @pl.when(stream == lax.axis_size("stream") - 1)
+    def _():
+        grid[9, inner] = blank
+
+    @pl.when(radial == 0)
+    def _():
+        grid[inner, 0] = blank
+
+    @pl.when(radial == lax.axis_size("radial") - 1)
+    def _():
+        grid[inner, 9] = blank
+
+    def sides(i, carry):
+        cells(i, (0, 7))
+        return carry
+
+    def first_last(i, carry):
+        cells(i * 7, range(1, 7))
+        return carry
+
+    lax.fori_loop(0, 8, sides, 0)
+    lax.fori_loop(0, 2, first_last, 0)
+    hooks[2]()
 
 
 def chemistry(lists_ref, state, rates_ref, sums_ref, out, send, recv, reply, back, result, sems, met):
@@ -559,47 +620,72 @@
 def first_step(blocks, tally, species, heat, courant, spread, settings):
     nrxn = settings[0].shape[1]
     padded = -(-nrxn // 8) * 8
-
-    def kernel(blocks_ref, tally_ref, species_ref, heat_ref, courant_ref, spread_ref, *refs):
-        settings_refs, refs = refs[: len(settings)], refs[len(settings) :]
-        out, lists, rates, sums = refs[:4]
-        scratch = refs[4:]
-        grid, edge, halo, *sems = scratch[: len(MOVE_SCRATCH)]
-        scratch = scratch[len(MOVE_SCRATCH) :]
-        first, second, third, *count_sems = scratch[:5]
-        codes, codes_smem, code_sem, table = scratch[5:9]
-        moved, *chem = scratch[9:]
-
-        def fill(b, cell):
-            cell[pl.ds(0, 53), :] = species_ref[pl.ds(b, 53, stride=64), :]
-            cell[pl.ds(53, 1), :] = heat_ref[pl.ds(b, 1), :]
-            cell[pl.ds(54, 2), :] = jnp.zeros((2, 128), F32)
+    brought = (tally, species, heat, courant, spread, *settings)
+
+    def kernel(blocks_ref, *refs):
+        anywhere, refs = refs[: len(brought)], refs[len(brought) :]
+        out, lists, rates, sums, spread_out = refs[:5]
+        near, refs = refs[5 : 5 + len(brought)], refs[5 + len(brought) :]
+        fetch_sem, refs = refs[0], refs[1:]
+        tally_ref, species_ref, heat_ref, courant_ref, spread_ref, *settings_refs = near
+        grid, edge, halo, *sems = refs[: len(MOVE_SCRATCH)]
+        refs = refs[len(MOVE_SCRATCH) :]
+        first, second, third, *count_sems = refs[:5]
+        codes, codes_smem, code_sem, table = refs[5:9]
+        moved, *chem = refs[9:]
 
         met = greet(others("stream") + others("radial") + others("azim"))
+        waits = fetch(list(zip(anywhere, near)), fetch_sem)
         stream, radial, azim = (lax.axis_index(axis) for axis in AXES)
         me = (stream * 4 + radial) * 4 + azim
+        waits[0]()
         own = jnp.sum(tally_ref[...], 1, keepdims=True)
         first[stream] = jnp.broadcast_to(own, (8, 128))
         stages = spread_counts(first, second, third, count_sems)
+        waits[1]()
+        waits[2]()
+
+        def load(i, carry):
+            for j in range(8):
+                b = i * 8 + j
+                cell = grid.at[i + 1, j + 1]
+                cell[pl.ds(0, 53), :] = species_ref[pl.ds(b, 53, stride=64), :]
+                cell[pl.ds(53, 1), :] = heat_ref[pl.ds(b, 1), :]
+                cell[pl.ds(54, 2), :] = jnp.zeros((2, 128), F32)
+            return carry
+
+        lax.fori_loop(0, 8, load, 0)
         waiting = []
 
         def ready():
             met()
             waiting.append(stages[0]())
 
-        def beside():
+        def at_once():
+            for wait in waits[3:]:
+                wait()
+            table[pl.ds(0, 1), pl.ds(0, 128)] = jnp.zeros((1, 128), F32)
+            table[pl.ds(0, 1), pl.ds(0, 54)] = spread_ref[...].reshape(1, 54)
+            row = lax.broadcasted_iota(jnp.int32, (ROWS, 128), 0)
+            lane = lax.broadcasted_iota(jnp.int32, (ROWS, 128), 1)
+            diagonal = jnp.where(row == lane, table[pl.ds(0, 1), pl.ds(0, 128)], 0.0)
+            column = jnp.sum(diagonal, 1, keepdims=True)
+            spread_out[...] = jnp.broadcast_to(column, (ROWS, 128))
             waiting[0]()
-            wait = stages[1]()
+            waiting.append(stages[1]())
             prepare(*settings_refs, rates, sums, table)
-            wait()
-            stages[2]()()
+            waiting[1]()
+            waiting.append(stages[2]())
+
+        def at_end():
+            waiting[2]()
             plan(me, stages[3](), blocks_ref, lists, codes, codes_smem, code_sem)
 
-        transport(fill, ready, beside, courant_ref, spread_ref, moved, grid, edge, halo, sems)
+        hooks = (at_once, lambda: None, at_end)
+        transport(ready, courant_ref, spread_out, moved, grid, edge, halo, sems, hooks)
         chemistry(lists, moved, rates, sums, out, *chem[:5], chem[5:], lambda: None)
 
     smem, vmem = pl.BlockSpec(memory_space=pltpu.SMEM), pl.BlockSpec(memory_space=pltpu.VMEM)
-    args = (blocks, tally, species, heat, courant, spread, *settings)
     return communicating(
         kernel,
         0,
@@ -608,25 +694,40 @@
             jax.ShapeDtypeStruct((256,), jnp.int32),
             jax.ShapeDtypeStruct((2 * padded, 4 * ROWS), BF16),
             jax.ShapeDtypeStruct((4 * ROWS, 2 * padded), BF16),
+            jax.ShapeDtypeStruct((ROWS, 128), F32),
         ],
-        [vmem, smem, vmem, vmem],
-        [smem] + [vmem] * (len(args) - 1),
-        args,
-        MOVE_SCRATCH + COUNT_SCRATCH + [pltpu.VMEM(STATE, F32)] + CHEM_SCRATCH,
+        [vmem, smem, vmem, vmem, vmem],
+        [smem] + [pl.BlockSpec(memory_space=pl.ANY)] * len(brought),
+        (blocks, *brought),
+        [pltpu.VMEM(x.shape, x.dtype) for x in brought]
+        + [pltpu.SemaphoreType.DMA((len(brought),))]
+        + MOVE_SCRATCH
+        + COUNT_SCRATCH
+        + [pltpu.VMEM(STATE, F32)]
+        + CHEM_SCRATCH,
     )
 
 
 def second_step(lists, state, courant, spread, rates, sums):
-    def kernel(lists_ref, state_ref, courant_ref, spread_ref, rates_ref, sums_ref, out, *scratch):
-        grid, edge, halo, *sems = scratch[: len(MOVE_SCRATCH)]
-        moved, *chem = scratch[len(MOVE_SCRATCH) :]
-
-        def fill(b, cell):
-            cell[...] = state_ref[b]
-
+    brought = (courant, spread, rates, sums)
+
+    def kernel(lists_ref, state_any, *refs):
+        anywhere, refs = refs[: len(brought)], refs[len(brought) :]
+        out, near, refs = refs[0], refs[1 : 1 + len(brought)], refs[1 + len(brought) :]
+        fetch_sem, refs = refs[0], refs[1:]
+        courant_ref, spread_ref, rates_ref, sums_ref = near
+        grid, edge, halo, *sems = refs[: len(MOVE_SCRATCH)]
+        moved, *chem = refs[len(MOVE_SCRATCH) :]
         met = greet(faces() + [shifted("stream", 2), shifted("stream", -2)])
+        pairs = [
+            (state_any.at[pl.ds(8 * i, 8)], grid.at[i + 1, pl.ds(1, 8)]) for i in range(8)
+        ]
+        waits = fetch(pairs + list(zip(anywhere, near)), fetch_sem)
+        for wait in waits:
+            wait()
         nothing = lambda: None
-        transport(fill, met, nothing, courant_ref, spread_ref, moved, grid, edge, halo, sems)
+        hooks = (nothing, nothing, nothing)
+        transport(met, courant_ref, spread_ref, moved, grid, edge, halo, sems, hooks)
         chemistry(lists_ref, moved, rates_ref, sums_ref, out, *chem[:5], chem[5:], nothing)
 
     smem, vmem = pl.BlockSpec(memory_space=pltpu.SMEM), pl.BlockSpec(memory_space=pltpu.VMEM)
@@ -635,9 +736,13 @@
         1,
         jax.ShapeDtypeStruct(STATE, F32),
         vmem,
-        [smem] + [vmem] * 5,
-        (lists, state, courant, spread, rates, sums),
-        MOVE_SCRATCH + [pltpu.VMEM(STATE, F32)] + CHEM_SCRATCH,
+        [smem] + [pl.BlockSpec(memory_space=pl.ANY)] * 5,
+        (lists, state, *brought),
+        [pltpu.VMEM(x.shape, x.dtype) for x in brought]
+        + [pltpu.SemaphoreType.DMA((8 + len(brought),))]
+        + MOVE_SCRATCH
+        + [pltpu.VMEM(STATE, F32)]
+        + CHEM_SCRATCH,
     )
 
 
@@ -660,18 +765,19 @@
     settings = (
         consumed_stoich_matrix,
         yield_stoich_matrix,
-        arrhenius_multiplier_exponent[None],
-        thermal_exponents[None],
-        arrhenius_barrier[None],
-        balance_constant_exponents[None],
-        enthalpy_formation[None],
+        arrhenius_multiplier_exponent,
+        thermal_exponents,
+        arrhenius_barrier,
+        balance_constant_exponents,
+        enthalpy_formation,
     )
     species = component_fractions.reshape(53 * 64, 128)
     heat = kilokelvin_field.reshape(64, 128)
     courant = axial_courant_number.reshape(64, 128)
-    spread = jnp.broadcast_to(jnp.pad(spreading_number, (0, 2))[:, None], (ROWS, 128))
     blocks, tally = processor_tiles_burning, tile_transfer_tally
-    state, lists, rates, sums = first_step(blocks, tally, species, heat, courant, spread, settings)
+    state, lists, rates, sums, spread = first_step(
+        blocks, tally, species, heat, courant, spreading_number, settings
+    )
     state = react_rest(lists, blocks, state, rates, sums)
     state = second_step(lists, state, courant, spread, rates, sums)
     species, heat = finish(lists, blocks, state, rates, sums)

time: 102 us -> 87.4 us (0.86)
  local copies, waits for them, and re-layouts: 12.9 us -> 0 us
  Pallas kernels: 88.2 us -> 86.5 us
    unnamed x22 -> x0, local copies, waits for them, and re-layouts: 9.46 us -> none
    broadcast_in_dim x5 -> x0, local copies, waits for them, and re-layouts: 2.8 us -> none  [the longest x1 0.68 us: shards(): arrhenius_multiplier_exponent[None]]
    pallas_call x2, Pallas kernels: 84.1 us -> 81.6 us  [communicating(): pl.pallas_call(kernel, out_shape=out_shape, in_specs=specs, out_specs=out...]
where the time goes in v4:
time: 87.4 us; the launch traced here: 87.2 us
  Pallas kernels  86.5 us (99%)
    pallas_call x2, Pallas kernels, communicating(): pl.pallas_call(kernel, out_shape=out_shape, in_specs=specs, out_specs=out...  81.6 us
    pallas_call x1, Pallas kernels, finish(): pl.pallas_call(last_kernel, out_shape=[jax.ShapeDtypeStruct((53, 64, 128)...  4.23 us

profile of v4, /device:TPU:0, one launch (start us, length us, event | category | flops | bytes accessed | tf_op | source)
XLA Modules:
  0.0 87.2 jit_solution(1441779567292313985)
XLA Ops:
  0.6 47.1 %shard_map.140 = (f32[64,56,128]{2,1,0:T(8,128)}, s32[256]{0:T(256)}, bf16[656,224]{1,0:T(8,128)(2,1)}, bf16[224,656]{1,0:T(8,128)(2,1)}, f32[56,128]{1,0:T(8,128)}) custom-call(s32[1,64]{1,0:T(1,128)} %blocks_ref.5, s32[1,128]{1,0:T(1,128)} %refs_0_.1, f32[3392,128]{1,0:T(8,128)} %bitcast.5, f32[64,128]{1,0:T(8,128)} %bitcast.8, f32[64,128]{1,0:T(8,128)} %bitcast.6, ...), custom_call_target="tpu_custom_call" | custom-call | tf_op jit(solution)/shard_map/pallas_call | solution.py:608
  47.7 0.7 shard_map.141.state_any
  48.4 34.5 %shard_map.142.state_any = f32[64,56,128]{2,1,0:T(8,128)} custom-call(s32[256]{0:T(256)} %get-tuple-element.9.lists_ref, f32[64,56,128]{2,1,0:T(8,128)} %shard_map.141.state_any, f32[64,128]{1,0:T(8,128)} %bitcast.7, f32[56,128]{1,0:T(8,128)} %get-tuple-element.13.refs_1_, bf16[656,224]{1,0:T(8,128)(2,1)} %get-tuple-element.11.rates_any.refs_2_, ...), custom_call_target="tpu_custom_call" | custom-call | tf_op jit(solution)/shard_map/pallas_call | solution.py:608
  83.0 4.2 %shard_map.143 = (f32[53,64,128]{2,1,0:T(8,128)}, f32[64,128]{1,0:T(8,128)}) custom-call(s32[256]{0:T(256)} %get-tuple-element.9.lists_ref, s32[1,64]{1,0:T(1,128)} %blocks_ref.5, f32[64,56,128]{2,1,0:T(8,128)} %shard_map.142.state_any, bf16[656,224]{1,0:T(8,128)(2,1)} %get-tuple-element.11.rates_any.refs_2_, bf16[224,656]{1,0:T(8,128)(2,1)} %get-tuple-element.12.sums_any.refs_3_), custom_call_target="tpu_custom_call" | custom-call | tf_op jit(solution)/shard_map/pallas_call | solution.py:326

commit v5 on v4

--- a/solution.py
+++ b/solution.py
@@ -23,14 +23,14 @@
 LATE = 8
 SPAN = WORK - EARLY - LATE
 FLOOR = 24
-SWEEPS = 3
+SWEEPS = 2
 PAIR = 16
 SIDE = 6
 SIZES = (PAIR,) + (SIDE,) * 6
 BASES = tuple(sum(SIZES[:k]) for k in range(7))
 SLOTS = sum(SIZES)
 OPPOSITE = (0, 2, 1, 4, 3, 6, 5)
-SEND_AT, WORK_AT, REPLY_AT, FINAL_AT, REST_AT = 0, 64, 96, 160, 224
+SEND, WORK_ROW, REPLY, FINAL, REST = range(5)
 
 
 def prepare(consumed, made, exponent, thermal, barrier, balance, enthalpy, rates, sums, table):
@@ -137,74 +137,60 @@
     return own, given, taken
 
 
-def plan(me, counts, blocks_ref, lists, codes, codes_smem, sem):
+def positions(blocks_ref):
+    lane = lax.broadcasted_iota(jnp.int32, (8, 128), 1)
+    found = jnp.zeros((8, 128), jnp.int32)
+    for n in range(64):
+        found = jnp.where(lane == blocks_ref[0, n], n, found)
+    return found
+
+
+def plan(me, counts, position, blocks_ref, codes, lists, sem):
     own, given, taken = flows(counts)
-    place = lax.broadcasted_iota(jnp.int32, (8, 128), 0) * 128
+    row = lax.broadcasted_iota(jnp.int32, (8, 128), 0)
     lane = lax.broadcasted_iota(jnp.int32, (8, 128), 1)
-    mine = place + lane == me
-
-    def pick(value):
-        return jnp.sum(jnp.where(mine, value, 0))
-
-    own, total = pick(own), pick(counts)
-    given, taken = [pick(v) for v in given], [pick(v) for v in taken]
+
+    def mine(value):
+        return jnp.sum(jnp.where(lane == me, value, 0), 1, keepdims=True)
+
+    own, total = mine(own), mine(counts)
+    given, taken = [mine(v) for v in given], [mine(v) for v in taken]
     received = sum(taken)
     kept = jnp.minimum(own, WORK - received)
-    sent_before, taken_before = [kept], [jnp.int32(0)]
+    sent_before, taken_before = [kept], [jnp.zeros_like(kept)]
     for p in range(len(SIZES)):
         sent_before.append(sent_before[p] + given[p])
         taken_before.append(taken_before[p] + taken[p])
 
-    position = jnp.zeros((8, 128), jnp.int32)
-    for n in range(64):
-        position = jnp.where(lane == blocks_ref[0, n], n, position)
     late = WORK - LATE - EARLY + position
     middle = received + position - LATE
     slot = jnp.where(position < EARLY, position, jnp.where(position < EARLY + LATE, late, middle))
-    code = jnp.where(position < kept, 128 + slot, lane)
-    for p, base in enumerate(BASES):
+    final = jnp.where(position < kept, 128 + slot, lane)
+    send, reply = jnp.zeros((8, 128), jnp.int32), jnp.zeros((8, 128), jnp.int32)
+    step = lane - EARLY
+    arrived = jnp.zeros((8, 128), jnp.int32)
+    for p, (base, size) in enumerate(zip(BASES, SIZES)):
         inside = (position >= sent_before[p]) & (position < sent_before[p + 1])
-        code = jnp.where(inside, 64 + base + position - sent_before[p], code)
-    codes[...] = code
-    copy = pltpu.make_async_copy(codes, codes_smem, sem)
+        final = jnp.where(inside, 64 + base + position - sent_before[p], final)
+        here = (lane >= base) & (lane < base + size)
+        send = jnp.where(here, sent_before[p] + lane - base, send)
+        reply = jnp.where(here, EARLY + taken_before[p] + lane - base, reply)
+        inside = (step >= taken_before[p]) & (step < taken_before[p + 1])
+        arrived = jnp.where(inside, 64 + base + step - taken_before[p], arrived)
+    place = jnp.where(lane < EARLY, lane, EARLY + LATE + step - received)
+    place = jnp.where(lane >= WORK - LATE, lane - (WORK - LATE - EARLY), place)
+    wanted = jnp.clip(jnp.where(row == SEND, send, place), 0, 63)
+    value = jnp.zeros((8, 128), jnp.int32)
+    for n in range(64):
+        value = jnp.where(wanted == n, blocks_ref[0, n], value)
+    value = jnp.where((row == WORK_ROW) & (arrived > 0), arrived, value)
+    value = jnp.where(row == REPLY, jnp.clip(reply, 0, WORK - 1), value)
+    value = jnp.where(row == FINAL, final, value)
+    value = jnp.where(row == REST, jnp.where(lane == 0, sent_before[-1], total), value)
+    codes[...] = value
+    copy = pltpu.make_async_copy(codes, lists, sem)
     copy.start()
-
-    for p, (base, size) in enumerate(zip(BASES, SIZES)):
-
-        def per_slot(k, carry):
-            at = jnp.clip(sent_before[p] + k, 0, 63)
-            lists[SEND_AT + base + k] = blocks_ref[0, at]
-            lists[REPLY_AT + base + k] = jnp.clip(EARLY + taken_before[p] + k, 0, WORK - 1)
-            return carry
-
-        lax.fori_loop(0, size, per_slot, 0)
-
-    def per_early(w, carry):
-        lists[WORK_AT + w] = blocks_ref[0, w]
-        lists[WORK_AT + WORK - LATE + w] = blocks_ref[0, EARLY + w]
-        return carry
-
-    lax.fori_loop(0, EARLY, per_early, 0)
-
-    def per_middle(j, carry):
-        at = jnp.clip(EARLY + LATE + j - received, 0, 63)
-        value = blocks_ref[0, at]
-        for p, base in enumerate(BASES):
-            inside = (j >= taken_before[p]) & (j < taken_before[p + 1])
-            value = jnp.where(inside, 64 + base + j - taken_before[p], value)
-        lists[WORK_AT + EARLY + j] = value
-        return carry
-
-    lax.fori_loop(0, SPAN, per_middle, 0)
-    lists[REST_AT] = sent_before[-1]
-    lists[REST_AT + 1] = total
     copy.wait()
-
-    def per_block(b, carry):
-        lists[FINAL_AT + b] = codes_smem[0, b]
-        return carry
-
-    lax.fori_loop(0, 64, per_block, 0)
 
 
 def fetch(pairs, sem):
@@ -219,7 +205,7 @@
 
 
 def rest_kernel(lists_ref, blocks_ref, state_ref, rates_any, sums_any, out_ref, rates, sums, held, sem):
-    start, count = lists_ref[REST_AT], lists_ref[REST_AT + 1]
+    start, count = lists_ref[REST, 0], lists_ref[REST, 1]
 
     def bring(source, target):
         copy = pltpu.make_async_copy(source, target, sem)
@@ -270,22 +256,19 @@
 def last_kernel(
     lists_ref, blocks_ref, state_any, rates_any, sums_any, species_any, heat_any, *scratch
 ):
-    state, work, species, heat, rates, sums, in_sem, out_sem, sem = scratch
-    start, count = lists_ref[REST_AT], lists_ref[REST_AT + 1]
+    state, species, heat, rates, sums, in_sem, out_sem, sem = scratch
+    start, count = lists_ref[REST, 0], lists_ref[REST, 1]
     rows = [pl.ds(8 * i, 8) for i in range(8)]
     waits = fetch([(state_any.at[row], state.at[row]) for row in rows], in_sem)
-
-    def put(source, b):
-        species[pl.ds(b, 53, stride=64), :] = source[b, pl.ds(0, 53), :]
-        heat[pl.ds(b, 1), :] = source[b, pl.ds(53, 1), :]
-
     copies = []
     for i, row in enumerate(rows):
         waits[i]()
-        for j in range(8):
-            put(state, 8 * i + j)
-        view = species.reshape(53, 64, 128).at[:, row]
-        copies.append(pltpu.make_async_copy(view, species_any.at[:, row], out_sem.at[i]))
+        turned = jnp.swapaxes(state[row], 0, 1)
+        species[:, row] = turned[:53]
+        heat[row] = turned[53]
+        copies.append(
+            pltpu.make_async_copy(species.at[:, row], species_any.at[:, row], out_sem.at[i])
+        )
         copies[-1].start()
     copies.append(pltpu.make_async_copy(heat, heat_any, out_sem.at[8]))
     copies[-1].start()
@@ -311,13 +294,16 @@
 
                 @pl.when(first + k < count)
                 def _():
-                    work[at[k]] = value[:, k * 128 : (k + 1) * 128]
-                    put(work, at[k])
+                    state[at[k]] = value[:, k * 128 : (k + 1) * 128]
 
             return carry
 
         lax.fori_loop(0, (count - start + GROUP - 1) // GROUP, group, 0)
-        bring(species.reshape(53, 64, 128), species_any)
+        for row in rows:
+            turned = jnp.swapaxes(state[row], 0, 1)
+            species[:, row] = turned[:53]
+            heat[row] = turned[53]
+        bring(species, species_any)
         bring(heat, heat_any)
 
 
@@ -330,8 +316,7 @@
         out_specs=[anywhere] * 2,
         scratch_shapes=[
             pltpu.VMEM(state.shape, F32),
-            pltpu.VMEM(state.shape, F32),
-            pltpu.VMEM((53 * 64, 128), F32),
+            pltpu.VMEM((53, 64, 128), F32),
             pltpu.VMEM((64, 128), F32),
             pltpu.VMEM(rates.shape, BF16),
             pltpu.VMEM(sums.shape, BF16),
@@ -385,31 +370,28 @@
         (grid.at[8, inner], grid.at[0, inner]),
         (grid.at[inner, 1], grid.at[inner, 9]),
         (grid.at[inner, 8], grid.at[inner, 0]),
-        (edge.at[0], halo.at[1]),
-        (edge.at[1], halo.at[0]),
+        (edge, halo.at[1]),
+        (edge, halo.at[0]),
     ]
     copies = [remote(*plans[k], sems, k, peers[k]) for k in range(6)]
     met()
     for k in (2, 3, 0, 1):
         copies[k].start()
 
-    def ends(i, carry):
-        low, high = carry
+    def ends(i, packed):
         for j in range(8):
             b = i * 8 + j
-            here = grid[i + 1, j + 1]
-            low = jnp.where(lane == b, pltpu.roll(here, b, 1), low)
-            high = jnp.where(lane == b, pltpu.roll(here, b + 1, 1), high)
-        return low, high
-
-    low, high = lax.fori_loop(0, 8, ends, (jnp.zeros((ROWS, 128), F32),) * 2)
-    edge[0] = low
-    edge[1] = high
+            turned = pltpu.roll(grid[i + 1, j + 1], 2 * b + 1, 1)
+            packed = jnp.where((lane >> 1) == b, turned, packed)
+        return packed
+
+    edge[...] = lax.fori_loop(0, 8, ends, jnp.zeros((ROWS, 128), F32))
     copies[4].start()
     copies[5].start()
     hooks[0]()
     copies[4].wait()
     copies[5].wait()
+    edge[...] = jnp.where((lane & 1) == 0, halo[0], halo[1])
     rate = spread_ref[...]
     keep = 1.0 - 6.0 * rate
 
@@ -418,10 +400,9 @@
             b = i * 8 + j
             here = grid[i + 1, j + 1]
             behind = grid[i, j + 1]
-            low = pltpu.roll(halo[0], lax.rem(128 - b, 128), 1)
-            high = pltpu.roll(halo[1], 127 - b, 1)
-            left = jnp.where(lane == 0, low, pltpu.roll(here, 1, 1))
-            right = jnp.where(lane == 127, high, pltpu.roll(here, 127, 1))
+            ends = pltpu.roll(edge[...], 127 - 2 * b, 1)
+            left = pltpu.roll(jnp.where(lane == 127, ends, here), 1, 1)
+            right = pltpu.roll(jnp.where(lane == 0, ends, here), 127, 1)
             around = (behind + grid[i + 2, j + 1]) + (grid[i + 1, j] + grid[i + 1, j + 2])
             around = around + (left + right)
             speed = courant_ref[pl.ds(b, 1), :]
@@ -464,15 +445,21 @@
 
     lax.fori_loop(0, 8, sides, 0)
     lax.fori_loop(0, 2, first_last, 0)
-    hooks[2]()
 
 
 def chemistry(lists_ref, state, rates_ref, sums_ref, out, send, recv, reply, back, result, sems, met):
-    def pack(s, carry):
-        send[s] = state[lists_ref[SEND_AT + s]]
-        return carry
-
-    lax.fori_loop(0, SLOTS, pack, 0)
+    def each(count, body):
+        def four(g, carry):
+            for k in range(4):
+                body(4 * g + k)
+            return carry
+
+        lax.fori_loop(0, count // 4, four, 0)
+
+    def pack(s):
+        send[s] = state[lists_ref[SEND, s]]
+
+    each(SLOTS, pack)
     met()
     peers = partners()
 
@@ -491,10 +478,10 @@
             result[first + k] = whole[:, k * 128 : (k + 1) * 128]
 
     def own(first):
-        run(first, [state[lists_ref[WORK_AT + first + k]] for k in range(GROUP)])
+        run(first, [state[lists_ref[WORK_ROW, first + k]] for k in range(GROUP)])
 
     def any_item(slot):
-        code = lists_ref[WORK_AT + slot]
+        code = lists_ref[WORK_ROW, slot]
         there = recv[jnp.maximum(code - 64, 0)]
         return jnp.where(code < 64, state[jnp.minimum(code, 63)], there)
 
@@ -509,31 +496,29 @@
         copy.wait()
     lax.fori_loop(0, SPAN // GROUP, middle, 0)
 
-    def answer(s, carry):
-        reply[s] = result[lists_ref[REPLY_AT + s]]
-        return carry
-
-    lax.fori_loop(0, SLOTS, answer, 0)
+    def answer(s):
+        reply[s] = result[lists_ref[REPLY, s]]
+
+    each(SLOTS, answer)
     copies = exchange(reply, back, 7, True)
     own(WORK - LATE)
     for copy in copies:
         copy.wait()
 
-    def settle(b, carry):
-        code = lists_ref[FINAL_AT + b]
+    def settle(b):
+        code = lists_ref[FINAL, b]
         here = state[jnp.minimum(code, 63)]
         there = back[jnp.clip(code - 64, 0, SLOTS - 1)]
         done = result[jnp.clip(code - 128, 0, WORK - 1)]
         out[b] = jnp.where(code < 64, here, jnp.where(code < 128, there, done))
-        return carry
-
-    lax.fori_loop(0, 64, settle, 0)
+
+    each(64, settle)
 
 
 STATE = (64, ROWS, 128)
 MOVE_SCRATCH = [
     pltpu.VMEM((10, 10, ROWS, 128), F32),
-    pltpu.VMEM((2, ROWS, 128), F32),
+    pltpu.VMEM((ROWS, 128), F32),
     pltpu.VMEM((2, ROWS, 128), F32),
     pltpu.SemaphoreType.DMA((6,)),
     pltpu.SemaphoreType.DMA((6,)),
@@ -552,7 +537,6 @@
     pltpu.SemaphoreType.DMA((13,)),
     pltpu.SemaphoreType.DMA((13,)),
     pltpu.VMEM((8, 128), jnp.int32),
-    pltpu.SMEM((8, 128), jnp.int32),
     pltpu.SemaphoreType.DMA(()),
     pltpu.VMEM((2 * ROWS, 768), F32),
 ]
@@ -619,7 +603,7 @@
 
 def first_step(blocks, tally, species, heat, courant, spread, settings):
     nrxn = settings[0].shape[1]
-    padded = -(-nrxn // 8) * 8
+    padded = -(-nrxn // 16) * 16
     brought = (tally, species, heat, courant, spread, *settings)
 
     def kernel(blocks_ref, *refs):
@@ -631,38 +615,31 @@
         grid, edge, halo, *sems = refs[: len(MOVE_SCRATCH)]
         refs = refs[len(MOVE_SCRATCH) :]
         first, second, third, *count_sems = refs[:5]
-        codes, codes_smem, code_sem, table = refs[5:9]
-        moved, *chem = refs[9:]
+        codes, code_sem, table = refs[5:8]
+        moved, *chem = refs[8:]
 
         met = greet(others("stream") + others("radial") + others("azim"))
-        waits = fetch(list(zip(anywhere, near)), fetch_sem)
+        rows = [pl.ds(8 * i, 8) for i in range(8)]
+        pairs = list(zip(anywhere, near))
+        pairs[1:2] = [(anywhere[1].at[:, row], species_ref.at[:, row]) for row in rows]
+        waits = fetch(pairs, fetch_sem)
         stream, radial, azim = (lax.axis_index(axis) for axis in AXES)
         me = (stream * 4 + radial) * 4 + azim
         waits[0]()
         own = jnp.sum(tally_ref[...], 1, keepdims=True)
         first[stream] = jnp.broadcast_to(own, (8, 128))
         stages = spread_counts(first, second, third, count_sems)
-        waits[1]()
-        waits[2]()
-
-        def load(i, carry):
-            for j in range(8):
-                b = i * 8 + j
-                cell = grid.at[i + 1, j + 1]
-                cell[pl.ds(0, 53), :] = species_ref[pl.ds(b, 53, stride=64), :]
-                cell[pl.ds(53, 1), :] = heat_ref[pl.ds(b, 1), :]
-                cell[pl.ds(54, 2), :] = jnp.zeros((2, 128), F32)
-            return carry
-
-        lax.fori_loop(0, 8, load, 0)
-        waiting = []
-
-        def ready():
-            met()
-            waiting.append(stages[0]())
+        met()
+        waiting = [stages[0]()]
+        waits[9]()
+        for i, row in enumerate(rows):
+            waits[1 + i]()
+            cells = [species_ref[:, row], heat_ref[row][None], jnp.zeros((2, 8, 128), F32)]
+            grid[i + 1, pl.ds(1, 8)] = jnp.swapaxes(jnp.concatenate(cells, 0), 0, 1)
+        found = []
 
         def at_once():
-            for wait in waits[3:]:
+            for wait in waits[10:]:
                 wait()
             table[pl.ds(0, 1), pl.ds(0, 128)] = jnp.zeros((1, 128), F32)
             table[pl.ds(0, 1), pl.ds(0, 54)] = spread_ref[...].reshape(1, 54)
@@ -671,18 +648,20 @@
             diagonal = jnp.where(row == lane, table[pl.ds(0, 1), pl.ds(0, 128)], 0.0)
             column = jnp.sum(diagonal, 1, keepdims=True)
             spread_out[...] = jnp.broadcast_to(column, (ROWS, 128))
+            found.append(positions(blocks_ref))
             waiting[0]()
             waiting.append(stages[1]())
             prepare(*settings_refs, rates, sums, table)
             waiting[1]()
             waiting.append(stages[2]())
 
-        def at_end():
+        def after_inner():
             waiting[2]()
-            plan(me, stages[3](), blocks_ref, lists, codes, codes_smem, code_sem)
-
-        hooks = (at_once, lambda: None, at_end)
-        transport(ready, courant_ref, spread_out, moved, grid, edge, halo, sems, hooks)
+            plan(me, stages[3](), found[0], blocks_ref, codes, lists, code_sem)
+
+        nothing = lambda: None
+        hooks = (at_once, after_inner)
+        transport(nothing, courant_ref, spread_out, moved, grid, edge, halo, sems, hooks)
         chemistry(lists, moved, rates, sums, out, *chem[:5], chem[5:], lambda: None)
 
     smem, vmem = pl.BlockSpec(memory_space=pltpu.SMEM), pl.BlockSpec(memory_space=pltpu.VMEM)
@@ -691,7 +670,7 @@
         0,
         [
             jax.ShapeDtypeStruct(STATE, F32),
-            jax.ShapeDtypeStruct((256,), jnp.int32),
+            jax.ShapeDtypeStruct((8, 128), jnp.int32),
             jax.ShapeDtypeStruct((2 * padded, 4 * ROWS), BF16),
             jax.ShapeDtypeStruct((4 * ROWS, 2 * padded), BF16),
             jax.ShapeDtypeStruct((ROWS, 128), F32),
@@ -700,7 +679,7 @@
         [smem] + [pl.BlockSpec(memory_space=pl.ANY)] * len(brought),
         (blocks, *brought),
         [pltpu.VMEM(x.shape, x.dtype) for x in brought]
-        + [pltpu.SemaphoreType.DMA((len(brought),))]
+        + [pltpu.SemaphoreType.DMA((7 + len(brought),))]
         + MOVE_SCRATCH
         + COUNT_SCRATCH
         + [pltpu.VMEM(STATE, F32)]
@@ -726,7 +705,7 @@
         for wait in waits:
             wait()
         nothing = lambda: None
-        hooks = (nothing, nothing, nothing)
+        hooks = (nothing, nothing)
         transport(met, courant_ref, spread_ref, moved, grid, edge, halo, sems, hooks)
         chemistry(lists_ref, moved, rates_ref, sums_ref, out, *chem[:5], chem[5:], nothing)
 
@@ -771,7 +750,7 @@
         balance_constant_exponents,
         enthalpy_formation,
     )
-    species = component_fractions.reshape(53 * 64, 128)
+    species = component_fractions.reshape(53, 64, 128)
     heat = kilokelvin_field.reshape(64, 128)
     courant = axial_courant_number.reshape(64, 128)
     blocks, tally = processor_tiles_burning, tile_transfer_tally

time: 87.4 us -> 86.2 us (0.986)
  Pallas kernels: 86.5 us -> 85.2 us
    pallas_call x1, Pallas kernels: 4.23 us -> 3.18 us  [finish(): pl.pallas_call(last_kernel, out_shape=[jax.ShapeDtypeStruct((53, 64, 128)...]
where the time goes in v5:
time: 86.2 us; the launch traced here: 85.9 us
  Pallas kernels  85.2 us (99%)
    pallas_call x2, Pallas kernels, communicating(): pl.pallas_call(kernel, out_shape=out_shape, in_specs=specs, out_specs=out...  81.3 us
    pallas_call x1, Pallas kernels, finish(): pl.pallas_call(last_kernel, out_shape=[jax.ShapeDtypeStruct((53, 64, 128)...  3.18 us

profile of v5, /device:TPU:0, one launch (start us, length us, event | category | flops | bytes accessed | tf_op | source)
XLA Modules:
  0.0 85.9 jit_solution(15129054355691168675)
XLA Ops:
  0.6 46.8 %shard_map.140 = (f32[64,56,128]{2,1,0:T(8,128)}, s32[8,128]{1,0:T(8,128)}, bf16[672,224]{1,0:T(8,128)(2,1)}, bf16[224,672]{1,0:T(8,128)(2,1)}, f32[56,128]{1,0:T(8,128)}) custom-call(s32[1,64]{1,0:T(1,128)} %blocks_ref.5, s32[1,128]{1,0:T(1,128)} %refs_0_.1, f32[53,64,128]{2,1,0:T(8,128)} %bitcast.5, f32[64,128]{1,0:T(8,128)} %bitcast.8, ...), custom_call_target="tpu_custom_call" | custom-call | tf_op jit(solution)/shard_map/pallas_call | solution.py:592
  47.4 0.7 shard_map.141.state_any
  48.2 34.5 %shard_map.142.state_any = f32[64,56,128]{2,1,0:T(8,128)} custom-call(s32[8,128]{1,0:T(8,128)} %get-tuple-element.9.lists_ref, f32[64,56,128]{2,1,0:T(8,128)} %shard_map.141.state_any, f32[64,128]{1,0:T(8,128)} %bitcast.7, f32[56,128]{1,0:T(8,128)} %get-tuple-element.13.refs_1_, bf16[672,224]{1,0:T(8,128)(2,1)} %get-tuple-element.11.rates_any.refs_2_, ...), custom_call_target="tpu_custom_call" | custom-call | tf_op jit(solution)/shard_map/pallas_call | solution.py:592
  82.7 3.2 %shard_map.143 = (f32[53,64,128]{2,1,0:T(8,128)}, f32[64,128]{1,0:T(8,128)}) custom-call(s32[8,128]{1,0:T(8,128)} %get-tuple-element.9.lists_ref, s32[1,64]{1,0:T(1,128)} %blocks_ref.5, f32[64,56,128]{2,1,0:T(8,128)} %shard_map.142.state_any, bf16[672,224]{1,0:T(8,128)(2,1)} %get-tuple-element.11.rates_any.refs_2_, ...), custom_call_target="tpu_custom_call" | custom-call | tf_op jit(solution)/shard_map/pallas_call | solution.py:312

commit v6 on v5

--- a/solution.py
+++ b/solution.py
@@ -23,9 +23,9 @@
 LATE = 8
 SPAN = WORK - EARLY - LATE
 FLOOR = 24
-SWEEPS = 2
-PAIR = 16
-SIDE = 6
+SWEEPS = 3
+PAIR = 10
+SIDE = 5
 SIZES = (PAIR,) + (SIDE,) * 6
 BASES = tuple(sum(SIZES[:k]) for k in range(7))
 SLOTS = sum(SIZES)
@@ -120,20 +120,29 @@
 
 
 def flows(counts):
-    load, own = jnp.maximum(counts, EARLY + LATE), counts
+    least = EARLY + LATE
+    load, own = jnp.maximum(counts, least), counts
     given = [jnp.zeros_like(counts) for _ in SIZES]
     taken = [jnp.zeros_like(counts) for _ in SIZES]
     for sweep in range(SWEEPS):
-        for k, size in enumerate(SIZES):
-            other = toward(load, k)
-            gap = load - other + (1 if sweep == SWEEPS - 1 else 0)
-            spare = jnp.maximum(own - (EARLY + LATE), 0)
-            give = jnp.minimum(jnp.minimum(size - given[k], spare), jnp.maximum(gap, 0) >> 1)
-            give = jnp.minimum(give, jnp.maximum(load - FLOOR, 0))
-            give = jnp.minimum(give, jnp.maximum(WORK - other, 0))
-            take = toward(give, OPPOSITE[k])
-            given[k], taken[k] = given[k] + give, taken[k] + take
-            own, load = own - give, load - give + take
+        for axis in ((0,), (1, 2), (3, 4), (5, 6)):
+            spare = jnp.minimum(jnp.maximum(own - least, 0), jnp.maximum(load - FLOOR, 0))
+            gives = []
+            for k in axis:
+                other = toward(load, k)
+                gap = load - other + (1 if sweep == SWEEPS - 1 else 0)
+                room = jnp.maximum(WORK - other, 0)
+                if len(axis) == 2:
+                    room = (room + (1 if k == axis[0] else 0)) >> 1
+                give = jnp.minimum(SIZES[k] - given[k], jnp.maximum(gap, 0) >> 1)
+                give = jnp.minimum(jnp.minimum(give, room), spare)
+                spare = spare - give
+                gives.append(give)
+            takes = [toward(give, OPPOSITE[k]) for k, give in zip(axis, gives)]
+            for k, give, take in zip(axis, gives, takes):
+                given[k], taken[k] = given[k] + give, taken[k] + take
+            own = own - sum(gives)
+            load = load - sum(gives) + sum(takes)
     return own, given, taken
 
 
@@ -445,6 +454,7 @@
 
     lax.fori_loop(0, 8, sides, 0)
     lax.fori_loop(0, 2, first_last, 0)
+    hooks[2]()
 
 
 def chemistry(lists_ref, state, rates_ref, sums_ref, out, send, recv, reply, back, result, sems, met):
@@ -455,6 +465,8 @@
             return carry
 
         lax.fori_loop(0, count // 4, four, 0)
+        for k in range(count // 4 * 4, count):
+            body(k)
 
     def pack(s):
         send[s] = state[lists_ref[SEND, s]]
@@ -629,13 +641,15 @@
         own = jnp.sum(tally_ref[...], 1, keepdims=True)
         first[stream] = jnp.broadcast_to(own, (8, 128))
         stages = spread_counts(first, second, third, count_sems)
-        met()
-        waiting = [stages[0]()]
         waits[9]()
+        waiting = []
         for i, row in enumerate(rows):
             waits[1 + i]()
             cells = [species_ref[:, row], heat_ref[row][None], jnp.zeros((2, 8, 128), F32)]
             grid[i + 1, pl.ds(1, 8)] = jnp.swapaxes(jnp.concatenate(cells, 0), 0, 1)
+            if i == 3:
+                met()
+                waiting.append(stages[0]())
         found = []
 
         def at_once():
@@ -655,12 +669,12 @@
             waiting[1]()
             waiting.append(stages[2]())
 
-        def after_inner():
+        def at_end():
             waiting[2]()
             plan(me, stages[3](), found[0], blocks_ref, codes, lists, code_sem)
 
         nothing = lambda: None
-        hooks = (at_once, after_inner)
+        hooks = (at_once, nothing, at_end)
         transport(nothing, courant_ref, spread_out, moved, grid, edge, halo, sems, hooks)
         chemistry(lists, moved, rates, sums, out, *chem[:5], chem[5:], lambda: None)
 
@@ -705,7 +719,7 @@
         for wait in waits:
             wait()
         nothing = lambda: None
-        hooks = (nothing, nothing)
+        hooks = (nothing, nothing, nothing)
         transport(met, courant_ref, spread_ref, moved, grid, edge, halo, sems, hooks)
         chemistry(lists_ref, moved, rates_ref, sums_ref, out, *chem[:5], chem[5:], nothing)
 

time: 86.2 us -> 81.8 us (0.949)
  Pallas kernels: 85.2 us -> 80.9 us
    pallas_call x2, Pallas kernels: 81.3 us -> 76.9 us  [communicating(): pl.pallas_call(kernel, out_shape=out_shape, in_specs=specs, out_specs=out...]
where the time goes in v6:
time: 81.8 us; the launch traced here: 81.5 us
  Pallas kernels  80.9 us (99%)
    pallas_call x2, Pallas kernels, communicating(): pl.pallas_call(kernel, out_shape=out_shape, in_specs=specs, out_specs=out...  76.9 us
    pallas_call x1, Pallas kernels, finish(): pl.pallas_call(last_kernel, out_shape=[jax.ShapeDtypeStruct((53, 64, 128)...  3.18 us

profile of v6, /device:TPU:0, one launch (start us, length us, event | category | flops | bytes accessed | tf_op | source)
XLA Modules:
  0.0 81.5 jit_solution(13465675681484167824)
XLA Ops:
  0.6 43.6 %shard_map.140 = (f32[64,56,128]{2,1,0:T(8,128)}, s32[8,128]{1,0:T(8,128)}, bf16[672,224]{1,0:T(8,128)(2,1)}, bf16[224,672]{1,0:T(8,128)(2,1)}, f32[56,128]{1,0:T(8,128)}) custom-call(s32[1,64]{1,0:T(1,128)} %blocks_ref.5, s32[1,128]{1,0:T(1,128)} %refs_0_.1, f32[53,64,128]{2,1,0:T(8,128)} %bitcast.5, f32[64,128]{1,0:T(8,128)} %bitcast.8, ...), custom_call_target="tpu_custom_call" | custom-call | tf_op jit(solution)/shard_map/pallas_call | solution.py:604
  44.2 0.7 shard_map.141.state_any
  45.0 33.3 %shard_map.142.state_any = f32[64,56,128]{2,1,0:T(8,128)} custom-call(s32[8,128]{1,0:T(8,128)} %get-tuple-element.9.lists_ref, f32[64,56,128]{2,1,0:T(8,128)} %shard_map.141.state_any, f32[64,128]{1,0:T(8,128)} %bitcast.7, f32[56,128]{1,0:T(8,128)} %get-tuple-element.13.refs_1_, bf16[672,224]{1,0:T(8,128)(2,1)} %get-tuple-element.11.rates_any.refs_2_, ...), custom_call_target="tpu_custom_call" | custom-call | tf_op jit(solution)/shard_map/pallas_call | solution.py:604
  78.3 3.2 %shard_map.143 = (f32[53,64,128]{2,1,0:T(8,128)}, f32[64,128]{1,0:T(8,128)}) custom-call(s32[8,128]{1,0:T(8,128)} %get-tuple-element.9.lists_ref, s32[1,64]{1,0:T(1,128)} %blocks_ref.5, f32[64,56,128]{2,1,0:T(8,128)} %shard_map.142.state_any, bf16[672,224]{1,0:T(8,128)(2,1)} %get-tuple-element.11.rates_any.refs_2_, ...), custom_call_target="tpu_custom_call" | custom-call | tf_op jit(solution)/shard_map/pallas_call | solution.py:321

commit v7 on v6

--- a/solution.py
+++ b/solution.py
@@ -162,6 +162,8 @@
     def mine(value):
         return jnp.sum(jnp.where(lane == me, value, 0), 1, keepdims=True)
 
+    over = own - jnp.minimum(own, WORK - sum(taken))
+    over = jnp.max(over, 1, keepdims=True)
     own, total = mine(own), mine(counts)
     given, taken = [mine(v) for v in given], [mine(v) for v in taken]
     received = sum(taken)
@@ -195,7 +197,8 @@
     value = jnp.where((row == WORK_ROW) & (arrived > 0), arrived, value)
     value = jnp.where(row == REPLY, jnp.clip(reply, 0, WORK - 1), value)
     value = jnp.where(row == FINAL, final, value)
-    value = jnp.where(row == REST, jnp.where(lane == 0, sent_before[-1], total), value)
+    rest = jnp.where(lane == 0, sent_before[-1], jnp.where(lane == 1, total, over))
+    value = jnp.where(row == REST, rest, value)
     codes[...] = value
     copy = pltpu.make_async_copy(codes, lists, sem)
     copy.start()
@@ -457,7 +460,7 @@
     hooks[2]()
 
 
-def chemistry(lists_ref, state, rates_ref, sums_ref, out, send, recv, reply, back, result, sems, met):
+def chemistry(lists_ref, state, rates_ref, sums_ref, put, send, recv, reply, back, result, sems, met):
     def each(count, body):
         def four(g, carry):
             for k in range(4):
@@ -517,14 +520,23 @@
     for copy in copies:
         copy.wait()
 
-    def settle(b):
-        code = lists_ref[FINAL, b]
-        here = state[jnp.minimum(code, 63)]
-        there = back[jnp.clip(code - 64, 0, SLOTS - 1)]
-        done = result[jnp.clip(code - 128, 0, WORK - 1)]
-        out[b] = jnp.where(code < 64, here, jnp.where(code < 128, there, done))
-
-    each(64, settle)
+    def settle(i, carry):
+        for j in range(8):
+            code = lists_ref[FINAL, i * 8 + j]
+            here = state[jnp.minimum(code, 63)]
+            there = back[jnp.clip(code - 64, 0, SLOTS - 1)]
+            done = result[jnp.clip(code - 128, 0, WORK - 1)]
+            put(i, j, jnp.where(code < 64, here, jnp.where(code < 128, there, done)))
+        return carry
+
+    lax.fori_loop(0, 8, settle, 0)
+
+
+def into(out):
+    def put(i, j, value):
+        out[i * 8 + j] = value
+
+    return put
 
 
 STATE = (64, ROWS, 128)
@@ -542,6 +554,10 @@
 ]
 
 
+AGAIN_SCRATCH = [pltpu.VMEM((SLOTS, ROWS, 128), F32)] * 2 + [
+    pltpu.SemaphoreType.DMA((14,)),
+    pltpu.SemaphoreType.DMA((14,)),
+]
 COUNT_SCRATCH = [
     pltpu.VMEM((8, 8, 128), jnp.int32),
     pltpu.VMEM((4, 8, 128), jnp.int32),
@@ -613,7 +629,7 @@
     )(*args)
 
 
-def first_step(blocks, tally, species, heat, courant, spread, settings):
+def first_steps(both, blocks, tally, species, heat, courant, spread, settings):
     nrxn = settings[0].shape[1]
     padded = -(-nrxn // 16) * 16
     brought = (tally, species, heat, courant, spread, *settings)
@@ -628,7 +644,8 @@
         refs = refs[len(MOVE_SCRATCH) :]
         first, second, third, *count_sems = refs[:5]
         codes, code_sem, table = refs[5:8]
-        moved, *chem = refs[8:]
+        moved, *refs = refs[8:]
+        chem, refs = refs[: len(CHEM_SCRATCH)], refs[len(CHEM_SCRATCH) :]
 
         met = greet(others("stream") + others("radial") + others("azim"))
         rows = [pl.ds(8 * i, 8) for i in range(8)]
@@ -676,12 +693,26 @@
         nothing = lambda: None
         hooks = (at_once, nothing, at_end)
         transport(nothing, courant_ref, spread_out, moved, grid, edge, halo, sems, hooks)
-        chemistry(lists, moved, rates, sums, out, *chem[:5], chem[5:], lambda: None)
+        if not both:
+            chemistry(lists, moved, rates, sums, into(out), *chem[:5], chem[5:], nothing)
+            return
+        grid, edge, halo, *sems = refs[: len(MOVE_SCRATCH)]
+        recv, back, *again_sems = refs[len(MOVE_SCRATCH) :]
+
+        def put(i, j, value):
+            grid[i + 1, j + 1] = value
+
+        chemistry(lists, moved, rates, sums, put, *chem[:5], chem[5:], nothing)
+        hooks = (nothing, nothing, nothing)
+        transport(nothing, courant_ref, spread_out, moved, grid, edge, halo, sems, hooks)
+        send, _, reply, _, result = chem[:5]
+        again = (send, recv, reply, back, result, again_sems)
+        chemistry(lists, moved, rates, sums, into(out), *again, nothing)
 
     smem, vmem = pl.BlockSpec(memory_space=pltpu.SMEM), pl.BlockSpec(memory_space=pltpu.VMEM)
     return communicating(
         kernel,
-        0,
+        0 if both else 1,
         [
             jax.ShapeDtypeStruct(STATE, F32),
             jax.ShapeDtypeStruct((8, 128), jnp.int32),
@@ -697,7 +728,8 @@
         + MOVE_SCRATCH
         + COUNT_SCRATCH
         + [pltpu.VMEM(STATE, F32)]
-        + CHEM_SCRATCH,
+        + CHEM_SCRATCH
+        + (MOVE_SCRATCH + AGAIN_SCRATCH if both else []),
     )
 
 
@@ -721,12 +753,12 @@
         nothing = lambda: None
         hooks = (nothing, nothing, nothing)
         transport(met, courant_ref, spread_ref, moved, grid, edge, halo, sems, hooks)
-        chemistry(lists_ref, moved, rates_ref, sums_ref, out, *chem[:5], chem[5:], nothing)
+        chemistry(lists_ref, moved, rates_ref, sums_ref, into(out), *chem[:5], chem[5:], nothing)
 
     smem, vmem = pl.BlockSpec(memory_space=pltpu.SMEM), pl.BlockSpec(memory_space=pltpu.VMEM)
     return communicating(
         kernel,
-        1,
+        2,
         jax.ShapeDtypeStruct(STATE, F32),
         vmem,
         [smem] + [pl.BlockSpec(memory_space=pl.ANY)] * 5,
@@ -768,12 +800,20 @@
     heat = kilokelvin_field.reshape(64, 128)
     courant = axial_courant_number.reshape(64, 128)
     blocks, tally = processor_tiles_burning, tile_transfer_tally
-    state, lists, rates, sums, spread = first_step(
-        blocks, tally, species, heat, courant, spreading_number, settings
-    )
-    state = react_rest(lists, blocks, state, rates, sums)
-    state = second_step(lists, state, courant, spread, rates, sums)
-    species, heat = finish(lists, blocks, state, rates, sums)
+    inputs = (blocks, tally, species, heat, courant, spreading_number, settings)
+    state, lists, rates, sums, _ = first_steps(True, *inputs)
+
+    def balanced(state, lists, rates, sums):
+        return finish(lists, blocks, state, rates, sums)
+
+    def with_rest(state, lists, rates, sums):
+        state, lists, rates, sums, spread = first_steps(False, *inputs)
+        state = react_rest(lists, blocks, state, rates, sums)
+        state = second_step(lists, state, courant, spread, rates, sums)
+        return finish(lists, blocks, state, rates, sums)
+
+    over = lists[REST, 2] > 0
+    species, heat = lax.cond(over, with_rest, balanced, state, lists, rates, sums)
     return species.reshape(shape), heat.reshape(shape[1:])
 
 

time: 81.8 us -> 78.1 us (0.955)
  Pallas kernels: 80.9 us -> 75.4 us
  between operations: 0.66 us -> 1.67 us
    pallas_call x2 -> x1, Pallas kernels: 76.9 us -> 72.3 us  [communicating(): pl.pallas_call(kernel, out_shape=out_shape, in_specs=specs, out_specs=out...]
where the time goes in v7:
time: 78.1 us; the launch traced here: 77.9 us
  Pallas kernels  75.4 us (97%)
  between operations  1.67 us (2%)
    pallas_call x1, Pallas kernels, communicating(): pl.pallas_call(kernel, out_shape=out_shape, in_specs=specs, out_specs=out...  72.3 us
    pallas_call x1, Pallas kernels, finish(): pl.pallas_call(last_kernel, out_shape=[jax.ShapeDtypeStruct((53, 64, 128)...  3.05 us

profile of v7, /device:TPU:0, one launch (start us, length us, event | category | flops | bytes accessed | tf_op | source)
XLA Modules:
  0.0 77.9 jit_solution(12015321634208889644)
XLA Ops:
  0.6 0.0 copy-start.4
  0.6 0.0 copy-start.9
  0.7 0.0 copy-start.1
  0.7 0.0 copy-start
  0.7 0.0 copy-start.11
  0.7 0.0 copy-start.8
  0.7 0.0 copy-start.7
  0.7 0.0 copy-start.6
  0.7 0.0 copy-start.5
  0.7 0.0 copy-start.10
  0.7 0.0 copy-start.2
  0.7 0.0 copy-start.3
  0.8 72.3 %shard_map.140 = (f32[64,56,128]{2,1,0:T(8,128)}, s32[8,128]{1,0:T(8,128)S(1)}, bf16[672,224]{1,0:T(8,128)(2,1)S(1)}, bf16[224,672]{1,0:T(8,128)(2,1)S(1)}, f32[56,128]{1,0:T(8,128)}) custom-call(s32[1,64]{1,0:T(1,128)} %blocks_ref.1, s32[1,128]{1,0:T(1,128)} %refs_0_.1, f32[53,64,128]{2,1,0:T(8,128)} %bitcast.6, f32[64,128]{1,0:T(8,128)} %bitcast.10, ...), custom_call_target="tpu_custom_call" | custom-call | tf_op jit(solution)/shard_map/pallas_call | solution.py:620
  73.1 0.6 slice.3
  74.3 0.0 copy-done.4
  74.3 0.0 copy-done.9
  74.3 0.0 copy-done.1
  74.3 0.0 copy-done
  74.4 0.0 copy-done.11
  74.4 0.0 copy-done.8
  74.4 0.0 copy-done.7
  74.4 0.0 copy-done.6
  74.4 0.0 copy-done.5
  74.4 0.0 copy-done.10
  74.4 0.0 copy-done.2
  74.4 0.0 copy-done.3
  74.4 3.3 %conditional.1 = ((f32[53,64,128]{2,1,0:T(8,128)}, f32[64,128]{1,0:T(8,128)})) conditional(s32[]{:T(128)} %bitcast.3, (s32[8,128]{1,0:T(8,128)S(1)}, s32[1,64]{1,0:T(1,128)S(1)}, f32[64,56,128]{2,1,0:T(8,128)}, bf16[672,224]{1,0:T(8,128)(2,1)S(1)}, bf16[224,672]{1,0:T(8,128)(2,1)S(1)}) %tuple.37, (s32[1,64]{1,0:T(1,128)S(1)}, ...), branch_computations={%region_0.0_spmd.clone, %region_1.0_spmd.clone} | conditional | bytes 8 | solution.py:816
  74.4 3.0 %branch_0_fun.1 = (f32[53,64,128]{2,1,0:T(8,128)}, f32[64,128]{1,0:T(8,128)}) custom-call(s32[8,128]{1,0:T(8,128)S(1)} %get-tuple-element.83.lists_ref, s32[1,64]{1,0:T(1,128)S(1)} %get-tuple-element.84.blocks_ref, f32[64,56,128]{2,1,0:T(8,128)} %get-tuple-element.85.state_any, bf16[672,224]{1,0:T(8,128)(2,1)S(1)} %get-tuple-element.86.rates_any, ...), custom_call_target="tpu_custom_call" | custom-call | tf_op jit(solution)/shard_map/cond/branch_0_fun/pallas_call | solution.py:324
Async XLA Ops:
  0.6 73.7 %copy-start.4 = (s32[1,64]{1,0:T(1,128)S(1)}, s32[1,64]{1,0:T(1,128)}, u32[]{:S(2)}) copy-start(s32[1,64]{1,0:T(1,128)} %blocks_ref.1) | copy-start | bytes 772
  0.6 73.7 %copy-start.9 = (s32[1,128]{1,0:T(1,128)S(1)}, s32[1,128]{1,0:T(1,128)}, u32[]{:S(2)}) copy-start(s32[1,128]{1,0:T(1,128)} %refs_0_.1) | copy-start | bytes 1540
  0.7 73.7 %copy-start.1 = (f32[53,325]{1,0:T(8,128)S(1)}, f32[53,325]{1,0:T(8,128)}, u32[]{:S(2)}) copy-start(f32[53,325]{1,0:T(8,128)} %refs_6_.1) | copy-start | bytes 206704
  0.7 73.7 %copy-start = (f32[53,325]{1,0:T(8,128)S(1)}, f32[53,325]{1,0:T(8,128)}, u32[]{:S(2)}) copy-start(f32[53,325]{1,0:T(8,128)} %refs_5_.1) | copy-start | bytes 206704
  0.7 73.7 %copy-start.11 = (f32[53]{0:T(128)S(1)}, f32[53]{0:T(128)}, u32[]{:S(2)}) copy-start(f32[53]{0:T(128)} %refs_11_.1) | copy-start | bytes 640
  0.7 73.7 %copy-start.8 = (f32[325]{0:T(512)S(1)}, f32[325]{0:T(512)}, u32[]{:S(2)}) copy-start(f32[325]{0:T(512)} %refs_10_.1) | copy-start | bytes 3904
  0.7 73.7 %copy-start.7 = (f32[325]{0:T(512)S(1)}, f32[325]{0:T(512)}, u32[]{:S(2)}) copy-start(f32[325]{0:T(512)} %refs_9_.1) | copy-start | bytes 3904
  0.7 73.7 %copy-start.6 = (f32[325]{0:T(512)S(1)}, f32[325]{0:T(512)}, u32[]{:S(2)}) copy-start(f32[325]{0:T(512)} %refs_8_.1) | copy-start | bytes 3904
  0.7 73.7 %copy-start.5 = (f32[325]{0:T(512)S(1)}, f32[325]{0:T(512)}, u32[]{:S(2)}) copy-start(f32[325]{0:T(512)} %refs_7_.1) | copy-start | bytes 3904
  0.7 73.7 %copy-start.10 = (f32[54]{0:T(128)S(1)}, f32[54]{0:T(128)}, u32[]{:S(2)}) copy-start(f32[54]{0:T(128)} %refs_4_.1) | copy-start | bytes 652
  0.7 73.7 %copy-start.2 = (f32[8,8,128]{2,1,0:T(8,128)S(1)}, f32[8,8,128]{2,1,0:T(8,128)}, u32[]{:S(2)}) copy-start(f32[8,8,128]{2,1,0:T(8,128)} %param.17) | copy-start | bytes 98308
  0.7 73.7 %copy-start.3 = (f32[8,8,128]{2,1,0:T(8,128)S(1)}, f32[8,8,128]{2,1,0:T(8,128)}, u32[]{:S(2)}) copy-start(f32[8,8,128]{2,1,0:T(8,128)} %param.16) | copy-start | bytes 98308

commit v8 on v7

--- a/solution.py
+++ b/solution.py
@@ -560,10 +560,9 @@
 ]
 COUNT_SCRATCH = [
     pltpu.VMEM((8, 8, 128), jnp.int32),
-    pltpu.VMEM((4, 8, 128), jnp.int32),
-    pltpu.VMEM((4, 4, 8, 128), jnp.int32),
-    pltpu.SemaphoreType.DMA((13,)),
-    pltpu.SemaphoreType.DMA((13,)),
+    pltpu.VMEM((16, 8, 128), jnp.int32),
+    pltpu.SemaphoreType.DMA((22,)),
+    pltpu.SemaphoreType.DMA((22,)),
     pltpu.VMEM((8, 128), jnp.int32),
     pltpu.SemaphoreType.DMA(()),
     pltpu.VMEM((2 * ROWS, 768), F32),
@@ -571,14 +570,21 @@
 
 
 def others(axis):
-    return [shifted(axis, step) for step in range(1, lax.axis_size(axis))]
-
-
-def spread_counts(first, second, third, sems):
+    n = lax.axis_size(axis)
+    return [shifted(axis, step) for step in sorted(range(1, n), key=lambda step: -min(step, n - step))]
+
+
+def plane():
+    far = (0, 1, 2, 1)
+    steps = sorted(range(1, 16), key=lambda step: -far[step // 4] - far[step % 4])
+    return [{**shifted("radial", step // 4), **shifted("azim", step % 4)} for step in steps]
+
+
+def spread_counts(first, second, sems):
     stream, radial, azim = (lax.axis_index(axis) for axis in AXES)
 
-    def stage(source, target, axis, start):
-        copies = [remote(source, target, sems, start + k, p) for k, p in enumerate(others(axis))]
+    def stage(buffer, peers, start):
+        copies = [remote(buffer, buffer, sems, start + k, p) for k, p in enumerate(peers)]
         for copy in copies:
             copy.start()
 
@@ -589,31 +595,26 @@
         return wait
 
     def along_stream():
-        return stage(first.at[stream], first.at[stream], "stream", 0)
-
-    def along_radial():
+        return stage(first.at[stream], others("stream"), 0)
+
+    def in_plane():
         row = lax.broadcasted_iota(jnp.int32, (8, 128), 0)
         joined = first[0]
         for s in range(1, 8):
             joined = jnp.where(row == s, first[s], joined)
-        second[radial] = joined
-        return stage(second.at[radial], second.at[radial], "radial", 7)
-
-    def along_azim():
-        third[azim] = second[...]
-        return stage(third.at[azim], third.at[azim], "azim", 10)
+        second[radial * 4 + azim] = joined
+        return stage(second.at[radial * 4 + azim], plane(), 7)
 
     def whole():
         row = lax.broadcasted_iota(jnp.int32, (8, 128), 0)
         lane = lax.broadcasted_iota(jnp.int32, (8, 128), 1)
         total = jnp.zeros((8, 128), jnp.int32)
-        for a in range(4):
-            for r in range(4):
-                here = (lane & 15 == r * 4 + a) & (lane >> 4 == row)
-                total = jnp.where(here, third[a, r], total)
+        for place in range(16):
+            here = (lane & 15 == place) & (lane >> 4 == row)
+            total = jnp.where(here, second[place], total)
         return jnp.broadcast_to(jnp.sum(total, 0, keepdims=True), (8, 128))
 
-    return along_stream, along_radial, along_azim, whole
+    return along_stream, in_plane, whole
 
 
 def communicating(kernel, name, out_shape, out_specs, specs, args, scratch):
@@ -642,31 +643,29 @@
         tally_ref, species_ref, heat_ref, courant_ref, spread_ref, *settings_refs = near
         grid, edge, halo, *sems = refs[: len(MOVE_SCRATCH)]
         refs = refs[len(MOVE_SCRATCH) :]
-        first, second, third, *count_sems = refs[:5]
-        codes, code_sem, table = refs[5:8]
-        moved, *refs = refs[8:]
+        first, second, *count_sems = refs[:4]
+        codes, code_sem, table = refs[4:7]
+        moved, *refs = refs[7:]
         chem, refs = refs[: len(CHEM_SCRATCH)], refs[len(CHEM_SCRATCH) :]
 
-        met = greet(others("stream") + others("radial") + others("azim"))
         rows = [pl.ds(8 * i, 8) for i in range(8)]
         pairs = list(zip(anywhere, near))
         pairs[1:2] = [(anywhere[1].at[:, row], species_ref.at[:, row]) for row in rows]
         waits = fetch(pairs, fetch_sem)
+        met = greet(others("stream") + plane())
         stream, radial, azim = (lax.axis_index(axis) for axis in AXES)
         me = (stream * 4 + radial) * 4 + azim
         waits[0]()
         own = jnp.sum(tally_ref[...], 1, keepdims=True)
         first[stream] = jnp.broadcast_to(own, (8, 128))
-        stages = spread_counts(first, second, third, count_sems)
+        stages = spread_counts(first, second, count_sems)
+        met()
+        waiting = [stages[0]()]
         waits[9]()
-        waiting = []
         for i, row in enumerate(rows):
             waits[1 + i]()
             cells = [species_ref[:, row], heat_ref[row][None], jnp.zeros((2, 8, 128), F32)]
             grid[i + 1, pl.ds(1, 8)] = jnp.swapaxes(jnp.concatenate(cells, 0), 0, 1)
-            if i == 3:
-                met()
-                waiting.append(stages[0]())
         found = []
 
         def at_once():
@@ -683,12 +682,10 @@
             waiting[0]()
             waiting.append(stages[1]())
             prepare(*settings_refs, rates, sums, table)
+
+        def at_end():
             waiting[1]()
-            waiting.append(stages[2]())
-
-        def at_end():
-            waiting[2]()
-            plan(me, stages[3](), found[0], blocks_ref, codes, lists, code_sem)
+            plan(me, stages[2](), found[0], blocks_ref, codes, lists, code_sem)
 
         nothing = lambda: None
         hooks = (at_once, nothing, at_end)

time: 78.1 us -> 77.5 us (level)
  no operation moved by 1% of the time
where the time goes in v8:
time: 77.5 us; the launch traced here: 77.3 us
  Pallas kernels  74.8 us (97%)
  between operations  1.67 us (2%)
    pallas_call x1, Pallas kernels, communicating(): pl.pallas_call(kernel, out_shape=out_shape, in_specs=specs, out_specs=out...  71.7 us
    pallas_call x1, Pallas kernels, finish(): pl.pallas_call(last_kernel, out_shape=[jax.ShapeDtypeStruct((53, 64, 128)...  3.05 us

profile of v8, /device:TPU:0, one launch (start us, length us, event | category | flops | bytes accessed | tf_op | source)
XLA Modules:
  0.0 77.3 jit_solution(4267926835527897165)
XLA Ops:
  0.6 0.0 copy-start.4
  0.6 0.0 copy-start.9
  0.7 0.0 copy-start.1
  0.7 0.0 copy-start
  0.7 0.0 copy-start.11
  0.7 0.0 copy-start.8
  0.7 0.0 copy-start.7
  0.7 0.0 copy-start.6
  0.7 0.0 copy-start.5
  0.7 0.0 copy-start.10
  0.7 0.0 copy-start.2
  0.7 0.0 copy-start.3
  0.8 71.7 %shard_map.140 = (f32[64,56,128]{2,1,0:T(8,128)}, s32[8,128]{1,0:T(8,128)S(1)}, bf16[672,224]{1,0:T(8,128)(2,1)S(1)}, bf16[224,672]{1,0:T(8,128)(2,1)S(1)}, f32[56,128]{1,0:T(8,128)}) custom-call(s32[1,64]{1,0:T(1,128)} %blocks_ref.1, s32[1,128]{1,0:T(1,128)} %refs_0_.1, f32[53,64,128]{2,1,0:T(8,128)} %bitcast.6, f32[64,128]{1,0:T(8,128)} %bitcast.10, ...), custom_call_target="tpu_custom_call" | custom-call | tf_op jit(solution)/shard_map/pallas_call | solution.py:621
  72.5 0.6 slice.3
  73.7 0.0 copy-done.4
  73.7 0.0 copy-done.9
  73.7 0.0 copy-done.1
  73.7 0.0 copy-done
  73.8 0.0 copy-done.11
  73.8 0.0 copy-done.8
  73.8 0.0 copy-done.7
  73.8 0.0 copy-done.6
  73.8 0.0 copy-done.5
  73.8 0.0 copy-done.10
  73.8 0.0 copy-done.2
  73.8 0.0 copy-done.3
  73.8 3.3 %conditional.1 = ((f32[53,64,128]{2,1,0:T(8,128)}, f32[64,128]{1,0:T(8,128)})) conditional(s32[]{:T(128)} %bitcast.3, (s32[8,128]{1,0:T(8,128)S(1)}, s32[1,64]{1,0:T(1,128)S(1)}, f32[64,56,128]{2,1,0:T(8,128)}, bf16[672,224]{1,0:T(8,128)(2,1)S(1)}, bf16[224,672]{1,0:T(8,128)(2,1)S(1)}) %tuple.37, (s32[1,64]{1,0:T(1,128)S(1)}, ...), branch_computations={%region_0.0_spmd.clone, %region_1.0_spmd.clone} | conditional | bytes 8 | solution.py:813
  73.8 3.0 %branch_0_fun.1 = (f32[53,64,128]{2,1,0:T(8,128)}, f32[64,128]{1,0:T(8,128)}) custom-call(s32[8,128]{1,0:T(8,128)S(1)} %get-tuple-element.83.lists_ref, s32[1,64]{1,0:T(1,128)S(1)} %get-tuple-element.84.blocks_ref, f32[64,56,128]{2,1,0:T(8,128)} %get-tuple-element.85.state_any, bf16[672,224]{1,0:T(8,128)(2,1)S(1)} %get-tuple-element.86.rates_any, ...), custom_call_target="tpu_custom_call" | custom-call | tf_op jit(solution)/shard_map/cond/branch_0_fun/pallas_call | solution.py:324
Async XLA Ops:
  0.6 73.1 %copy-start.4 = (s32[1,64]{1,0:T(1,128)S(1)}, s32[1,64]{1,0:T(1,128)}, u32[]{:S(2)}) copy-start(s32[1,64]{1,0:T(1,128)} %blocks_ref.1) | copy-start | bytes 772
  0.6 73.1 %copy-start.9 = (s32[1,128]{1,0:T(1,128)S(1)}, s32[1,128]{1,0:T(1,128)}, u32[]{:S(2)}) copy-start(s32[1,128]{1,0:T(1,128)} %refs_0_.1) | copy-start | bytes 1540
  0.7 73.1 %copy-start.1 = (f32[53,325]{1,0:T(8,128)S(1)}, f32[53,325]{1,0:T(8,128)}, u32[]{:S(2)}) copy-start(f32[53,325]{1,0:T(8,128)} %refs_6_.1) | copy-start | bytes 206704
  0.7 73.1 %copy-start = (f32[53,325]{1,0:T(8,128)S(1)}, f32[53,325]{1,0:T(8,128)}, u32[]{:S(2)}) copy-start(f32[53,325]{1,0:T(8,128)} %refs_5_.1) | copy-start | bytes 206704
  0.7 73.1 %copy-start.11 = (f32[53]{0:T(128)S(1)}, f32[53]{0:T(128)}, u32[]{:S(2)}) copy-start(f32[53]{0:T(128)} %refs_11_.1) | copy-start | bytes 640
  0.7 73.1 %copy-start.8 = (f32[325]{0:T(512)S(1)}, f32[325]{0:T(512)}, u32[]{:S(2)}) copy-start(f32[325]{0:T(512)} %refs_10_.1) | copy-start | bytes 3904
  0.7 73.1 %copy-start.7 = (f32[325]{0:T(512)S(1)}, f32[325]{0:T(512)}, u32[]{:S(2)}) copy-start(f32[325]{0:T(512)} %refs_9_.1) | copy-start | bytes 3904
  0.7 73.1 %copy-start.6 = (f32[325]{0:T(512)S(1)}, f32[325]{0:T(512)}, u32[]{:S(2)}) copy-start(f32[325]{0:T(512)} %refs_8_.1) | copy-start | bytes 3904
  0.7 73.1 %copy-start.5 = (f32[325]{0:T(512)S(1)}, f32[325]{0:T(512)}, u32[]{:S(2)}) copy-start(f32[325]{0:T(512)} %refs_7_.1) | copy-start | bytes 3904
  0.7 73.1 %copy-start.10 = (f32[54]{0:T(128)S(1)}, f32[54]{0:T(128)}, u32[]{:S(2)}) copy-start(f32[54]{0:T(128)} %refs_4_.1) | copy-start | bytes 652
  0.7 73.1 %copy-start.2 = (f32[8,8,128]{2,1,0:T(8,128)S(1)}, f32[8,8,128]{2,1,0:T(8,128)}, u32[]{:S(2)}) copy-start(f32[8,8,128]{2,1,0:T(8,128)} %param.17) | copy-start | bytes 98308
  0.7 73.1 %copy-start.3 = (f32[8,8,128]{2,1,0:T(8,128)S(1)}, f32[8,8,128]{2,1,0:T(8,128)}, u32[]{:S(2)}) copy-start(f32[8,8,128]{2,1,0:T(8,128)} %param.16) | copy-start | bytes 98308

commit v9 on v8

--- a/solution.py
+++ b/solution.py
@@ -91,11 +91,16 @@
     second, third = parted(rest)
     first, second = first.astype(F32), second.astype(F32)
     stacked = jnp.concatenate([first, second, first, third], 0).astype(BF16)
-    flux = jnp.exp2(product(rates, stacked))
-    high, low = parted(flux)
-    half = sums.shape[0] // 2
-    both = product(sums, high)
-    total = both[:half] + both[half:] + product(sums[:half], low.astype(BF16))
+    count, half = rates.shape[0], sums.shape[0] // 2
+    size = count if state.shape[1] <= GROUP * 128 else 256
+    total = None
+    for start in range(0, count, size):
+        stop = min(start + size, count)
+        flux = jnp.exp2(product(rates[start:stop], stacked))
+        high, low = parted(flux)
+        both = product(sums[:, start:stop], high)
+        part = both[:half] + both[half:] + product(sums[:half, start:stop], low.astype(BF16))
+        total = part if total is None else total + part
     gain, loss = total[:ROWS], total[ROWS:]
     species = (state + gain) * moved / (moved + loss)
     return jnp.where(row == 53, heat * jnp.exp2(gain[53:54]), species)
@@ -373,8 +378,7 @@
     )
 
 
-def transport(met, courant_ref, spread_ref, out, grid, edge, halo, sems, hooks):
-    lane = lax.broadcasted_iota(jnp.int32, (ROWS, 128), 1)
+def face_copies(grid, edge, halo, sems):
     peers = faces()
     inner = pl.ds(1, 8)
     plans = [
@@ -385,10 +389,17 @@
         (edge, halo.at[1]),
         (edge, halo.at[0]),
     ]
-    copies = [remote(*plans[k], sems, k, peers[k]) for k in range(6)]
-    met()
+    return [remote(*plans[k], sems, k, peers[k]) for k in range(6)]
+
+
+def send_faces(copies):
     for k in (2, 3, 0, 1):
         copies[k].start()
+
+
+def transport(copies, courant_ref, spread_ref, out, grid, edge, halo, hooks):
+    lane = lax.broadcasted_iota(jnp.int32, (ROWS, 128), 1)
+    inner = pl.ds(1, 8)
 
     def ends(i, packed):
         for j in range(8):
@@ -460,7 +471,9 @@
     hooks[2]()
 
 
-def chemistry(lists_ref, state, rates_ref, sums_ref, put, send, recv, reply, back, result, sems, met):
+def chemistry(lists_ref, state, rates_ref, sums_ref, places, send, recv, reply, back, result, sems, met):
+    put, border, row = places
+
     def each(count, body):
         def four(g, carry):
             for k in range(4):
@@ -500,16 +513,11 @@
         there = recv[jnp.maximum(code - 64, 0)]
         return jnp.where(code < 64, state[jnp.minimum(code, 63)], there)
 
-    def middle(g, carry):
-        first = EARLY + g * GROUP
-        run(first, [any_item(first + k) for k in range(GROUP)])
-        return carry
-
     copies = exchange(send, recv, 0, False)
     own(0)
     for copy in copies:
         copy.wait()
-    lax.fori_loop(0, SPAN // GROUP, middle, 0)
+    run(EARLY, [any_item(EARLY + k) for k in range(SPAN)])
 
     def answer(s):
         reply[s] = result[lists_ref[REPLY, s]]
@@ -520,23 +528,42 @@
     for copy in copies:
         copy.wait()
 
-    def settle(i, carry):
-        for j in range(8):
+    def settle(i, columns):
+        for j in columns:
             code = lists_ref[FINAL, i * 8 + j]
             here = state[jnp.minimum(code, 63)]
             there = back[jnp.clip(code - 64, 0, SLOTS - 1)]
             done = result[jnp.clip(code - 128, 0, WORK - 1)]
             put(i, j, jnp.where(code < 64, here, jnp.where(code < 128, there, done)))
+
+    def sides(i, carry):
+        settle(i, (0, 7))
         return carry
 
-    lax.fori_loop(0, 8, settle, 0)
+    def first_last(i, carry):
+        settle(i * 7, range(1, 7))
+        return carry
+
+    def middle_rows(i, carry):
+        settle(i, range(1, 7))
+        row(i)
+        return carry
+
+    lax.fori_loop(0, 8, sides, 0)
+    lax.fori_loop(0, 2, first_last, 0)
+    border()
+    lax.fori_loop(1, 7, middle_rows, 0)
+
+
+def nothing(*_):
+    return None
 
 
 def into(out):
     def put(i, j, value):
         out[i * 8 + j] = value
 
-    return put
+    return put, nothing, nothing
 
 
 STATE = (64, ROWS, 128)
@@ -558,6 +585,7 @@
     pltpu.SemaphoreType.DMA((14,)),
     pltpu.SemaphoreType.DMA((14,)),
 ]
+FINAL_SCRATCH = [pltpu.VMEM(STATE, F32), pltpu.SemaphoreType.DMA((8,))]
 COUNT_SCRATCH = [
     pltpu.VMEM((8, 8, 128), jnp.int32),
     pltpu.VMEM((16, 8, 128), jnp.int32),
@@ -633,14 +661,15 @@
 def first_steps(both, blocks, tally, species, heat, courant, spread, settings):
     nrxn = settings[0].shape[1]
     padded = -(-nrxn // 16) * 16
-    brought = (tally, species, heat, courant, spread, *settings)
-
-    def kernel(blocks_ref, *refs):
+    brought = (tally, species, heat, courant, spread, *settings, blocks)
+
+    def kernel(*refs):
         anywhere, refs = refs[: len(brought)], refs[len(brought) :]
-        out, lists, rates, sums, spread_out = refs[:5]
-        near, refs = refs[5 : 5 + len(brought)], refs[5 + len(brought) :]
+        out, lists, rates, sums, spread_out, flag = refs[:6]
+        near, refs = refs[6 : 6 + len(brought)], refs[6 + len(brought) :]
         fetch_sem, refs = refs[0], refs[1:]
         tally_ref, species_ref, heat_ref, courant_ref, spread_ref, *settings_refs = near
+        blocks_ref = settings_refs.pop()
         grid, edge, halo, *sems = refs[: len(MOVE_SCRATCH)]
         refs = refs[len(MOVE_SCRATCH) :]
         first, second, *count_sems = refs[:4]
@@ -686,27 +715,46 @@
         def at_end():
             waiting[1]()
             plan(me, stages[2](), found[0], blocks_ref, codes, lists, code_sem)
-
-        nothing = lambda: None
+            flag[0] = lists[REST, 2]
+
+        copies = face_copies(grid, edge, halo, sems)
+        send_faces(copies)
         hooks = (at_once, nothing, at_end)
-        transport(nothing, courant_ref, spread_out, moved, grid, edge, halo, sems, hooks)
+        transport(copies, courant_ref, spread_out, moved, grid, edge, halo, hooks)
         if not both:
             chemistry(lists, moved, rates, sums, into(out), *chem[:5], chem[5:], nothing)
             return
         grid, edge, halo, *sems = refs[: len(MOVE_SCRATCH)]
-        recv, back, *again_sems = refs[len(MOVE_SCRATCH) :]
+        refs = refs[len(MOVE_SCRATCH) :]
+        recv, back, *again_sems = refs[: len(AGAIN_SCRATCH)]
+        last, last_sem = refs[len(AGAIN_SCRATCH) :]
+        copies = face_copies(grid, edge, halo, sems)
 
         def put(i, j, value):
             grid[i + 1, j + 1] = value
 
-        chemistry(lists, moved, rates, sums, put, *chem[:5], chem[5:], nothing)
+        places = (put, lambda: send_faces(copies), nothing)
+        chemistry(lists, moved, rates, sums, places, *chem[:5], chem[5:], nothing)
         hooks = (nothing, nothing, nothing)
-        transport(nothing, courant_ref, spread_out, moved, grid, edge, halo, sems, hooks)
+        transport(copies, courant_ref, spread_out, moved, grid, edge, halo, hooks)
         send, _, reply, _, result = chem[:5]
         again = (send, recv, reply, back, result, again_sems)
-        chemistry(lists, moved, rates, sums, into(out), *again, nothing)
+
+        def leave(i):
+            row = pl.ds(8 * i, 8)
+            return pltpu.make_async_copy(last.at[row], out.at[row], last_sem.at[i])
+
+        def outer():
+            leave(0).start()
+            leave(7).start()
+
+        places = (into(last)[0], outer, lambda i: leave(i).start())
+        chemistry(lists, moved, rates, sums, places, *again, nothing)
+        for i in range(8):
+            leave(i).wait()
 
     smem, vmem = pl.BlockSpec(memory_space=pltpu.SMEM), pl.BlockSpec(memory_space=pltpu.VMEM)
+    anywhere = pl.BlockSpec(memory_space=pl.ANY)
     return communicating(
         kernel,
         0 if both else 1,
@@ -716,17 +764,19 @@
             jax.ShapeDtypeStruct((2 * padded, 4 * ROWS), BF16),
             jax.ShapeDtypeStruct((4 * ROWS, 2 * padded), BF16),
             jax.ShapeDtypeStruct((ROWS, 128), F32),
+            jax.ShapeDtypeStruct((1,), jnp.int32),
         ],
-        [vmem, smem, vmem, vmem, vmem],
-        [smem] + [pl.BlockSpec(memory_space=pl.ANY)] * len(brought),
-        (blocks, *brought),
-        [pltpu.VMEM(x.shape, x.dtype) for x in brought]
+        [anywhere if both else vmem, smem, vmem, vmem, vmem, smem],
+        [anywhere] * len(brought),
+        brought,
+        [pltpu.VMEM(x.shape, x.dtype) for x in brought[:-1]]
+        + [pltpu.SMEM(blocks.shape, blocks.dtype)]
         + [pltpu.SemaphoreType.DMA((7 + len(brought),))]
         + MOVE_SCRATCH
         + COUNT_SCRATCH
         + [pltpu.VMEM(STATE, F32)]
         + CHEM_SCRATCH
-        + (MOVE_SCRATCH + AGAIN_SCRATCH if both else []),
+        + (MOVE_SCRATCH + AGAIN_SCRATCH + FINAL_SCRATCH if both else []),
     )
 
 
@@ -747,9 +797,11 @@
         waits = fetch(pairs + list(zip(anywhere, near)), fetch_sem)
         for wait in waits:
             wait()
-        nothing = lambda: None
+        met()
+        copies = face_copies(grid, edge, halo, sems)
+        send_faces(copies)
         hooks = (nothing, nothing, nothing)
-        transport(met, courant_ref, spread_ref, moved, grid, edge, halo, sems, hooks)
+        transport(copies, courant_ref, spread_ref, moved, grid, edge, halo, hooks)
         chemistry(lists_ref, moved, rates_ref, sums_ref, into(out), *chem[:5], chem[5:], nothing)
 
     smem, vmem = pl.BlockSpec(memory_space=pltpu.SMEM), pl.BlockSpec(memory_space=pltpu.VMEM)
@@ -798,18 +850,18 @@
     courant = axial_courant_number.reshape(64, 128)
     blocks, tally = processor_tiles_burning, tile_transfer_tally
     inputs = (blocks, tally, species, heat, courant, spreading_number, settings)
-    state, lists, rates, sums, _ = first_steps(True, *inputs)
+    state, lists, rates, sums, _, flag = first_steps(True, *inputs)
 
     def balanced(state, lists, rates, sums):
         return finish(lists, blocks, state, rates, sums)
 
     def with_rest(state, lists, rates, sums):
-        state, lists, rates, sums, spread = first_steps(False, *inputs)
+        state, lists, rates, sums, spread, _ = first_steps(False, *inputs)
         state = react_rest(lists, blocks, state, rates, sums)
         state = second_step(lists, state, courant, spread, rates, sums)
         return finish(lists, blocks, state, rates, sums)
 
-    over = lists[REST, 2] > 0
+    over = flag.reshape(()) > 0
     species, heat = lax.cond(over, with_rest, balanced, state, lists, rates, sums)
     return species.reshape(shape), heat.reshape(shape[1:])
 

time: 77.5 us -> 74.5 us (0.961)
  Pallas kernels: 74.8 us -> 72.7 us
    pallas_call x1, Pallas kernels: 71.7 us -> 69.7 us  [communicating(): pl.pallas_call(kernel, out_shape=out_shape, in_specs=specs, out_specs=out...]
where the time goes in v9:
time: 74.5 us; the launch traced here: 74.4 us
  Pallas kernels  72.7 us (98%)
  between operations  1.61 us (2%)
    pallas_call x1, Pallas kernels, communicating(): pl.pallas_call(kernel, out_shape=out_shape, in_specs=specs, out_specs=out...  69.7 us
    pallas_call x1, Pallas kernels, finish(): pl.pallas_call(last_kernel, out_shape=[jax.ShapeDtypeStruct((53, 64, 128)...  3.05 us

profile of v9, /device:TPU:0, one launch (start us, length us, event | category | flops | bytes accessed | tf_op | source)
XLA Modules:
  0.0 74.4 jit_solution(12792868335704700450)
XLA Ops:
  0.6 0.0 copy-start.4
  0.6 0.0 copy-start.9
  0.7 0.0 copy-start.1
  0.7 0.0 copy-start
  0.7 0.0 copy-start.11
  0.7 0.0 copy-start.8
  0.7 0.0 copy-start.7
  0.7 0.0 copy-start.6
  0.7 0.0 copy-start.5
  0.7 0.0 copy-start.10
  0.7 0.0 copy-start.2
  0.7 0.0 copy-start.3
  0.8 69.7 %shard_map.140 = (f32[64,56,128]{2,1,0:T(8,128)}, s32[8,128]{1,0:T(8,128)S(1)}, bf16[672,224]{1,0:T(8,128)(2,1)S(1)}, bf16[224,672]{1,0:T(8,128)(2,1)S(1)}, f32[56,128]{1,0:T(8,128)}, /*index=5*/s32[1]{0:T(128)}) custom-call(s32[1,128]{1,0:T(1,128)} %refs_0_.1, f32[53,64,128]{2,1,0:T(8,128)} %bitcast.6, f32[64,128]{1,0:T(8,128)} %bitcast.10, ...), custom_call_target="tpu_custom_call" | custom-call | tf_op jit(solution)/shard_map/pallas_call | solution.py:649
  71.0 0.0 copy-done.4
  71.0 0.0 copy-done.9
  71.1 0.0 copy-done.1
  71.1 0.0 copy-done
  71.1 0.0 copy-done.11
  71.1 0.0 copy-done.8
  71.1 0.0 copy-done.7
  71.1 0.0 copy-done.6
  71.1 0.0 copy-done.5
  71.1 0.0 copy-done.10
  71.1 0.0 copy-done.2
  71.1 0.0 copy-done.3
  71.2 3.1 %conditional.1 = ((f32[53,64,128]{2,1,0:T(8,128)}, f32[64,128]{1,0:T(8,128)})) conditional(s32[]{:T(128)} %bitcast.3, (s32[8,128]{1,0:T(8,128)S(1)}, s32[1,64]{1,0:T(1,128)S(1)}, f32[64,56,128]{2,1,0:T(8,128)}, bf16[672,224]{1,0:T(8,128)(2,1)S(1)}, bf16[224,672]{1,0:T(8,128)(2,1)S(1)}) %tuple.37, (s32[1,128]{1,0:T(1,128)S(1)}, ...), branch_computations={%region_0.0_spmd.clone, %region_1.0_spmd.clone} | conditional | bytes 8 | solution.py:865
  71.2 3.0 %branch_0_fun.1 = (f32[53,64,128]{2,1,0:T(8,128)}, f32[64,128]{1,0:T(8,128)}) custom-call(s32[8,128]{1,0:T(8,128)S(1)} %get-tuple-element.85.lists_ref, s32[1,64]{1,0:T(1,128)S(1)} %get-tuple-element.86.blocks_ref, f32[64,56,128]{2,1,0:T(8,128)} %get-tuple-element.87.state_any, bf16[672,224]{1,0:T(8,128)(2,1)S(1)} %get-tuple-element.88.rates_any, ...), custom_call_target="tpu_custom_call" | custom-call | tf_op jit(solution)/shard_map/cond/branch_0_fun/pallas_call | solution.py:329
Async XLA Ops:
  0.6 70.4 %copy-start.4 = (s32[1,64]{1,0:T(1,128)S(1)}, s32[1,64]{1,0:T(1,128)}, u32[]{:S(2)}) copy-start(s32[1,64]{1,0:T(1,128)} %refs_12_.1) | copy-start | bytes 772
  0.6 70.4 %copy-start.9 = (s32[1,128]{1,0:T(1,128)S(1)}, s32[1,128]{1,0:T(1,128)}, u32[]{:S(2)}) copy-start(s32[1,128]{1,0:T(1,128)} %refs_0_.1) | copy-start | bytes 1540
  0.7 70.4 %copy-start.1 = (f32[53,325]{1,0:T(8,128)S(1)}, f32[53,325]{1,0:T(8,128)}, u32[]{:S(2)}) copy-start(f32[53,325]{1,0:T(8,128)} %refs_6_.1) | copy-start | bytes 206704
  0.7 70.4 %copy-start = (f32[53,325]{1,0:T(8,128)S(1)}, f32[53,325]{1,0:T(8,128)}, u32[]{:S(2)}) copy-start(f32[53,325]{1,0:T(8,128)} %refs_5_.1) | copy-start | bytes 206704
  0.7 70.4 %copy-start.11 = (f32[53]{0:T(128)S(1)}, f32[53]{0:T(128)}, u32[]{:S(2)}) copy-start(f32[53]{0:T(128)} %refs_11_.1) | copy-start | bytes 640
  0.7 70.4 %copy-start.8 = (f32[325]{0:T(512)S(1)}, f32[325]{0:T(512)}, u32[]{:S(2)}) copy-start(f32[325]{0:T(512)} %refs_10_.1) | copy-start | bytes 3904
  0.7 70.4 %copy-start.7 = (f32[325]{0:T(512)S(1)}, f32[325]{0:T(512)}, u32[]{:S(2)}) copy-start(f32[325]{0:T(512)} %refs_9_.1) | copy-start | bytes 3904
  0.7 70.4 %copy-start.6 = (f32[325]{0:T(512)S(1)}, f32[325]{0:T(512)}, u32[]{:S(2)}) copy-start(f32[325]{0:T(512)} %refs_8_.1) | copy-start | bytes 3904
  0.7 70.4 %copy-start.5 = (f32[325]{0:T(512)S(1)}, f32[325]{0:T(512)}, u32[]{:S(2)}) copy-start(f32[325]{0:T(512)} %refs_7_.1) | copy-start | bytes 3904
  0.7 70.4 %copy-start.10 = (f32[54]{0:T(128)S(1)}, f32[54]{0:T(128)}, u32[]{:S(2)}) copy-start(f32[54]{0:T(128)} %refs_4_.1) | copy-start | bytes 652
  0.7 70.4 %copy-start.2 = (f32[8,8,128]{2,1,0:T(8,128)S(1)}, f32[8,8,128]{2,1,0:T(8,128)}, u32[]{:S(2)}) copy-start(f32[8,8,128]{2,1,0:T(8,128)} %param.17) | copy-start | bytes 98308
  0.7 70.4 %copy-start.3 = (f32[8,8,128]{2,1,0:T(8,128)S(1)}, f32[8,8,128]{2,1,0:T(8,128)}, u32[]{:S(2)}) copy-start(f32[8,8,128]{2,1,0:T(8,128)} %param.16) | copy-start | bytes 98308
